TPU v7x, 256 devices: a whole 4x4x8 slice. The times are simulated.
256 devices in a mesh: rows: 32 (over z, y), snode: 8 (over x, core).
Axes of the slice: x: 4, y: 4, z: 8, core: 2. Of those that a mesh axis runs over, the one named last changes fastest.
Arguments:
- a_tiles: bfloat16 [6144, 256, 256], P(('rows', 'snode')), may hold values from -0.21875 to 0.21875
- tile_row: int32 [6144], P(('rows', 'snode')), may hold values from 0 to 7
- tile_col: int32 [6144], P(('rows', 'snode')), may hold values from 0 to 127, as said below
- right_side: float32 [2048, 32, 256], P(('rows', 'snode')), may hold values from -6 to 6
- estimate: float32 [4, 32, 32, 256], P(None, 'snode'), may hold values from -6 to 6
- diag_inverse: bfloat16 [4, 32, 256, 256], P(None, 'snode'), may hold values from -1.5 to 3
- coupling: bfloat16 [3, 32, 3, 256, 256], P(None, 'snode'), may hold values from -0.15625 to 0.15625
- coupling_source: int32 [3, 32, 3], P(None, 'snode'), may hold values from 0 to 95, as said below
Outputs:
- new_estimate: float32 [4, 32, 32, 256], P(None, 'snode')
- residual: float32 [2048, 32, 256], P(('rows', 'snode'))
Inputs may be any that keep to these rules, and one draw needn't show every extreme that they name: `tile_col`: on each device (each aligned block of 24 entries), at most 6 entries name column tiles c with (c % 32) // 4 equal to one value, and on every device some value is named exactly 6 times. `coupling_source`: at level index m, entry 0 of the 32 supernodes is a permutation of the supernodes of level m (indices m * 32 to (m + 1) * 32 - 1); the other entries are below (m + 1) * 32.
All inputs are finite; a program needn't handle non-finite values.
Results may differ from a plain program's by a relative error of at most 0.012.
Values may be sent and summed in bfloat16 or wider, within the bound.
No kernel may reach another device: no remote copies, remote signals or barrier semaphores. Data moves between devices by JAX's collectives and lax.ppermute only.
A program may use at most 64 MiB of HBM per device.

v0:
```python
import jax
import jax.numpy as jnp
from jax import lax
from jax.sharding import PartitionSpec as P


def local(
    a_tiles, tile_row, tile_col, right_side, estimate, diag_inverse, coupling, coupling_source
):
    tile_count, tile_order = (a_tiles.shape[0], a_tiles.shape[1])
    row_tiles = right_side.shape[0]
    levels, per_owner, rhs_count = (estimate.shape[0], estimate.shape[1], estimate.shape[2])
    owners = lax.axis_size("snode")
    level_width = per_owner * owners
    node_total = levels * level_width
    flat_width = rhs_count * tile_order
    highest = lax.Precision.HIGHEST
    estimate_low = estimate.astype(jnp.bfloat16)
    row_pick = tile_row[:, None] == jnp.arange(row_tiles, dtype=jnp.int32)[None, :]
    col_pick = tile_col[:, None] == jnp.arange(node_total, dtype=jnp.int32)[None, :]
    picked = jnp.dot(
        col_pick.astype(jnp.bfloat16),
        lax.all_gather(estimate_low, "snode", axis=1, tiled=True).reshape(node_total, flat_width),
        preferred_element_type=jnp.bfloat16,
    )
    tiles_x = picked.reshape(tile_count, rhs_count, tile_order)
    product = jnp.einsum("nkc,nrc->nkr", tiles_x, a_tiles, preferred_element_type=jnp.float32)
    applied = jnp.einsum(
        "nq,nx->qx",
        row_pick.astype(jnp.float32),
        product.reshape(tile_count, flat_width),
        precision=highest,
    )
    residual = right_side - applied.reshape(row_tiles, rhs_count, tile_order)
    residual_low = residual.astype(jnp.bfloat16)
    tile_res = jnp.einsum(
        "nq,qx->nx",
        row_pick.astype(jnp.bfloat16),
        residual_low.reshape(row_tiles, flat_width),
        preferred_element_type=jnp.bfloat16,
    )
    tile_terms = jnp.einsum(
        "nkr,nrc->nkc",
        tile_res.reshape(tile_count, rhs_count, tile_order),
        a_tiles,
        preferred_element_type=jnp.float32,
    ).reshape(tile_count, flat_width)
    spread_terms = jnp.einsum(
        "nc,nx->cx", col_pick.astype(jnp.float32), tile_terms, precision=highest
    )
    summed = lax.psum(spread_terms.reshape(levels, level_width, flat_width), ("rows", "snode"))
    my_index = lax.axis_index("snode")
    gradient = lax.dynamic_slice_in_dim(summed, my_index * per_owner, per_owner, 1)
    gradient = gradient.reshape(levels, per_owner, rhs_count, tile_order)
    gathered = []
    solved = []
    for level in range(levels):
        accumulated = gradient[level]
        if level > 0:
            known_low = jnp.concatenate(gathered, axis=0).reshape(level * level_width, flat_width)
            sources = coupling_source[level - 1]
            source_pick = (
                sources[..., None] == jnp.arange(level * level_width, dtype=jnp.int32)
            ).astype(jnp.bfloat16)
            lookup = jnp.einsum(
                "sna,ax->snx", source_pick, known_low, preferred_element_type=jnp.bfloat16
            )
            lookup = lookup.reshape(per_owner, -1, rhs_count, tile_order)
            accumulated = accumulated - jnp.einsum(
                "snkc,sncj->skj", lookup, coupling[level - 1], preferred_element_type=jnp.float32
            )
        value = jnp.einsum(
            "skt,stj->skj",
            accumulated.astype(jnp.bfloat16),
            diag_inverse[level],
            preferred_element_type=jnp.float32,
        )
        solved.append(value)
        if level < levels - 1:
            gathered.append(lax.all_gather(value.astype(jnp.bfloat16), "snode", axis=0, tiled=True))
    pending = jnp.zeros((node_total, flat_width), jnp.float32)
    updates = [None] * levels
    for level in reversed(range(levels)):
        remaining = solved[level]
        if level < levels - 1:
            level_terms = pending[level * level_width : (level + 1) * level_width].reshape(
                level_width, rhs_count, tile_order
            )
            received = lax.psum_scatter(level_terms, "snode", scatter_dimension=0, tiled=True)
            remaining = remaining - received
        change = jnp.einsum(
            "skj,stj->skt",
            remaining.astype(jnp.bfloat16),
            diag_inverse[level],
            preferred_element_type=jnp.float32,
        )
        updates[level] = change
        if level > 0:
            change_low = change.astype(jnp.bfloat16)
            pushed = jnp.einsum(
                "skj,sncj->snkc",
                change_low,
                coupling[level - 1],
                preferred_element_type=jnp.float32,
            )
            target_pick = (
                coupling_source[level - 1][..., None] == jnp.arange(node_total, dtype=jnp.int32)
            ).astype(jnp.float32)
            pending = pending + jnp.einsum(
                "sna,snx->ax",
                target_pick,
                pushed.reshape(per_owner, -1, flat_width),
                precision=highest,
            )
    new_estimate = estimate + jnp.stack(updates)
    return (new_estimate, residual)


def solution(mesh):
    in_specs = (
        P(("rows", "snode"), None, None),
        P(("rows", "snode")),
        P(("rows", "snode")),
        P(("rows", "snode"), None, None),
        P(None, "snode", None, None),
        P(None, "snode", None, None),
        P(None, "snode", None, None, None),
        P(None, "snode", None),
    )
    out_specs = (P(None, "snode", None, None), P(("rows", "snode"), None, None))
    return jax.shard_map(local, mesh=mesh, in_specs=in_specs, out_specs=out_specs, check_vma=False)
```

profile of v0, /device:TPU:2, one launch (start us, length us, event | category | flops | bytes accessed | tf_op | source)
XLA Modules:
  0.0 536.1 jit_solution(7607537404219092998)
XLA Ops:
  7.2 1.9 convert_element_type.59
  9.2 31.0 %all-gather.2.cloned.1.call-done = bf16[4,32,32,256]{3,2,1,0:T(8,128)(2,1)} async-done(((bf16[4,4,32,256]{3,2,1,0:T(8,128)(2,1)}), bf16[4,32,32,256]{3,2,1,0:T(8,128)(2,1)}) %all-gather.2.cloned.1.call-update) | async-done | bytes 2097168 | tf_op jit(solution)/shard_map/all_gather | solution.py:23
  40.2 4.3 copy.73
  44.5 4.1 copy.42
  48.6 2.3 fusion.118
  54.7 2.2 reshape.103
  56.8 4.7 fusion.113
  62.3 269.3 %all-reduce.2.cloned.1.call-done = f32[4,32,8192]{2,1,0:T(8,128)} async-done(((f32[4,32,8192]{2,1,0:T(8,128)}), f32[4,32,8192]{2,1,0:T(8,128)}) %all-reduce.2.cloned.1.call-update) | async-done | bytes 4194320 | tf_op jit(solution)/shard_map/psum | solution.py:51
  332.6 1.9 fusion.138
  334.5 13.1 %all_gather.13 = bf16[32,32,256]{2,1,0:T(8,128)(2,1)S(1)} all-gather(bf16[4,32,256]{2,1,0:T(8,128)(2,1)S(1)} %get-tuple-element.16), channel_id=1, replica_groups=mesh['rows'=32,'snode'=8] {'snode'}, dimensions={0}, use_global_device_ids=true | all-gather | bytes 589824 | tf_op jit(solution)/shard_map/all_gather | solution.py:80
  349.5 1.9 constant_dynamic-slice_fusion.1
  351.4 2.8 fusion.139
  354.2 13.3 %all_gather.14 = bf16[32,32,256]{2,1,0:T(8,128)(2,1)S(1)} all-gather(bf16[4,32,256]{2,1,0:T(8,128)(2,1)} %get-tuple-element.18), channel_id=1, replica_groups=mesh['rows'=32,'snode'=8] {'snode'}, dimensions={0}, use_global_device_ids=true | all-gather | bytes 589824 | tf_op jit(solution)/shard_map/all_gather | solution.py:80
  370.9 2.8 fusion.144
  373.6 13.5 %all_gather.15 = bf16[32,32,256]{2,1,0:T(8,128)(2,1)S(1)} all-gather(bf16[4,32,256]{2,1,0:T(8,128)(2,1)} %get-tuple-element.20), channel_id=1, replica_groups=mesh['rows'=32,'snode'=8] {'snode'}, dimensions={0}, use_global_device_ids=true | all-gather | bytes 589824 | tf_op jit(solution)/shard_map/all_gather | solution.py:80
  389.5 2.4 fusion.54
  391.9 1.6 fusion.57
  393.5 2.0 fusion.27
  396.3 1.9 reshape.95
  398.2 2.9 convolution_bitcast_fusion.2
  401.3 1.6 copy.82
  403.6 29.7 %reduce-scatter.4.cloned.1.call-done = f32[4,32,256]{2,1,0:T(8,128)} async-done(((f32[32,32,256]{2,1,0:T(8,128)}), f32[4,32,256]{2,1,0:T(8,128)}) %reduce-scatter.4.cloned.1.call-update) | async-done | bytes 131088 | tf_op jit(solution)/shard_map/reduce_scatter | solution.py:89
  435.5 2.0 fusion.24
  438.2 1.9 reshape.97
  440.2 4.4 fusion
  444.7 1.6 copy.83
  447.1 33.3 %reduce-scatter.6.cloned.1.call-done = f32[4,32,256]{2,1,0:T(8,128)} async-done(((f32[32,32,256]{2,1,0:T(8,128)}), f32[4,32,256]{2,1,0:T(8,128)}) %reduce-scatter.6.cloned.1.call-update) | async-done | bytes 131088 | tf_op jit(solution)/shard_map/reduce_scatter | solution.py:89
  482.4 2.0 fusion.21
  485.2 1.9 reshape.99
  487.1 2.9 convolution_bitcast_fusion
  493.5 32.6 %reduce-scatter.8.cloned.1.call-done = f32[4,32,256]{2,1,0:T(8,128)} async-done(((f32[32,32,256]{2,1,0:T(8,128)}), f32[4,32,256]{2,1,0:T(8,128)}) %reduce-scatter.8.cloned.1.call-update) | async-done | bytes 131088 | tf_op jit(solution)/shard_map/reduce_scatter | solution.py:89
  527.6 2.0 maximum_add_fusion
  (60 shorter events, 26.3 us)
Async XLA Ops:
  7.2 43.7 %copy-start = (bf16[24,256,256]{2,1,0:T(8,128)(2,1)S(1)}, bf16[24,256,256]{2,1,0:T(8,128)(2,1)}, u32[]{:S(2)}) copy-start(bf16[24,256,256]{2,1,0:T(8,128)(2,1)} %param.8) | copy-start | bytes 9437188
  7.2 33.0 %all-gather.2.cloned.1.call-start = ((), (), s32[]{:S(2)}) async-start(), calls=%async_computation.3 | async-start | bytes 2359296 | tf_op jit(solution)/shard_map/all_gather | solution.py:23
  9.2 322.4 %all-reduce.2.cloned.1.call-start = ((), (), s32[]{:S(2)}) async-start(), calls=%async_computation.4 | async-start | bytes 8388608 | tf_op jit(solution)/shard_map/psum | solution.py:51
  44.5 4.1 copy-start.11
  50.9 1.0 copy-start.7
  50.9 1.0 copy-start.10
  61.5 0.7 copy-start.9
  61.5 371.8 %reduce-scatter.4.cloned.1.call-start = ((), (), s32[]{:S(2)}) async-start(), calls=%async_computation.5 | async-start | bytes 1179648 | tf_op jit(solution)/shard_map/reduce_scatter | solution.py:89
  347.6 0.8 copy-start.3
  367.5 0.8 copy-start.4
  387.1 2.4 copy-start.8
  401.2 2.3 copy-start.1
  403.5 76.8 %reduce-scatter.6.cloned.1.call-start = ((), (), s32[]{:S(2)}) async-start(), calls=%async_computation.6 | async-start | bytes 1179648 | tf_op jit(solution)/shard_map/reduce_scatter | solution.py:89
  434.8 0.7 copy-start.5
  444.6 2.3 copy-start.2
  446.9 79.2 %reduce-scatter.8.cloned.1.call-start = ((), (), s32[]{:S(2)}) async-start(), calls=%async_computation.7 | async-start | bytes 1179648 | tf_op jit(solution)/shard_map/reduce_scatter | solution.py:89
  481.7 0.7 copy-start.6
Sparse Core Ops, SparseCore 0:
  10.4 29.7 all-gather.1
  61.6 269.9 all-reduce.1
  403.6 29.7 reduce-scatter.3
  447.0 33.2 reduce-scatter.5
  492.9 33.2 reduce-scatter.7
where the time goes:
time: 540 us; the launch traced here: 536 us
  waiting for transfers between devices  396 us (73%)
  matrix products  46 us (9%)
  blocking collectives  39.9 us (7%)
  local copies, waits for them, and re-layouts  32.2 us (6%)
  between operations  14 us (3%)
  other arithmetic  7.82 us (1%)
    psum x1, waiting for transfers between devices, local(): lax.psum(spread_terms.reshape(levels, level_width, flat_width), ('rows',...  269 us
    reduce_scatter x3, waiting for transfers between devices, local(): lax.psum_scatter(level_terms, 'snode', scatter_dimension=0, tiled=True)  95.6 us
    all_gather x3, blocking collectives, local(): lax.all_gather(value.astype(jnp.bfloat16), 'snode', axis=0, tiled=True)  39.9 us
    all_gather x1, waiting for transfers between devices, local(): lax.all_gather(estimate_low, 'snode', axis=1, tiled=True)  31 us
    unnamed x29, local copies, waits for them, and re-layouts  14.5 us
  transfers between devices with their start and end apart: 5, of which 5 were waited for; matrix products, arithmetic and copies ran while one was open for 0% of the time, Pallas kernels for 0%

commit v1 on v0

v1 whole, which is shorter than its diff:
```python
import functools

import jax
import jax.numpy as jnp
from jax import lax
from jax.experimental import pallas as pl
from jax.experimental.pallas import tpu as pltpu
from jax.sharding import PartitionSpec as P

CAP = 6
X, CORE, Y, Z = 4, 2, 4, 8
OWNERS = X * CORE
F32 = jnp.float32
BF16 = jnp.bfloat16
NT = (((1,), (1,)), ((), ()))
NN = (((1,), (0,)), ((), ()))
SMEM = pl.BlockSpec(memory_space=pltpu.SMEM)
VMEM = pl.BlockSpec(memory_space=pltpu.VMEM)
ANY = pl.BlockSpec(memory_space=pl.ANY)
PARAMS = pltpu.CompilerParams(vmem_limit_bytes=16 * 1024 * 1024)


def dot(x, y, dims):
    return lax.dot_general(x, y, dims, preferred_element_type=F32)


def ring_away(owner, here):
    step = (lax.shift_right_logical(owner, 1) + X - lax.shift_right_logical(here, 1)) & (X - 1)
    return step * CORE + ((owner ^ here) & 1)


def plan_kernel(sn, here_ref, col_ref, row_ref, plan_ref, note_ref, count_ref, note):
    note[...] = jnp.zeros_like(note)
    for o in range(OWNERS):
        count_ref[o] = 0
    for t in range(col_ref.shape[0]):
        c = col_ref[t]
        level, owner, inner = c // (sn * OWNERS), (c // sn) % OWNERS, c % sn
        rank = count_ref[owner]
        count_ref[owner] = rank + 1
        plan_ref[0, t] = ring_away(owner, here_ref[0])
        plan_ref[1, t] = level * sn + inner
        plan_ref[2, t] = row_ref[t]
        plan_ref[3, t] = owner
        plan_ref[4, t] = rank
        mark = (level * sn + inner + 1).astype(F32)
        note[owner, pl.ds(rank, 1), :] = jnp.full((1, note.shape[2]), mark, F32)
    note_ref[...] = note[...].astype(BF16)


def tile_kernel(n_blocks, plan_ref, note_ref, side_ref, a_ref, *refs):
    blocks = refs[:n_blocks]
    res_ref, send_ref, x_all, low_ref, sems = refs[n_blocks:]
    tiles = a_ref.shape[0]
    mine = x_all.shape[0] // OWNERS
    half = x_all.shape[1] // 2
    per = send_ref.shape[0] // OWNERS
    copies = []
    for i, block in enumerate(blocks):
        target = x_all.at[pl.ds(i * mine, mine)]
        copies.append(pltpu.make_async_copy(block, target, sems.at[i]))
    for copy in copies:
        copy.start()
    send_ref[...] = jnp.zeros_like(send_ref)
    for o in range(OWNERS):
        send_ref[o * per + per - 1] = note_ref[o]
    res_ref[...] = side_ref[...]
    for copy in copies:
        copy.wait()
    for t in range(tiles):
        q = plan_ref[2, t]
        res_ref[q] -= dot(x_all[plan_ref[0, t] * mine + plan_ref[1, t]], a_ref[t], NT)
    low_ref[...] = res_ref[...].astype(BF16)
    for t in range(tiles):
        spot = plan_ref[3, t] * per + 2 * plan_ref[4, t]
        term = dot(low_ref[plan_ref[2, t]], a_ref[t], NN).astype(BF16)
        send_ref[spot] = term[:half]
        send_ref[spot + 1] = term[half:]


def in_hbm(x):
    return pltpu.with_memory_space_constraint(x, pltpu.HBM)


def in_vmem(x):
    return pltpu.with_memory_space_constraint(x, pltpu.VMEM)


def near_kernel(n, parts, *refs):
    sems = refs[-1]
    outs = refs[-1 - n : -1]
    copies = []
    for i in range(n):
        size = refs[i].shape[0] // parts[i]
        for k in range(parts[i]):
            piece = pl.ds(k * size, size)
            copies.append(pltpu.make_async_copy(refs[i].at[piece], outs[i].at[piece], sems.at[len(copies)]))
    for copy in copies:
        copy.start()
    for copy in copies:
        copy.wait()


def bring_near(after, *operands):
    n = len(operands)
    parts = tuple(4 if x.shape[0] % 4 == 0 else x.shape[0] for x in operands)
    operands = [in_hbm(x) for x in operands]
    if after is not None:
        operands.append(in_hbm(after))
    out_shape = [pltpu.VMEM(x.shape, x.dtype) if after is not None else jax.ShapeDtypeStruct(x.shape, x.dtype) for x in operands]
    return pl.pallas_call(
        functools.partial(near_kernel, n, parts),
        out_shape=tuple(out_shape[:n]),
        in_specs=[ANY] * len(operands),
        out_specs=(VMEM,) * n,
        scratch_shapes=[pltpu.SemaphoreType.DMA((sum(parts),))],
        compiler_params=PARAMS,
        name="bring_near",
    )(*operands)


def forward_rows(level, sn, g, look_ref, known_refs, c_ref, d_ref):
    if level > 0:
        known = jnp.concatenate([ref[...].reshape(-1, ref.shape[2]) for ref in known_refs], axis=0).astype(BF16)
        found = dot(look_ref[...], known, NN)
    rows = []
    for j in range(sn):
        acc = g[level * sn + j : level * sn + j + 1, :]
        if level > 0:
            n = c_ref.shape[2]
            for i in range(n):
                row = found[j * n + i : j * n + i + 1, :].astype(BF16)
                acc = acc - dot(row, c_ref[0, j, i], NN)
        rows.append(dot(acc.astype(BF16), d_ref[0, j], NN))
    return rows


def backward_rows(level, sn, remaining, c_ref, d_ref, change_ref, stage):
    for j in range(sn):
        change = dot(remaining[j].astype(BF16), d_ref[0, j], NT)
        change_ref[j : j + 1, :] = change
        if level > 0:
            n = c_ref.shape[2]
            low = change.astype(BF16)
            for i in range(n):
                stage[j * n + i : j * n + i + 1, :] = dot(low, c_ref[0, j, i], NT)


def spread(scatter_ref, stage):
    terms = stage[...]
    high = terms.astype(BF16)
    low = (terms - high.astype(F32)).astype(BF16)
    return dot(scatter_ref[...], high, NN) + dot(scatter_ref[...], low, NN)


def store_pend(pend, out_ref, rest_refs):
    n, rows, width = out_ref.shape
    base = pend.shape[0] - n * rows
    out_ref[...] = pend[base:, :].reshape(n, rows, width)
    for ref in rest_refs:
        ref[...] = pend[:base, :]


def spread_rows(rows, own_ref, out_ref):
    out_ref[...] = jnp.zeros_like(out_ref)
    for j, row in enumerate(rows):
        own_ref[j : j + 1, :] = row
        for o in range(out_ref.shape[0]):
            out_ref[o, j : j + 1, :] = row


def first_kernel(sn, parts_ref, d_ref, g_ref, own_ref, out_ref):
    total = parts_ref[0].astype(F32)
    for i in range(1, parts_ref.shape[0]):
        total = total + parts_ref[i].astype(F32)
    g_ref[...] = total
    spread_rows(forward_rows(0, sn, total, None, [], None, d_ref), own_ref, out_ref)


def forward_kernel(level, sn, g_ref, look_ref, *refs):
    known_refs, (c_ref, d_ref, own_ref, out_ref) = refs[:level], refs[level:]
    rows = forward_rows(level, sn, g_ref[...], look_ref, known_refs, c_ref, d_ref)
    spread_rows(rows, own_ref, out_ref)


def turn_kernel(level, sn, g_ref, look_ref, scatter_ref, *refs):
    known_refs, refs = refs[:level], refs[level:]
    c_ref, d_ref, change_ref, out_ref, rest_ref, stage = refs
    rows = forward_rows(level, sn, g_ref[...], look_ref, known_refs, c_ref, d_ref)
    stage[...] = jnp.zeros_like(stage)
    backward_rows(level, sn, rows, c_ref, d_ref, change_ref, stage)
    store_pend(spread(scatter_ref, stage), out_ref, [rest_ref])


def remaining_rows(sn, solved_ref, recv_ref):
    got = recv_ref[0]
    for i in range(1, recv_ref.shape[0]):
        got = got + recv_ref[i]
    return [solved_ref[j : j + 1, :] - got[j : j + 1, :] for j in range(sn)]


def backward_kernel(level, sn, solved_ref, recv_ref, pend_ref, scatter_ref, c_ref, d_ref, *refs):
    change_ref, out_ref, rest_refs, stage = refs[0], refs[1], refs[2:-1], refs[-1]
    stage[...] = jnp.zeros_like(stage)
    backward_rows(level, sn, remaining_rows(sn, solved_ref, recv_ref), c_ref, d_ref, change_ref, stage)
    store_pend(pend_ref[...] + spread(scatter_ref, stage), out_ref, rest_refs)


def last_kernel(sn, solved_ref, recv_ref, c3_ref, c2_ref, c1_ref, d_ref, out_ref, change):
    backward_rows(0, sn, remaining_rows(sn, solved_ref, recv_ref), None, d_ref, change, None)
    mine = jnp.concatenate([change[...], c1_ref[...], c2_ref[...], c3_ref[...]], axis=0).astype(BF16)
    for i in range(out_ref.shape[0]):
        out_ref[i] = mine


def shift(size, step):
    return [(i, (i + step) % size) for i in range(size)]


def local(a_tiles, tile_row, tile_col, right_side, estimate, diag_inverse, coupling, coupling_source):
    tiles, T = a_tiles.shape[0], a_tiles.shape[1]
    row_tiles, K = right_side.shape[0], right_side.shape[1]
    levels, sn = estimate.shape[0], estimate.shape[1]
    snode = ("x", "core")
    width = sn * OWNERS
    mine = levels * sn
    me = lax.axis_index("x") * CORE + lax.axis_index("core")
    here = me.reshape(1)

    e = estimate.astype(BF16).reshape(mine, K, T)
    other = functools.partial(lax.ppermute, axis_name="core", perm=shift(CORE, 1))

    ahead = lax.ppermute(e, "x", shift(X, X - 1))
    behind = lax.ppermute(e, "x", shift(X, 1))
    swapped = other(e)
    plan, note = pl.pallas_call(
        functools.partial(plan_kernel, sn),
        out_shape=(
            jax.ShapeDtypeStruct((5, tiles), jnp.int32),
            jax.ShapeDtypeStruct((OWNERS, 16, T), BF16),
        ),
        in_specs=[SMEM, SMEM, SMEM],
        out_specs=(SMEM, VMEM),
        scratch_shapes=[pltpu.SMEM((OWNERS,), jnp.int32), pltpu.VMEM((OWNERS, 16, T), F32)],
        compiler_params=PARAMS,
        name="plan",
    )(here, in_hbm(tile_col), in_hbm(tile_row))
    a_near, side = bring_near(None, a_tiles, right_side)
    ahead, behind, note, a_near = lax.optimization_barrier((ahead, behind, note, a_near))
    core = lax.axis_index("core")
    onward = []
    for x in range(X):
        onward.append((x * CORE, (x + 1) % X * CORE))
        onward.append((x * CORE + 1, (x - 1) % X * CORE + 1))
    far = lax.ppermute(jnp.where(core == 0, behind, ahead), snode, onward)
    blocks = [e, swapped, ahead, other(ahead), far, other(far), behind, other(behind)]

    slot_rows = CAP * K + 16
    residual, send = pl.pallas_call(
        functools.partial(tile_kernel, len(blocks)),
        out_shape=(
            jax.ShapeDtypeStruct((row_tiles, K, T), F32),
            jax.ShapeDtypeStruct((OWNERS * slot_rows // 16, 16, T), BF16),
        ),
        in_specs=[SMEM, VMEM, VMEM, VMEM] + [ANY] * len(blocks),
        out_specs=(VMEM, VMEM),
        scratch_shapes=[
            pltpu.VMEM((OWNERS * mine, K, T), BF16),
            pltpu.VMEM((row_tiles, K, T), BF16),
            pltpu.SemaphoreType.DMA((len(blocks),)),
        ],
        compiler_params=PARAMS,
        name="tile_products",
    )(plan, note, side, a_near, *blocks)

    send, coupling_source = lax.optimization_barrier((send, coupling_source))
    source = coupling_source.reshape(levels - 1, -1)
    block_rows = 8
    spot_at = source // sn * block_rows + source % sn
    n_terms = source.shape[1]
    pad_terms = -n_terms % 16
    spot_at = jnp.pad(spot_at, ((0, 0), (0, pad_terms)), constant_values=-1)
    look, scatter = [], []
    for level in range(1, levels):
        spots = jnp.arange(level * OWNERS * block_rows)
        look.append((spot_at[level - 1][:, None] == spots[None, :]).astype(BF16))
        scatter.append((spots[:, None] == spot_at[level - 1][None, :]).astype(BF16))
    stage = pltpu.VMEM((n_terms + pad_terms, T), F32)

    recv = lax.all_to_all(send, snode, 0, 0, tiled=True)
    (c_near,) = bring_near(residual, coupling)
    recv, c_near, look, scatter = lax.optimization_barrier((recv, c_near, look, scatter))
    recv = recv.reshape(OWNERS, slot_rows, T)

    spot = recv[:, CAP * K : CAP * K + CAP, 0].astype(jnp.int32) - 1
    spot = jnp.pad(jnp.repeat(spot, K, axis=1), ((0, 0), (0, 16)), constant_values=-1).reshape(-1)
    pick_row = jnp.arange(K * mine)
    pick_col = jnp.arange(OWNERS * slot_rows) % slot_rows
    y = lax.axis_index("y")
    row_k = (pick_row // mine) % Z * Y + (pick_row // (mine * Z) + y) % Y
    pick = (row_k[:, None] == pick_col[None, :] % K) & (pick_row[:, None] % mine == spot[None, :])
    part = jnp.dot(pick.astype(BF16), recv.reshape(OWNERS * slot_rows, T), preferred_element_type=F32)
    part = part.astype(BF16).reshape(Y, Z * mine, T)
    total = part[0].astype(F32)
    for s in range(1, Y):
        total = total + lax.ppermute(part[s], "y", shift(Y, s)).astype(F32)
    parts = lax.all_to_all(total.astype(BF16).reshape(Z, mine, T), "z", 0, 0, tiled=True)

    def d_spec(level):
        return pl.BlockSpec((1, sn, T, T), lambda i: (level, 0, 0, 0))

    def c_spec(level):
        return pl.BlockSpec((1, sn, coupling.shape[2], T, T), lambda i: (level - 1, 0, 0, 0, 0))

    row4 = jax.ShapeDtypeStruct((sn, T), F32)
    by_owner = jax.ShapeDtypeStruct((OWNERS, block_rows, T), F32)

    def rest_of(level):
        return (jax.ShapeDtypeStruct(((level - 1) * OWNERS * block_rows, T), F32),) if level > 1 else ()

    g, value, out = pl.pallas_call(
        functools.partial(first_kernel, sn),
        grid=(1,),
        out_shape=(jax.ShapeDtypeStruct((mine, T), F32), row4, by_owner),
        in_specs=[VMEM, d_spec(0)],
        out_specs=(VMEM, VMEM, VMEM),
        compiler_params=PARAMS,
        name="forward_0",
    )(parts, diag_inverse)
    known, solved = [], [value]
    for level in range(1, levels):
        known.append(lax.all_to_all(out, snode, 0, 0, tiled=True))
        if level < levels - 1:
            value, out = pl.pallas_call(
                functools.partial(forward_kernel, level, sn),
                grid=(1,),
                out_shape=(row4, by_owner),
                in_specs=[VMEM] * (2 + level) + [c_spec(level), d_spec(level)],
                out_specs=(VMEM, VMEM),
                compiler_params=PARAMS,
                name=f"forward_{level}",
            )(g, look[level - 1], *known, in_vmem(c_near), diag_inverse)
            solved.append(value)
        else:
            out_shape = (row4, by_owner) + rest_of(level)
            change, out, *rest = pl.pallas_call(
                functools.partial(turn_kernel, level, sn),
                grid=(1,),
                out_shape=out_shape,
                in_specs=[VMEM] * (3 + level) + [c_spec(level), d_spec(level)],
                out_specs=(VMEM,) * len(out_shape),
                scratch_shapes=[stage],
                compiler_params=PARAMS,
                name="turn",
            )(g, look[level - 1], scatter[level - 1], *known, in_vmem(c_near), diag_inverse)
    changes = [change]
    for level in reversed(range(levels - 1)):
        arrived = lax.all_to_all(out, snode, 0, 0, tiled=True)
        if level > 0:
            out_shape = (row4, by_owner) + rest_of(level)
            change, out, *rest = pl.pallas_call(
                functools.partial(backward_kernel, level, sn),
                grid=(1,),
                out_shape=out_shape,
                in_specs=[VMEM] * 4 + [c_spec(level), d_spec(level)],
                out_specs=(VMEM,) * len(out_shape),
                scratch_shapes=[stage],
                compiler_params=PARAMS,
                name=f"backward_{level}",
            )(solved[level], arrived, rest[0], scatter[level - 1], in_vmem(c_near), diag_inverse)
            changes.append(change)
        else:
            change = pl.pallas_call(
                functools.partial(last_kernel, sn),
                grid=(1,),
                out_shape=jax.ShapeDtypeStruct((Z, mine, T), BF16),
                in_specs=[VMEM] * 5 + [d_spec(0)],
                out_specs=VMEM,
                scratch_shapes=[pltpu.VMEM((sn, T), F32)],
                compiler_params=PARAMS,
                name="backward_0",
            )(solved[0], arrived, *changes, diag_inverse)
    column = lax.all_to_all(change, "z", 0, 0, tiled=True)
    pieces = [column] + [lax.ppermute(column, "y", shift(Y, -s % Y)) for s in range(1, Y)]
    pieces = jnp.concatenate(pieces, axis=0).reshape(Y * Z * mine, T)
    to = jnp.arange(mine * K)
    source = jnp.arange(Y * Z * mine)
    column_k = (source // mine) % Z * Y + (source // (mine * Z) + y) % Y
    source = (source % mine) * K + column_k
    sort = (to[:, None] == source[None, :]).astype(BF16)
    change = jnp.dot(sort, pieces, preferred_element_type=F32)
    new_estimate = estimate + change.reshape(estimate.shape)
    return new_estimate, residual


def solution(mesh):
    grid = jax.sharding.Mesh(mesh.devices.reshape(Z, Y, X, CORE), ("z", "y", "x", "core"))
    every, snode = ("z", "y", "x", "core"), ("x", "core")
    in_specs = (
        P(every, None, None),
        P(every),
        P(every),
        P(every, None, None),
        P(None, snode, None, None),
        P(None, snode, None, None),
        P(None, snode, None, None, None),
        P(None, snode, None),
    )
    out_specs = (P(None, snode, None, None), P(every, None, None))
    return jax.shard_map(local, mesh=grid, in_specs=in_specs, out_specs=out_specs, check_vma=False)
```

time: 540 us -> 150 us (0.28)
  waiting for transfers between devices: 396 us -> 33.9 us
  matrix products: 46 us -> 2.02 us
  local copies, waits for them, and re-layouts: 32.2 us -> 5.23 us
  blocking collectives: 39.9 us -> 64.8 us
  starting transfers between devices: 0.21 us -> 23 us
  Pallas kernels: 0 us -> 16.9 us
  between operations: 14 us -> 0.85 us
    psum x1 -> x0, waiting for transfers between devices: 269 us -> none  [local(): lax.psum(spread_terms.reshape(levels, level_width, flat_width), ('rows',...]
    reduce_scatter x3 -> x0, waiting for transfers between devices: 95.6 us -> none  [local(): lax.psum_scatter(level_terms, 'snode', scatter_dimension=0, tiled=True)]
    all_to_all x0 -> x7, blocking collectives: none -> 64.8 us  [the longest x3 24.2 us: local(): arrived = lax.all_to_all(out, snode, 0, 0, tiled=True)]
    dot_general x23 -> x2, matrix products: 46 us -> 2.02 us  [the longest x1 1.16 us: local(): change = jnp.dot(sort, pieces, preferred_element_type=F32)]
    all_gather x3 -> x0, blocking collectives: 39.9 us -> none  [local(): lax.all_gather(value.astype(jnp.bfloat16), 'snode', axis=0, tiled=True)]
    all_gather x1 -> x0, waiting for transfers between devices: 31 us -> none  [local(): lax.all_gather(estimate_low, 'snode', axis=1, tiled=True)]
    ppermute x0 -> x13, waiting for transfers between devices: none -> 18.1 us  [the longest x1 5.58 us: local(): far = lax.ppermute(jnp.where(core == 0, behind, ahead), snode, onward)]
    pallas_call x0 -> x11, Pallas kernels: none -> 16.9 us  [the longest x1 4.36 us: local(): pl.pallas_call(functools.partial(tile_kernel, len(blocks)), out_shape=(ja...]
  transfers between devices with their start and end apart: 5 -> 15, of which waited for: 5 -> 11; matrix products, arithmetic and copies ran while one was open for 0% -> 0% of each run, Pallas kernels for 0% -> 4%
where the time goes in v1:
time: 150 us; the launch traced here: 149 us
  blocking collectives  64.8 us (43%)
  waiting for transfers between devices  33.9 us (23%)
  starting transfers between devices  23 us (15%)
  Pallas kernels  16.9 us (11%)
  local copies, waits for them, and re-layouts  5.23 us (3%)
  other arithmetic  2.46 us (2%)
  matrix products  2.02 us (1%)
    all_to_all x3, blocking collectives, local(): arrived = lax.all_to_all(out, snode, 0, 0, tiled=True)  24.2 us
    all_to_all x3, blocking collectives, local(): known.append(lax.all_to_all(out, snode, 0, 0, tiled=True))  24 us
    all_to_all x1, blocking collectives, local(): lax.all_to_all(total.astype(BF16).reshape(Z, mine, T), 'z', 0, 0, tiled=T...  16.6 us
    all_to_all x1, waiting for transfers between devices, local(): column = lax.all_to_all(change, 'z', 0, 0, tiled=True)  8.28 us
    all_to_all x1, waiting for transfers between devices, local(): recv = lax.all_to_all(send, snode, 0, 0, tiled=True)  7.5 us
    all_to_all x1, starting transfers between devices, local(): recv = lax.all_to_all(send, snode, 0, 0, tiled=True)  6.69 us
    ppermute x1, waiting for transfers between devices, local(): far = lax.ppermute(jnp.where(core == 0, behind, ahead), snode, onward)  5.58 us
    unnamed x17, local copies, waits for them, and re-layouts  4.88 us
  transfers between devices with their start and end apart: 15, of which 11 were waited for; matrix products, arithmetic and copies ran while one was open for 0% of the time, Pallas kernels for 4%

profile of v1, /device:TPU:2, one launch (start us, length us, event | category | flops | bytes accessed | tf_op | source)
XLA Modules:
  0.0 149.1 jit_solution(7981229203414311453)
XLA Ops:
  0.6 1.1 convert_element_type.45
  1.7 2.3 %collective-permute-start = (bf16[16,32,256]{2,1,0:T(8,128)(2,1)S(1)}, bf16[16,32,256]{2,1,0:T(8,128)(2,1)}, u32[]{:S(2)}, u32[]{:S(2)}) collective-permute-start(bf16[16,32,256]{2,1,0:T(8,128)(2,1)S(1)} %bitcast.20), channel_id=1, source_target_pairs={{0,6},{2,0},{4,2},{6,4},{1,7},{3,1},{5,3},{7,5},{8,14},{10,8},{12,... | collective-permute-start | bytes 786440 | tf_op jit(solution)/shard_map/ppermute | solution.py:233
  4.1 1.9 %bring_near.2 = (bf16[24,256,256]{2,1,0:T(8,128)(2,1)S(1)}, f32[8,32,256]{2,1,0:T(8,128)S(1)}) custom-call(bf16[24,256,256]{2,1,0:T(8,128)(2,1)} %refs_0_.2, f32[8,32,256]{2,1,0:T(8,128)} %refs_1_.1), custom_call_target="tpu_custom_call" | custom-call | tf_op jit(solution)/shard_map/bring_near/pallas_call | solution.py:111
  6.7 1.8 %plan.1 = (s32[5,24]{1,0:T(8,128)S(1)}, bf16[8,16,256]{2,1,0:T(8,128)(2,1)S(1)}) custom-call(s32[1]{0:T(128)} %bitcast.here_ref, s32[24]{0:T(128)} %col_ref.1, s32[24]{0:T(128)} %row_ref.1), custom_call_target="tpu_custom_call" | custom-call | tf_op jit(solution)/shard_map/plan/pallas_call | solution.py:236
  8.5 1.5 collective-permute-done.refs_2_
  9.9 1.3 collective-permute-done.1.refs_6_
  11.2 1.0 broadcast_select_fusion
  14.1 5.6 %collective-permute-done.4.refs_4_ = bf16[16,32,256]{2,1,0:T(8,128)(2,1)} collective-permute-done((bf16[16,32,256]{2,1,0:T(8,128)(2,1)S(1)}, bf16[16,32,256]{2,1,0:T(8,128)(2,1)}, u32[]{:S(2)}, u32[]{:S(2)}) %collective-permute-start.4) | collective-permute-done | bytes 262176 | tf_op jit(solution)/shard_map/ppermute | solution.py:255
  19.7 1.8 %collective-permute-done.5.refs_5_ = bf16[16,32,256]{2,1,0:T(8,128)(2,1)} collective-permute-done((bf16[16,32,256]{2,1,0:T(8,128)(2,1)}, bf16[16,32,256]{2,1,0:T(8,128)(2,1)}, u32[]{:S(2)}, u32[]{:S(2)}) %collective-permute-start.5) | collective-permute-done | bytes 262176 | tf_op jit(solution)/shard_map/ppermute | solution.py:256
  22.5 4.4 %tile_products.1 = (f32[8,32,256]{2,1,0:T(8,128)}, bf16[104,16,256]{2,1,0:T(8,128)(2,1)S(1)}) custom-call(s32[5,24]{1,0:T(8,128)S(1)} %get-tuple-element.37.plan_ref, bf16[8,16,256]{2,1,0:T(8,128)(2,1)S(1)} %get-tuple-element.40.note_ref, f32[8,32,256]{2,1,0:T(8,128)S(1)} %copy-done.5, bf16[24,256,256]{2,1,0:T(8,128)(2,1)S(1)} %get-tuple-element.42.a_ref, ...), custom_call_target="tpu_custom_call" | custom-call | tf_op jit(solution)/shard_map/tile_products/pallas_call | solution.py:259
  27.8 6.7 %all-to-all-start = ((bf16[104,16,256]{2,1,0:T(8,128)(2,1)}), bf16[104,16,256]{2,1,0:T(8,128)(2,1)S(1)}, u32[]{:S(2)}, u32[]{:S(2)}) async-start(bf16[104,16,256]{2,1,0:T(8,128)(2,1)} %copy-done.3), calls=%async_computation | async-start | bytes 1703936 | tf_op jit(solution)/shard_map/all_to_all | solution.py:290
  34.8 2.4 %bring_near.3.refs_1_.refs_2_.refs_3_.c_ref = bf16[3,4,3,256,256]{4,3,2,1,0:T(8,128)(2,1)S(1)} custom-call(bf16[3,4,3,256,256]{4,3,2,1,0:T(8,128)(2,1)} %refs_0_.3, f32[8,32,256]{2,1,0:T(8,128)} %get-tuple-element.36.refs_1_), custom_call_target="tpu_custom_call" | custom-call | tf_op jit(solution)/shard_map/bring_near/pallas_call | solution.py:111
  37.2 2.1 %copy-done = bf16[3,4,3,256,256]{4,3,2,1,0:T(8,128)(2,1)} copy-done((bf16[3,4,3,256,256]{4,3,2,1,0:T(8,128)(2,1)}, bf16[3,4,3,256,256]{4,3,2,1,0:T(8,128)(2,1)S(1)}, u32[]{:S(2)}) %copy-start) | copy-done | bytes 4718616
  39.4 7.5 %all-to-all-done = bf16[104,16,256]{2,1,0:T(8,128)(2,1)S(1)} async-done(((bf16[104,16,256]{2,1,0:T(8,128)(2,1)}), bf16[104,16,256]{2,1,0:T(8,128)(2,1)S(1)}, u32[]{:S(2)}, u32[]{:S(2)}) %all-to-all-start) | async-done | bytes 852000 | tf_op jit(solution)/shard_map/all_to_all | solution.py:290
  48.3 3.1 %collective-permute-start.9 = (bf16[128,256]{1,0:T(8,128)(2,1)S(1)}, bf16[128,256]{1,0:T(8,128)(2,1)S(1)}, u32[]{:S(2)}, u32[]{:S(2)}) collective-permute-start(bf16[128,256]{1,0:T(8,128)(2,1)S(1)} %get-tuple-element.73), channel_id=1, source_target_pairs={{0,24},{8,0},{16,8},{24,16},{1,25},{9,1},{17,9},{25,17},{2,26},{10... | collective-permute-start | bytes 196616 | tf_op jit(solution)/shard_map/ppermute | solution.py:306
  53.3 3.9 %collective-permute-done.8 = bf16[128,256]{1,0:T(8,128)(2,1)S(1)} collective-permute-done((bf16[128,256]{1,0:T(8,128)(2,1)S(1)}, bf16[128,256]{1,0:T(8,128)(2,1)S(1)}, u32[]{:S(2)}, u32[]{:S(2)}) %collective-permute-start.8) | collective-permute-done | bytes 65568 | tf_op jit(solution)/shard_map/ppermute | solution.py:306
  57.9 16.6 %all_to_all.45.parts_ref = bf16[8,16,256]{2,1,0:T(8,128)(2,1)S(1)} all-to-all(bf16[8,16,256]{2,1,0:T(8,128)(2,1)S(1)} %bitcast.27), channel_id=1, replica_groups=mesh['z'=8,'y'=4,'x'=4,'core'=2] {'z'}, dimensions={0} | all-to-all | bytes 131072 | tf_op jit(solution)/shard_map/all_to_all | solution.py:307
  74.7 8.0 %all_to_all.46.refs_0_ = f32[8,8,256]{2,1,0:T(8,128)S(1)} all-to-all(f32[8,8,256]{2,1,0:T(8,128)S(1)} %get-tuple-element.53), channel_id=1, replica_groups=mesh['z'=8,'y'=4,'x'=4,'core'=2] {'x','core'}, dimensions={0} | all-to-all | bytes 131072 | tf_op jit(solution)/shard_map/all_to_all | solution.py:332
  83.5 8.0 %all_to_all.47.refs_1_ = f32[8,8,256]{2,1,0:T(8,128)S(1)} all-to-all(f32[8,8,256]{2,1,0:T(8,128)S(1)} %get-tuple-element.57), channel_id=1, replica_groups=mesh['z'=8,'y'=4,'x'=4,'core'=2] {'x','core'}, dimensions={0} | all-to-all | bytes 131072 | tf_op jit(solution)/shard_map/all_to_all | solution.py:332
  92.4 8.0 %all_to_all.48.refs_2_ = f32[8,8,256]{2,1,0:T(8,128)S(1)} all-to-all(f32[8,8,256]{2,1,0:T(8,128)S(1)} %get-tuple-element.61), channel_id=1, replica_groups=mesh['z'=8,'y'=4,'x'=4,'core'=2] {'x','core'}, dimensions={0} | all-to-all | bytes 131072 | tf_op jit(solution)/shard_map/all_to_all | solution.py:332
  100.4 1.6 %turn.1 = (f32[4,256]{1,0:T(4,128)S(1)}, f32[8,8,256]{2,1,0:T(8,128)S(1)}, f32[128,256]{1,0:T(8,128)S(1)}) custom-call(f32[16,256]{1,0:T(8,128)S(1)} %get-tuple-element.51.g_ref, bf16[16,192]{1,0:T(8,128)(2,1)S(1)} %fusion.17.look_ref, bf16[192,16]{1,0:T(8,128)(2,1)S(1)} %fusion.14.scatter_ref, f32[8,8,256]{2,1,0:T(8,128)S(1)} %all_to_all.46.refs_0_, ...), custom_call_target="tpu_custom_call" | custom-call | tf_op jit(solution)/shard_map/turn/pallas_call | solution.py:346
  102.0 8.2 %all_to_all.49.recv_ref = f32[8,8,256]{2,1,0:T(8,128)S(1)} all-to-all(f32[8,8,256]{2,1,0:T(8,128)S(1)} %get-tuple-element.62), channel_id=1, replica_groups=mesh['z'=8,'y'=4,'x'=4,'core'=2] {'x','core'}, dimensions={0} | all-to-all | bytes 131072 | tf_op jit(solution)/shard_map/all_to_all | solution.py:358
  110.2 1.1 backward_2.1
  111.3 8.0 %all_to_all.50.recv_ref = f32[8,8,256]{2,1,0:T(8,128)S(1)} all-to-all(f32[8,8,256]{2,1,0:T(8,128)S(1)} %get-tuple-element.65), channel_id=1, replica_groups=mesh['z'=8,'y'=4,'x'=4,'core'=2] {'x','core'}, dimensions={0} | all-to-all | bytes 131072 | tf_op jit(solution)/shard_map/all_to_all | solution.py:358
  119.3 1.1 backward_1.1
  120.3 8.0 %all_to_all.51.recv_ref = f32[8,8,256]{2,1,0:T(8,128)S(1)} all-to-all(f32[8,8,256]{2,1,0:T(8,128)S(1)} %get-tuple-element.68), channel_id=1, replica_groups=mesh['z'=8,'y'=4,'x'=4,'core'=2] {'x','core'}, dimensions={0} | all-to-all | bytes 131072 | tf_op jit(solution)/shard_map/all_to_all | solution.py:358
  129.2 3.4 %all-to-all-start.8 = ((bf16[8,16,256]{2,1,0:T(8,128)(2,1)}), bf16[8,16,256]{2,1,0:T(8,128)(2,1)S(1)}, u32[]{:S(2)}, u32[]{:S(2)}) async-start(bf16[8,16,256]{2,1,0:T(8,128)(2,1)} %backward_0.1), calls=%async_computation.8 | async-start | bytes 131072 | tf_op jit(solution)/shard_map/all_to_all | solution.py:383
  132.6 8.3 %all-to-all-done.8 = bf16[8,16,256]{2,1,0:T(8,128)(2,1)S(1)} async-done(((bf16[8,16,256]{2,1,0:T(8,128)(2,1)}), bf16[8,16,256]{2,1,0:T(8,128)(2,1)S(1)}, u32[]{:S(2)}, u32[]{:S(2)}) %all-to-all-start.8) | async-done | bytes 65568 | tf_op jit(solution)/shard_map/all_to_all | solution.py:383
  140.9 2.0 %collective-permute-start.11 = (bf16[8,16,256]{2,1,0:T(8,128)(2,1)S(1)}, bf16[8,16,256]{2,1,0:T(8,128)(2,1)S(1)}, u32[]{:S(2)}, u32[]{:S(2)}) collective-permute-start(bf16[8,16,256]{2,1,0:T(8,128)(2,1)S(1)} %all-to-all-done.8), channel_id=1, source_target_pairs={{0,16},{8,24},{16,0},{24,8},{1,17},{9,25},{17,1},{25,9},{2,18},{10... | collective-permute-start | bytes 196616 | tf_op jit(solution)/shard_map/ppermute | solution.py:384
  142.9 1.9 %collective-permute-start.10 = (bf16[8,16,256]{2,1,0:T(8,128)(2,1)S(1)}, bf16[8,16,256]{2,1,0:T(8,128)(2,1)S(1)}, u32[]{:S(2)}, u32[]{:S(2)}) collective-permute-start(bf16[8,16,256]{2,1,0:T(8,128)(2,1)S(1)} %all-to-all-done.8), channel_id=1, source_target_pairs={{0,24},{8,0},{16,8},{24,16},{1,25},{9,1},{17,9},{25,17},{2,26},{10... | collective-permute-start | bytes 196616 | tf_op jit(solution)/shard_map/ppermute | solution.py:384
  144.8 2.2 %collective-permute-done.12 = bf16[8,16,256]{2,1,0:T(8,128)(2,1)S(1)} collective-permute-done((bf16[8,16,256]{2,1,0:T(8,128)(2,1)S(1)}, bf16[8,16,256]{2,1,0:T(8,128)(2,1)S(1)}, u32[]{:S(2)}, u32[]{:S(2)}) %collective-permute-start.12) | collective-permute-done | bytes 65568 | tf_op jit(solution)/shard_map/ppermute | solution.py:384
  148.0 1.2 convolution_add_fusion
  (59 shorter events, 12.5 us)
Async XLA Ops:
  1.7 8.2 %collective-permute-start = (bf16[16,32,256]{2,1,0:T(8,128)(2,1)S(1)}, bf16[16,32,256]{2,1,0:T(8,128)(2,1)}, u32[]{:S(2)}, u32[]{:S(2)}) collective-permute-start(bf16[16,32,256]{2,1,0:T(8,128)(2,1)S(1)} %bitcast.20), channel_id=1, source_target_pairs={{0,6},{2,0},{4,2},{6,4},{1,7},{3,1},{5,3},{7,5},{8,14},{10,8},{12,... | collective-permute-start | bytes 786440 | tf_op jit(solution)/shard_map/ppermute | solution.py:233
  4.1 7.2 %collective-permute-start.1 = (bf16[16,32,256]{2,1,0:T(8,128)(2,1)S(1)}, bf16[16,32,256]{2,1,0:T(8,128)(2,1)}, u32[]{:S(2)}, u32[]{:S(2)}) collective-permute-start(bf16[16,32,256]{2,1,0:T(8,128)(2,1)S(1)} %bitcast.21), channel_id=1, source_target_pairs={{0,2},{2,4},{4,6},{6,0},{1,3},{3,5},{5,7},{7,1},{8,10},{10,12},{12... | collective-permute-start | bytes 786440 | tf_op jit(solution)/shard_map/ppermute | solution.py:234
  6.0 0.7 copy-start.4
  12.2 7.5 %collective-permute-start.4 = (bf16[16,32,256]{2,1,0:T(8,128)(2,1)S(1)}, bf16[16,32,256]{2,1,0:T(8,128)(2,1)}, u32[]{:S(2)}, u32[]{:S(2)}) collective-permute-start(bf16[16,32,256]{2,1,0:T(8,128)(2,1)S(1)} %broadcast_select_fusion), channel_id=1, source_target_pairs={{0,2},{1,7},{2,4},{3,1},{4,6},{5,3},{6,0},{7,5},{8,10},{9,15},{10,... | collective-permute-start | bytes 786440 | tf_op jit(solution)/shard_map/ppermute | solution.py:255
  12.7 7.0 %collective-permute-start.2 = (bf16[16,32,256]{2,1,0:T(8,128)(2,1)S(1)}, bf16[16,32,256]{2,1,0:T(8,128)(2,1)}, u32[]{:S(2)}, u32[]{:S(2)}) collective-permute-start(bf16[16,32,256]{2,1,0:T(8,128)(2,1)S(1)} %bitcast.22), channel_id=1, source_target_pairs={{0,1},{1,0},{2,3},{3,2},{4,5},{5,4},{6,7},{7,6},{8,9},{9,8},{10,11... | collective-permute-start | bytes 786440 | tf_op jit(solution)/shard_map/ppermute | solution.py:235
  13.6 6.1 %collective-permute-start.3 = (bf16[16,32,256]{2,1,0:T(8,128)(2,1)}, bf16[16,32,256]{2,1,0:T(8,128)(2,1)}, u32[]{:S(2)}, u32[]{:S(2)}) collective-permute-start(bf16[16,32,256]{2,1,0:T(8,128)(2,1)} %collective-permute-done.refs_2_), channel_id=1, source_target_pairs={{0,1},{1,0},{2,3},{3,2},{4,5},{5,4},{6,7},{7,6},{8,9},{9,8},{10,11... | collective-permute-start | bytes 786440 | tf_op jit(solution)/shard_map/ppermute | solution.py:256
  13.6 6.1 %collective-permute-start.6 = (bf16[16,32,256]{2,1,0:T(8,128)(2,1)}, bf16[16,32,256]{2,1,0:T(8,128)(2,1)}, u32[]{:S(2)}, u32[]{:S(2)}) collective-permute-start(bf16[16,32,256]{2,1,0:T(8,128)(2,1)} %collective-permute-done.1.refs_6_), channel_id=1, source_target_pairs={{0,1},{1,0},{2,3},{3,2},{4,5},{5,4},{6,7},{7,6},{8,9},{9,8},{10,11... | collective-permute-start | bytes 786440 | tf_op jit(solution)/shard_map/ppermute | solution.py:256
  19.7 1.9 %collective-permute-start.5 = (bf16[16,32,256]{2,1,0:T(8,128)(2,1)}, bf16[16,32,256]{2,1,0:T(8,128)(2,1)}, u32[]{:S(2)}, u32[]{:S(2)}) collective-permute-start(bf16[16,32,256]{2,1,0:T(8,128)(2,1)} %collective-permute-done.4.refs_4_), channel_id=1, source_target_pairs={{0,1},{1,0},{2,3},{3,2},{4,5},{5,4},{6,7},{7,6},{8,9},{9,8},{10,11... | collective-permute-start | bytes 786440 | tf_op jit(solution)/shard_map/ppermute | solution.py:256
  21.6 1.0 copy-start.5
  22.5 12.0 %copy-start.7 = (s32[3,4,3]{2,1,0:T(4,128)S(1)}, s32[3,4,3]{2,1,0:T(4,128)}, u32[]{:S(2)}) copy-start(s32[3,4,3]{2,1,0:T(4,128)} %param.15) | copy-start | bytes 436
  26.9 0.9 copy-start.3
  27.8 19.1 %all-to-all-start = ((bf16[104,16,256]{2,1,0:T(8,128)(2,1)}), bf16[104,16,256]{2,1,0:T(8,128)(2,1)S(1)}, u32[]{:S(2)}, u32[]{:S(2)}) async-start(bf16[104,16,256]{2,1,0:T(8,128)(2,1)} %copy-done.3), calls=%async_computation | async-start | bytes 1703936 | tf_op jit(solution)/shard_map/all_to_all | solution.py:290
  37.2 2.1 %copy-start = (bf16[3,4,3,256,256]{4,3,2,1,0:T(8,128)(2,1)}, bf16[3,4,3,256,256]{4,3,2,1,0:T(8,128)(2,1)S(1)}, u32[]{:S(2)}) copy-start(bf16[3,4,3,256,256]{4,3,2,1,0:T(8,128)(2,1)S(1)} %bring_near.3.refs_1_.refs_2_.refs_3_.c_ref) | copy-start | bytes 14155780
  39.4 35.1 %copy-start.2 = (bf16[4,4,256,256]{3,2,1,0:T(8,128)(2,1)S(1)}, bf16[4,4,256,256]{3,2,1,0:T(8,128)(2,1)}, u32[]{:S(2)}) copy-start(bf16[4,4,256,256]{3,2,1,0:T(8,128)(2,1)} %d_ref.7) | copy-start | bytes 6291460
  47.4 35.3 %copy-start.1 = (bf16[3,4,3,256,256]{4,3,2,1,0:T(8,128)(2,1)S(1)}, bf16[3,4,3,256,256]{4,3,2,1,0:T(8,128)(2,1)}, u32[]{:S(2)}) copy-start(bf16[3,4,3,256,256]{4,3,2,1,0:T(8,128)(2,1)} %copy-done) | copy-start | bytes 14155780
  48.3 5.0 %collective-permute-start.9 = (bf16[128,256]{1,0:T(8,128)(2,1)S(1)}, bf16[128,256]{1,0:T(8,128)(2,1)S(1)}, u32[]{:S(2)}, u32[]{:S(2)}) collective-permute-start(bf16[128,256]{1,0:T(8,128)(2,1)S(1)} %get-tuple-element.73), channel_id=1, source_target_pairs={{0,24},{8,0},{16,8},{24,16},{1,25},{9,1},{17,9},{25,17},{2,26},{10... | collective-permute-start | bytes 196616 | tf_op jit(solution)/shard_map/ppermute | solution.py:306
  51.3 5.8 %collective-permute-start.8 = (bf16[128,256]{1,0:T(8,128)(2,1)S(1)}, bf16[128,256]{1,0:T(8,128)(2,1)S(1)}, u32[]{:S(2)}, u32[]{:S(2)}) collective-permute-start(bf16[128,256]{1,0:T(8,128)(2,1)S(1)} %get-tuple-element.74), channel_id=1, source_target_pairs={{0,16},{8,24},{16,0},{24,8},{1,17},{9,25},{17,1},{25,9},{2,18},{10... | collective-permute-start | bytes 196616 | tf_op jit(solution)/shard_map/ppermute | solution.py:306
  52.0 5.8 %collective-permute-start.7 = (bf16[128,256]{1,0:T(8,128)(2,1)S(1)}, bf16[128,256]{1,0:T(8,128)(2,1)S(1)}, u32[]{:S(2)}, u32[]{:S(2)}) collective-permute-start(bf16[128,256]{1,0:T(8,128)(2,1)S(1)} %get-tuple-element.72), channel_id=1, source_target_pairs={{0,8},{8,16},{16,24},{24,0},{1,9},{9,17},{17,25},{25,1},{2,10},{10... | collective-permute-start | bytes 196616 | tf_op jit(solution)/shard_map/ppermute | solution.py:306
  119.3 28.7 %copy-start.6 = (f32[4,4,32,256]{3,2,1,0:T(8,128)S(1)}, f32[4,4,32,256]{3,2,1,0:T(8,128)}, u32[]{:S(2)}) copy-start(f32[4,4,32,256]{3,2,1,0:T(8,128)} %param.12) | copy-start | bytes 1572868
  129.2 11.7 %all-to-all-start.8 = ((bf16[8,16,256]{2,1,0:T(8,128)(2,1)}), bf16[8,16,256]{2,1,0:T(8,128)(2,1)S(1)}, u32[]{:S(2)}, u32[]{:S(2)}) async-start(bf16[8,16,256]{2,1,0:T(8,128)(2,1)} %backward_0.1), calls=%async_computation.8 | async-start | bytes 131072 | tf_op jit(solution)/shard_map/all_to_all | solution.py:383
  140.9 6.2 %collective-permute-start.12 = (bf16[8,16,256]{2,1,0:T(8,128)(2,1)S(1)}, bf16[8,16,256]{2,1,0:T(8,128)(2,1)S(1)}, u32[]{:S(2)}, u32[]{:S(2)}) collective-permute-start(bf16[8,16,256]{2,1,0:T(8,128)(2,1)S(1)} %all-to-all-done.8), channel_id=1, source_target_pairs={{0,8},{8,16},{16,24},{24,0},{1,9},{9,17},{17,25},{25,1},{2,10},{10... | collective-permute-start | bytes 196616 | tf_op jit(solution)/shard_map/ppermute | solution.py:384
  140.9 6.2 %collective-permute-start.11 = (bf16[8,16,256]{2,1,0:T(8,128)(2,1)S(1)}, bf16[8,16,256]{2,1,0:T(8,128)(2,1)S(1)}, u32[]{:S(2)}, u32[]{:S(2)}) collective-permute-start(bf16[8,16,256]{2,1,0:T(8,128)(2,1)S(1)} %all-to-all-done.8), channel_id=1, source_target_pairs={{0,16},{8,24},{16,0},{24,8},{1,17},{9,25},{17,1},{25,9},{2,18},{10... | collective-permute-start | bytes 196616 | tf_op jit(solution)/shard_map/ppermute | solution.py:384
  142.9 5.0 %collective-permute-start.10 = (bf16[8,16,256]{2,1,0:T(8,128)(2,1)S(1)}, bf16[8,16,256]{2,1,0:T(8,128)(2,1)S(1)}, u32[]{:S(2)}, u32[]{:S(2)}) collective-permute-start(bf16[8,16,256]{2,1,0:T(8,128)(2,1)S(1)} %all-to-all-done.8), channel_id=1, source_target_pairs={{0,24},{8,0},{16,8},{24,16},{1,25},{9,1},{17,9},{25,17},{2,26},{10... | collective-permute-start | bytes 196616 | tf_op jit(solution)/shard_map/ppermute | solution.py:384

commit v2 on v1

--- a/solution.py
+++ b/solution.py
@@ -48,23 +48,27 @@
     note_ref[...] = note[...].astype(BF16)
 
 
-def tile_kernel(n_blocks, plan_ref, note_ref, side_ref, a_ref, *refs):
+def tile_kernel(n_blocks, core_ref, plan_ref, note_ref, side_ref, a_ref, *refs):
     blocks = refs[:n_blocks]
-    res_ref, send_ref, x_all, low_ref, sems = refs[n_blocks:]
+    core = core_ref[0]
+    res_ref, send_ref, x_all, low_ref, sems, note_sems = refs[n_blocks:]
     tiles = a_ref.shape[0]
     mine = x_all.shape[0] // OWNERS
     half = x_all.shape[1] // 2
     per = send_ref.shape[0] // OWNERS
-    copies = []
+    copies = [pltpu.make_async_copy(side_ref, res_ref, sems.at[len(blocks)])]
+    own, rest = (2 * X - 2 - 4 * core) * mine, (2 + 4 * core) * mine
+    spots = [0, mine, 4 * mine, 9 * mine // 2, 5 * mine, 11 * mine // 2]
+    spots += [own, own + mine // 2, own + mine, rest, rest + mine, rest + 3 * mine // 2]
     for i, block in enumerate(blocks):
-        target = x_all.at[pl.ds(i * mine, mine)]
+        target = x_all.at[pl.ds(spots[i], block.shape[0])]
         copies.append(pltpu.make_async_copy(block, target, sems.at[i]))
     for copy in copies:
         copy.start()
     send_ref[...] = jnp.zeros_like(send_ref)
     for o in range(OWNERS):
-        send_ref[o * per + per - 1] = note_ref[o]
-    res_ref[...] = side_ref[...]
+        copies.append(pltpu.make_async_copy(note_ref.at[o], send_ref.at[(o + 1) * per - 1], note_sems.at[o]))
+        copies[-1].start()
     for copy in copies:
         copy.wait()
     for t in range(tiles):
@@ -107,7 +111,7 @@
     operands = [in_hbm(x) for x in operands]
     if after is not None:
         operands.append(in_hbm(after))
-    out_shape = [pltpu.VMEM(x.shape, x.dtype) if after is not None else jax.ShapeDtypeStruct(x.shape, x.dtype) for x in operands]
+    out_shape = [jax.ShapeDtypeStruct(x.shape, x.dtype) for x in operands]
     return pl.pallas_call(
         functools.partial(near_kernel, n, parts),
         out_shape=tuple(out_shape[:n]),
@@ -230,14 +234,22 @@
     e = estimate.astype(BF16).reshape(mine, K, T)
     other = functools.partial(lax.ppermute, axis_name="core", perm=shift(CORE, 1))
 
-    ahead = lax.ppermute(e, "x", shift(X, X - 1))
-    behind = lax.ppermute(e, "x", shift(X, 1))
+    def along(block, way=1):
+        perm = []
+        for x in range(X):
+            perm.append((x * CORE, (x + way) % X * CORE))
+            perm.append((x * CORE + 1, (x - way) % X * CORE + 1))
+        return lax.ppermute(block, snode, perm)
+
+    half = mine // 2
+    first = [along(e[:half]), along(e[half:])]
+    second = along(e, -1)
     swapped = other(e)
     plan, note = pl.pallas_call(
         functools.partial(plan_kernel, sn),
         out_shape=(
             jax.ShapeDtypeStruct((5, tiles), jnp.int32),
-            jax.ShapeDtypeStruct((OWNERS, 16, T), BF16),
+            pltpu.HBM((OWNERS, 16, T), BF16),
         ),
         in_specs=[SMEM, SMEM, SMEM],
         out_specs=(SMEM, VMEM),
@@ -245,34 +257,38 @@
         compiler_params=PARAMS,
         name="plan",
     )(here, in_hbm(tile_col), in_hbm(tile_row))
-    a_near, side = bring_near(None, a_tiles, right_side)
-    ahead, behind, note, a_near = lax.optimization_barrier((ahead, behind, note, a_near))
-    core = lax.axis_index("core")
-    onward = []
-    for x in range(X):
-        onward.append((x * CORE, (x + 1) % X * CORE))
-        onward.append((x * CORE + 1, (x - 1) % X * CORE + 1))
-    far = lax.ppermute(jnp.where(core == 0, behind, ahead), snode, onward)
-    blocks = [e, swapped, ahead, other(ahead), far, other(far), behind, other(behind)]
+    first_lo, first_hi, note = lax.optimization_barrier((*first, note))
+    first = [first_lo, first_hi]
+    far = [along(x) for x in first]
+    (a_near,) = bring_near(None, a_tiles)
+    second, a_near = lax.optimization_barrier((second, a_near))
+    side = in_hbm(right_side)
+    blocks = [e, swapped] + far + [other(x) for x in far] + first + [other(second), second] + [other(x) for x in first]
 
     slot_rows = CAP * K + 16
     residual, send = pl.pallas_call(
         functools.partial(tile_kernel, len(blocks)),
         out_shape=(
             jax.ShapeDtypeStruct((row_tiles, K, T), F32),
-            jax.ShapeDtypeStruct((OWNERS * slot_rows // 16, 16, T), BF16),
+            pltpu.HBM((OWNERS * slot_rows // 16, 16, T), BF16),
         ),
-        in_specs=[SMEM, VMEM, VMEM, VMEM] + [ANY] * len(blocks),
+        in_specs=[SMEM, SMEM, ANY, ANY, VMEM] + [ANY] * len(blocks),
         out_specs=(VMEM, VMEM),
         scratch_shapes=[
             pltpu.VMEM((OWNERS * mine, K, T), BF16),
             pltpu.VMEM((row_tiles, K, T), BF16),
-            pltpu.SemaphoreType.DMA((len(blocks),)),
+            pltpu.SemaphoreType.DMA((len(blocks) + 1,)),
+            pltpu.SemaphoreType.DMA((OWNERS,)),
         ],
         compiler_params=PARAMS,
         name="tile_products",
-    )(plan, note, side, a_near, *blocks)
-
+    )(lax.axis_index("core").reshape(1), plan, in_hbm(note), side, a_near, *blocks)
+
+    to = jnp.arange(mine * K)
+    y = lax.axis_index("y")
+    place = jnp.arange(Y * Z * mine)
+    column_k = (place // mine) % Z * Y + (place // (mine * Z) + y) % Y
+    place = (place % mine) * K + column_k
     send, coupling_source = lax.optimization_barrier((send, coupling_source))
     source = coupling_source.reshape(levels - 1, -1)
     block_rows = 8
@@ -289,7 +305,7 @@
 
     recv = lax.all_to_all(send, snode, 0, 0, tiled=True)
     (c_near,) = bring_near(residual, coupling)
-    recv, c_near, look, scatter = lax.optimization_barrier((recv, c_near, look, scatter))
+    recv, c_near, look, scatter, to, place = lax.optimization_barrier((recv, c_near, look, scatter, to, place))
     recv = recv.reshape(OWNERS, slot_rows, T)
 
     spot = recv[:, CAP * K : CAP * K + CAP, 0].astype(jnp.int32) - 1
@@ -339,7 +355,7 @@
                 out_specs=(VMEM, VMEM),
                 compiler_params=PARAMS,
                 name=f"forward_{level}",
-            )(g, look[level - 1], *known, in_vmem(c_near), diag_inverse)
+            )(g, look[level - 1], *known, c_near, diag_inverse)
             solved.append(value)
         else:
             out_shape = (row4, by_owner) + rest_of(level)
@@ -352,7 +368,7 @@
                 scratch_shapes=[stage],
                 compiler_params=PARAMS,
                 name="turn",
-            )(g, look[level - 1], scatter[level - 1], *known, in_vmem(c_near), diag_inverse)
+            )(g, look[level - 1], scatter[level - 1], *known, c_near, diag_inverse)
     changes = [change]
     for level in reversed(range(levels - 1)):
         arrived = lax.all_to_all(out, snode, 0, 0, tiled=True)
@@ -367,7 +383,7 @@
                 scratch_shapes=[stage],
                 compiler_params=PARAMS,
                 name=f"backward_{level}",
-            )(solved[level], arrived, rest[0], scatter[level - 1], in_vmem(c_near), diag_inverse)
+            )(solved[level], arrived, rest[0], scatter[level - 1], c_near, diag_inverse)
             changes.append(change)
         else:
             change = pl.pallas_call(
@@ -383,11 +399,7 @@
     column = lax.all_to_all(change, "z", 0, 0, tiled=True)
     pieces = [column] + [lax.ppermute(column, "y", shift(Y, -s % Y)) for s in range(1, Y)]
     pieces = jnp.concatenate(pieces, axis=0).reshape(Y * Z * mine, T)
-    to = jnp.arange(mine * K)
-    source = jnp.arange(Y * Z * mine)
-    column_k = (source // mine) % Z * Y + (source // (mine * Z) + y) % Y
-    source = (source % mine) * K + column_k
-    sort = (to[:, None] == source[None, :]).astype(BF16)
+    sort = (to[:, None] == place[None, :]).astype(BF16)
     change = jnp.dot(sort, pieces, preferred_element_type=F32)
     new_estimate = estimate + change.reshape(estimate.shape)
     return new_estimate, residual

time: 150 us -> 145 us (0.967)
  waiting for transfers between devices: 33.9 us -> 20.5 us
  blocking collectives: 64.8 us -> 75.4 us
  local copies, waits for them, and re-layouts: 5.23 us -> 3.45 us
    all_to_all x0 -> x1, blocking collectives: none -> 10.8 us  [local(): column = lax.all_to_all(change, 'z', 0, 0, tiled=True)]
    all_to_all x1 -> x0, waiting for transfers between devices: 8.28 us -> none  [local(): column = lax.all_to_all(change, 'z', 0, 0, tiled=True)]
    ppermute x6 -> x10, waiting for transfers between devices: 10.1 us -> 5.79 us  [the longest x5 4.27 us: along(): return lax.ppermute(block, snode, perm)]
    ppermute x6 -> x10, starting transfers between devices: 3.42 us -> 7.03 us  [the longest x5 5.91 us: along(): return lax.ppermute(block, snode, perm)]
    all_to_all x1 -> x0, starting transfers between devices: 3.35 us -> none  [local(): column = lax.all_to_all(change, 'z', 0, 0, tiled=True)]
    unnamed x17 -> x13, local copies, waits for them, and re-layouts: 4.88 us -> 2.3 us
  transfers between devices with their start and end apart: 15 -> 18, of which waited for: 11 -> 12; matrix products, arithmetic and copies ran while one was open for 0% -> 1% of each run, Pallas kernels for 4% -> 4%
where the time goes in v2:
time: 145 us; the launch traced here: 144 us
  blocking collectives  75.4 us (52%)
  starting transfers between devices  22.4 us (15%)
  waiting for transfers between devices  20.5 us (14%)
  Pallas kernels  17.2 us (12%)
  local copies, waits for them, and re-layouts  3.45 us (2%)
  other arithmetic  2.07 us (1%)
  matrix products  2.02 us (1%)
    all_to_all x3, blocking collectives, local(): known.append(lax.all_to_all(out, snode, 0, 0, tiled=True))  24 us
    all_to_all x3, blocking collectives, local(): arrived = lax.all_to_all(out, snode, 0, 0, tiled=True)  24 us
    all_to_all x1, blocking collectives, local(): lax.all_to_all(total.astype(BF16).reshape(Z, mine, T), 'z', 0, 0, tiled=T...  16.6 us
    all_to_all x1, blocking collectives, local(): column = lax.all_to_all(change, 'z', 0, 0, tiled=True)  10.8 us
    all_to_all x1, waiting for transfers between devices, local(): recv = lax.all_to_all(send, snode, 0, 0, tiled=True)  6.81 us
    all_to_all x1, starting transfers between devices, local(): recv = lax.all_to_all(send, snode, 0, 0, tiled=True)  6.71 us
    ppermute x5, starting transfers between devices, along(): return lax.ppermute(block, snode, perm)  5.91 us
    pallas_call x1, Pallas kernels, local(): pl.pallas_call(functools.partial(tile_kernel, len(blocks)), out_shape=(ja...  5.25 us
  transfers between devices with their start and end apart: 18, of which 12 were waited for; matrix products, arithmetic and copies ran while one was open for 1% of the time, Pallas kernels for 4%

profile of v2, /device:TPU:2, one launch (start us, length us, event | category | flops | bytes accessed | tf_op | source)
XLA Modules:
  0.0 143.8 jit_solution(2571505358464627)
XLA Ops:
  0.6 1.1 convert_element_type.45
  1.7 2.3 %collective-permute-start.2 = (bf16[16,32,256]{2,1,0:T(8,128)(2,1)S(1)}, bf16[16,32,256]{2,1,0:T(8,128)(2,1)}, u32[]{:S(2)}, u32[]{:S(2)}) collective-permute-start(bf16[16,32,256]{2,1,0:T(8,128)(2,1)S(1)} %bitcast.23), channel_id=1, source_target_pairs={{0,6},{1,3},{2,0},{3,5},{4,2},{5,7},{6,4},{7,1},{8,14},{9,11},{10,... | collective-permute-start | bytes 786440 | tf_op jit(solution)/shard_map/ppermute | solution.py:242
  4.2 1.2 collective-permute-start.1
  5.4 1.8 %plan.1 = (s32[5,24]{1,0:T(8,128)S(1)}, bf16[8,16,256]{2,1,0:T(8,128)(2,1)}) custom-call(s32[1]{0:T(128)} %bitcast.1.here_ref, s32[24]{0:T(128)} %col_ref.1, s32[24]{0:T(128)} %row_ref.1), custom_call_target="tpu_custom_call" | custom-call | tf_op jit(solution)/shard_map/plan/pallas_call | solution.py:248
  7.2 1.9 %collective-permute-done.refs_6_ = bf16[8,32,256]{2,1,0:T(8,128)(2,1)S(1)} collective-permute-done((bf16[8,32,256]{2,1,0:T(8,128)(2,1)S(1)}, bf16[8,32,256]{2,1,0:T(8,128)(2,1)S(1)}, u32[]{:S(2)}, u32[]{:S(2)}) %collective-permute-start) | collective-permute-done | bytes 131104 | tf_op jit(solution)/shard_map/ppermute | solution.py:242
  9.1 1.5 %collective-permute-done.1.refs_7_ = bf16[8,32,256]{2,1,0:T(8,128)(2,1)} collective-permute-done((bf16[8,32,256]{2,1,0:T(8,128)(2,1)S(1)}, bf16[8,32,256]{2,1,0:T(8,128)(2,1)}, u32[]{:S(2)}, u32[]{:S(2)}) %collective-permute-start.1) | collective-permute-done | bytes 131104 | tf_op jit(solution)/shard_map/ppermute | solution.py:242
  11.4 1.5 %collective-permute-start.5 = (bf16[8,32,256]{2,1,0:T(8,128)(2,1)}, bf16[8,32,256]{2,1,0:T(8,128)(2,1)}, u32[]{:S(2)}, u32[]{:S(2)}) collective-permute-start(bf16[8,32,256]{2,1,0:T(8,128)(2,1)} %collective-permute-done.1.refs_7_), channel_id=1, source_target_pairs={{0,2},{1,7},{2,4},{3,1},{4,6},{5,3},{6,0},{7,5},{8,10},{9,15},{10,... | collective-permute-start | bytes 393224 | tf_op jit(solution)/shard_map/ppermute | solution.py:242
  12.9 1.9 %bring_near.2.a_ref = bf16[24,256,256]{2,1,0:T(8,128)(2,1)S(1)} custom-call(bf16[24,256,256]{2,1,0:T(8,128)(2,1)} %refs_0_.2), custom_call_target="tpu_custom_call" | custom-call | tf_op jit(solution)/shard_map/bring_near/pallas_call | solution.py:115
  17.8 1.1 collective-permute-done.7.refs_5_
  18.9 5.2 %tile_products.1 = (f32[8,32,256]{2,1,0:T(8,128)}, bf16[104,16,256]{2,1,0:T(8,128)(2,1)}) custom-call(s32[1]{0:T(128)} %bitcast.core_ref, s32[5,24]{1,0:T(8,128)S(1)} %get-tuple-element.38.plan_ref, bf16[8,16,256]{2,1,0:T(8,128)(2,1)} %get-tuple-element.40.note_ref, f32[8,32,256]{2,1,0:T(8,128)} %side_ref.1, bf16[24,256,256]{2,1,0:T(8,128)(2,1)S(1)} %bring_near.2.a_ref, ...), custom_call_target="tpu_custom_call" | custom-call | tf_op jit(solution)/shard_map/tile_products/pallas_call | solution.py:269
  24.1 6.7 %all-to-all-start = ((bf16[104,16,256]{2,1,0:T(8,128)(2,1)}), bf16[104,16,256]{2,1,0:T(8,128)(2,1)S(1)}, u32[]{:S(2)}, u32[]{:S(2)}) async-start(bf16[104,16,256]{2,1,0:T(8,128)(2,1)} %get-tuple-element.46), calls=%async_computation | async-start | bytes 1703936 | tf_op jit(solution)/shard_map/all_to_all | solution.py:306
  31.9 2.4 %bring_near.3.refs_1_.refs_2_.refs_3_.c_ref = bf16[3,4,3,256,256]{4,3,2,1,0:T(8,128)(2,1)S(1)} custom-call(bf16[3,4,3,256,256]{4,3,2,1,0:T(8,128)(2,1)} %refs_0_.3, f32[8,32,256]{2,1,0:T(8,128)} %get-tuple-element.37.refs_1_), custom_call_target="tpu_custom_call" | custom-call | tf_op jit(solution)/shard_map/bring_near/pallas_call | solution.py:115
  34.3 2.1 %copy-done = bf16[3,4,3,256,256]{4,3,2,1,0:T(8,128)(2,1)} copy-done((bf16[3,4,3,256,256]{4,3,2,1,0:T(8,128)(2,1)}, bf16[3,4,3,256,256]{4,3,2,1,0:T(8,128)(2,1)S(1)}, u32[]{:S(2)}) %copy-start) | copy-done | bytes 4718616
  36.5 6.8 %all-to-all-done = bf16[104,16,256]{2,1,0:T(8,128)(2,1)S(1)} async-done(((bf16[104,16,256]{2,1,0:T(8,128)(2,1)}), bf16[104,16,256]{2,1,0:T(8,128)(2,1)S(1)}, u32[]{:S(2)}, u32[]{:S(2)}) %all-to-all-start) | async-done | bytes 852000 | tf_op jit(solution)/shard_map/all_to_all | solution.py:306
  44.6 3.1 %collective-permute-start.13 = (bf16[128,256]{1,0:T(8,128)(2,1)S(1)}, bf16[128,256]{1,0:T(8,128)(2,1)S(1)}, u32[]{:S(2)}, u32[]{:S(2)}) collective-permute-start(bf16[128,256]{1,0:T(8,128)(2,1)S(1)} %get-tuple-element.75), channel_id=1, source_target_pairs={{0,24},{8,0},{16,8},{24,16},{1,25},{9,1},{17,9},{25,17},{2,26},{10... | collective-permute-start | bytes 196616 | tf_op jit(solution)/shard_map/ppermute | solution.py:322
  48.3 1.0 collective-permute-start.11
  49.6 3.9 %collective-permute-done.12 = bf16[128,256]{1,0:T(8,128)(2,1)S(1)} collective-permute-done((bf16[128,256]{1,0:T(8,128)(2,1)S(1)}, bf16[128,256]{1,0:T(8,128)(2,1)S(1)}, u32[]{:S(2)}, u32[]{:S(2)}) %collective-permute-start.12) | collective-permute-done | bytes 65568 | tf_op jit(solution)/shard_map/ppermute | solution.py:322
  54.2 16.6 %all_to_all.45.parts_ref = bf16[8,16,256]{2,1,0:T(8,128)(2,1)S(1)} all-to-all(bf16[8,16,256]{2,1,0:T(8,128)(2,1)S(1)} %bitcast.29), channel_id=1, replica_groups=mesh['z'=8,'y'=4,'x'=4,'core'=2] {'z'}, dimensions={0} | all-to-all | bytes 131072 | tf_op jit(solution)/shard_map/all_to_all | solution.py:323
  71.0 8.0 %all_to_all.46.refs_0_ = f32[8,8,256]{2,1,0:T(8,128)S(1)} all-to-all(f32[8,8,256]{2,1,0:T(8,128)S(1)} %get-tuple-element.55), channel_id=1, replica_groups=mesh['z'=8,'y'=4,'x'=4,'core'=2] {'x','core'}, dimensions={0} | all-to-all | bytes 131072 | tf_op jit(solution)/shard_map/all_to_all | solution.py:348
  79.9 8.0 %all_to_all.47.refs_1_ = f32[8,8,256]{2,1,0:T(8,128)S(1)} all-to-all(f32[8,8,256]{2,1,0:T(8,128)S(1)} %get-tuple-element.59), channel_id=1, replica_groups=mesh['z'=8,'y'=4,'x'=4,'core'=2] {'x','core'}, dimensions={0} | all-to-all | bytes 131072 | tf_op jit(solution)/shard_map/all_to_all | solution.py:348
  88.7 8.0 %all_to_all.48.refs_2_ = f32[8,8,256]{2,1,0:T(8,128)S(1)} all-to-all(f32[8,8,256]{2,1,0:T(8,128)S(1)} %get-tuple-element.63), channel_id=1, replica_groups=mesh['z'=8,'y'=4,'x'=4,'core'=2] {'x','core'}, dimensions={0} | all-to-all | bytes 131072 | tf_op jit(solution)/shard_map/all_to_all | solution.py:348
  96.7 1.6 %turn.1 = (f32[4,256]{1,0:T(4,128)S(1)}, f32[8,8,256]{2,1,0:T(8,128)S(1)}, f32[128,256]{1,0:T(8,128)S(1)}) custom-call(f32[16,256]{1,0:T(8,128)S(1)} %get-tuple-element.53.g_ref, bf16[16,192]{1,0:T(8,128)(2,1)S(1)} %fusion.17.look_ref, bf16[192,16]{1,0:T(8,128)(2,1)S(1)} %fusion.14.scatter_ref, f32[8,8,256]{2,1,0:T(8,128)S(1)} %all_to_all.46.refs_0_, ...), custom_call_target="tpu_custom_call" | custom-call | tf_op jit(solution)/shard_map/turn/pallas_call | solution.py:362
  98.4 8.0 %all_to_all.49.recv_ref = f32[8,8,256]{2,1,0:T(8,128)S(1)} all-to-all(f32[8,8,256]{2,1,0:T(8,128)S(1)} %get-tuple-element.64), channel_id=1, replica_groups=mesh['z'=8,'y'=4,'x'=4,'core'=2] {'x','core'}, dimensions={0} | all-to-all | bytes 131072 | tf_op jit(solution)/shard_map/all_to_all | solution.py:374
  106.3 1.1 backward_2.1
  107.4 8.0 %all_to_all.50.recv_ref = f32[8,8,256]{2,1,0:T(8,128)S(1)} all-to-all(f32[8,8,256]{2,1,0:T(8,128)S(1)} %get-tuple-element.67), channel_id=1, replica_groups=mesh['z'=8,'y'=4,'x'=4,'core'=2] {'x','core'}, dimensions={0} | all-to-all | bytes 131072 | tf_op jit(solution)/shard_map/all_to_all | solution.py:374
  115.4 1.1 backward_1.1
  116.5 8.0 %all_to_all.51.recv_ref = f32[8,8,256]{2,1,0:T(8,128)S(1)} all-to-all(f32[8,8,256]{2,1,0:T(8,128)S(1)} %get-tuple-element.70), channel_id=1, replica_groups=mesh['z'=8,'y'=4,'x'=4,'core'=2] {'x','core'}, dimensions={0} | all-to-all | bytes 131072 | tf_op jit(solution)/shard_map/all_to_all | solution.py:374
  124.8 10.8 %all_to_all.52 = bf16[8,16,256]{2,1,0:T(8,128)(2,1)S(1)} all-to-all(bf16[8,16,256]{2,1,0:T(8,128)(2,1)S(1)} %backward_0.1), channel_id=1, replica_groups=mesh['z'=8,'y'=4,'x'=4,'core'=2] {'z'}, dimensions={0} | all-to-all | bytes 131072 | tf_op jit(solution)/shard_map/all_to_all | solution.py:399
  135.5 2.0 %collective-permute-start.15 = (bf16[8,16,256]{2,1,0:T(8,128)(2,1)S(1)}, bf16[8,16,256]{2,1,0:T(8,128)(2,1)S(1)}, u32[]{:S(2)}, u32[]{:S(2)}) collective-permute-start(bf16[8,16,256]{2,1,0:T(8,128)(2,1)S(1)} %all_to_all.52), channel_id=1, source_target_pairs={{0,16},{8,24},{16,0},{24,8},{1,17},{9,25},{17,1},{25,9},{2,18},{10... | collective-permute-start | bytes 196616 | tf_op jit(solution)/shard_map/ppermute | solution.py:400
  137.5 1.9 %collective-permute-start.14 = (bf16[8,16,256]{2,1,0:T(8,128)(2,1)S(1)}, bf16[8,16,256]{2,1,0:T(8,128)(2,1)S(1)}, u32[]{:S(2)}, u32[]{:S(2)}) collective-permute-start(bf16[8,16,256]{2,1,0:T(8,128)(2,1)S(1)} %all_to_all.52), channel_id=1, source_target_pairs={{0,24},{8,0},{16,8},{24,16},{1,25},{9,1},{17,9},{25,17},{2,26},{10... | collective-permute-start | bytes 196616 | tf_op jit(solution)/shard_map/ppermute | solution.py:400
  139.6 2.1 %collective-permute-done.16 = bf16[8,16,256]{2,1,0:T(8,128)(2,1)S(1)} collective-permute-done((bf16[8,16,256]{2,1,0:T(8,128)(2,1)S(1)}, bf16[8,16,256]{2,1,0:T(8,128)(2,1)S(1)}, u32[]{:S(2)}, u32[]{:S(2)}) %collective-permute-start.16) | collective-permute-done | bytes 65568 | tf_op jit(solution)/shard_map/ppermute | solution.py:400
  142.6 1.2 convolution_add_fusion
  (63 shorter events, 11.0 us)
Async XLA Ops:
  1.7 13.1 %collective-permute-start.2 = (bf16[16,32,256]{2,1,0:T(8,128)(2,1)S(1)}, bf16[16,32,256]{2,1,0:T(8,128)(2,1)}, u32[]{:S(2)}, u32[]{:S(2)}) collective-permute-start(bf16[16,32,256]{2,1,0:T(8,128)(2,1)S(1)} %bitcast.23), channel_id=1, source_target_pairs={{0,6},{1,3},{2,0},{3,5},{4,2},{5,7},{6,4},{7,1},{8,14},{9,11},{10,... | collective-permute-start | bytes 786440 | tf_op jit(solution)/shard_map/ppermute | solution.py:242
  4.1 5.0 %collective-permute-start = (bf16[8,32,256]{2,1,0:T(8,128)(2,1)S(1)}, bf16[8,32,256]{2,1,0:T(8,128)(2,1)S(1)}, u32[]{:S(2)}, u32[]{:S(2)}) collective-permute-start(bf16[8,32,256]{2,1,0:T(8,128)(2,1)S(1)} %bitcast.31), channel_id=1, source_target_pairs={{0,2},{1,7},{2,4},{3,1},{4,6},{5,3},{6,0},{7,5},{8,10},{9,15},{10,... | collective-permute-start | bytes 393224 | tf_op jit(solution)/shard_map/ppermute | solution.py:242
  4.2 6.5 %collective-permute-start.1 = (bf16[8,32,256]{2,1,0:T(8,128)(2,1)S(1)}, bf16[8,32,256]{2,1,0:T(8,128)(2,1)}, u32[]{:S(2)}, u32[]{:S(2)}) collective-permute-start(bf16[8,32,256]{2,1,0:T(8,128)(2,1)S(1)} %bitcast.30), channel_id=1, source_target_pairs={{0,2},{1,7},{2,4},{3,1},{4,6},{5,3},{6,0},{7,5},{8,10},{9,15},{10,... | collective-permute-start | bytes 393224 | tf_op jit(solution)/shard_map/ppermute | solution.py:242
  5.4 10.6 %collective-permute-start.3 = (bf16[16,32,256]{2,1,0:T(8,128)(2,1)S(1)}, bf16[16,32,256]{2,1,0:T(8,128)(2,1)}, u32[]{:S(2)}, u32[]{:S(2)}) collective-permute-start(bf16[16,32,256]{2,1,0:T(8,128)(2,1)S(1)} %bitcast.24), channel_id=1, source_target_pairs={{0,1},{1,0},{2,3},{3,2},{4,5},{5,4},{6,7},{7,6},{8,9},{9,8},{10,11... | collective-permute-start | bytes 786440 | tf_op jit(solution)/shard_map/ppermute | solution.py:247
  10.6 5.6 %collective-permute-start.4 = (bf16[8,32,256]{2,1,0:T(8,128)(2,1)S(1)}, bf16[8,32,256]{2,1,0:T(8,128)(2,1)}, u32[]{:S(2)}, u32[]{:S(2)}) collective-permute-start(bf16[8,32,256]{2,1,0:T(8,128)(2,1)S(1)} %collective-permute-done.refs_6_), channel_id=1, source_target_pairs={{0,2},{1,7},{2,4},{3,1},{4,6},{5,3},{6,0},{7,5},{8,10},{9,15},{10,... | collective-permute-start | bytes 393224 | tf_op jit(solution)/shard_map/ppermute | solution.py:242
  11.4 5.9 %collective-permute-start.5 = (bf16[8,32,256]{2,1,0:T(8,128)(2,1)}, bf16[8,32,256]{2,1,0:T(8,128)(2,1)}, u32[]{:S(2)}, u32[]{:S(2)}) collective-permute-start(bf16[8,32,256]{2,1,0:T(8,128)(2,1)} %collective-permute-done.1.refs_7_), channel_id=1, source_target_pairs={{0,2},{1,7},{2,4},{3,1},{4,6},{5,3},{6,0},{7,5},{8,10},{9,15},{10,... | collective-permute-start | bytes 393224 | tf_op jit(solution)/shard_map/ppermute | solution.py:242
  14.8 4.1 %collective-permute-start.8 = (bf16[16,32,256]{2,1,0:T(8,128)(2,1)}, bf16[16,32,256]{2,1,0:T(8,128)(2,1)S(1)}, u32[]{:S(2)}, u32[]{:S(2)}) collective-permute-start(bf16[16,32,256]{2,1,0:T(8,128)(2,1)} %collective-permute-done.2.refs_9_), channel_id=1, source_target_pairs={{0,1},{1,0},{2,3},{3,2},{4,5},{5,4},{6,7},{7,6},{8,9},{9,8},{10,11... | collective-permute-start | bytes 786440 | tf_op jit(solution)/shard_map/ppermute | solution.py:266
  15.7 1.7 %collective-permute-start.9 = (bf16[8,32,256]{2,1,0:T(8,128)(2,1)S(1)}, bf16[8,32,256]{2,1,0:T(8,128)(2,1)S(1)}, u32[]{:S(2)}, u32[]{:S(2)}) collective-permute-start(bf16[8,32,256]{2,1,0:T(8,128)(2,1)S(1)} %collective-permute-done.refs_6_), channel_id=1, source_target_pairs={{0,1},{1,0},{2,3},{3,2},{4,5},{5,4},{6,7},{7,6},{8,9},{9,8},{10,11... | collective-permute-start | bytes 393224 | tf_op jit(solution)/shard_map/ppermute | solution.py:266
  16.0 1.6 %collective-permute-start.10 = (bf16[8,32,256]{2,1,0:T(8,128)(2,1)}, bf16[8,32,256]{2,1,0:T(8,128)(2,1)S(1)}, u32[]{:S(2)}, u32[]{:S(2)}) collective-permute-start(bf16[8,32,256]{2,1,0:T(8,128)(2,1)} %collective-permute-done.1.refs_7_), channel_id=1, source_target_pairs={{0,1},{1,0},{2,3},{3,2},{4,5},{5,4},{6,7},{7,6},{8,9},{9,8},{10,11... | collective-permute-start | bytes 393224 | tf_op jit(solution)/shard_map/ppermute | solution.py:266
  16.2 1.6 %collective-permute-start.6 = (bf16[8,32,256]{2,1,0:T(8,128)(2,1)}, bf16[8,32,256]{2,1,0:T(8,128)(2,1)S(1)}, u32[]{:S(2)}, u32[]{:S(2)}) collective-permute-start(bf16[8,32,256]{2,1,0:T(8,128)(2,1)} %collective-permute-done.4.refs_2_), channel_id=1, source_target_pairs={{0,1},{1,0},{2,3},{3,2},{4,5},{5,4},{6,7},{7,6},{8,9},{9,8},{10,11... | collective-permute-start | bytes 393224 | tf_op jit(solution)/shard_map/ppermute | solution.py:266
  17.3 1.6 %collective-permute-start.7 = (bf16[8,32,256]{2,1,0:T(8,128)(2,1)}, bf16[8,32,256]{2,1,0:T(8,128)(2,1)S(1)}, u32[]{:S(2)}, u32[]{:S(2)}) collective-permute-start(bf16[8,32,256]{2,1,0:T(8,128)(2,1)} %collective-permute-done.5.refs_3_), channel_id=1, source_target_pairs={{0,1},{1,0},{2,3},{3,2},{4,5},{5,4},{6,7},{7,6},{8,9},{9,8},{10,11... | collective-permute-start | bytes 393224 | tf_op jit(solution)/shard_map/ppermute | solution.py:266
  24.1 19.1 %all-to-all-start = ((bf16[104,16,256]{2,1,0:T(8,128)(2,1)}), bf16[104,16,256]{2,1,0:T(8,128)(2,1)S(1)}, u32[]{:S(2)}, u32[]{:S(2)}) async-start(bf16[104,16,256]{2,1,0:T(8,128)(2,1)} %get-tuple-element.46), calls=%async_computation | async-start | bytes 1703936 | tf_op jit(solution)/shard_map/all_to_all | solution.py:306
  31.9 11.8 %copy-start.4 = (s32[512]{0:T(512)S(1)}, s32[512]{0:T(512)}, u32[]{:S(2)}) copy-start(s32[512]{0:T(512)} %get-tuple-element.82) | copy-start | bytes 6148
  31.9 11.8 %copy-start.5 = (s32[512]{0:T(512)S(1)}, s32[512]{0:T(512)}, u32[]{:S(2)}) copy-start(s32[512]{0:T(512)} %get-tuple-element.83) | copy-start | bytes 6148
  34.3 2.1 %copy-start = (bf16[3,4,3,256,256]{4,3,2,1,0:T(8,128)(2,1)}, bf16[3,4,3,256,256]{4,3,2,1,0:T(8,128)(2,1)S(1)}, u32[]{:S(2)}) copy-start(bf16[3,4,3,256,256]{4,3,2,1,0:T(8,128)(2,1)S(1)} %bring_near.3.refs_1_.refs_2_.refs_3_.c_ref) | copy-start | bytes 14155780
  36.4 34.4 %copy-start.2 = (bf16[4,4,256,256]{3,2,1,0:T(8,128)(2,1)S(1)}, bf16[4,4,256,256]{3,2,1,0:T(8,128)(2,1)}, u32[]{:S(2)}) copy-start(bf16[4,4,256,256]{3,2,1,0:T(8,128)(2,1)} %d_ref.7) | copy-start | bytes 6291460
  43.7 35.3 %copy-start.1 = (bf16[3,4,3,256,256]{4,3,2,1,0:T(8,128)(2,1)S(1)}, bf16[3,4,3,256,256]{4,3,2,1,0:T(8,128)(2,1)}, u32[]{:S(2)}) copy-start(bf16[3,4,3,256,256]{4,3,2,1,0:T(8,128)(2,1)} %copy-done) | copy-start | bytes 14155780
  44.6 5.0 %collective-permute-start.13 = (bf16[128,256]{1,0:T(8,128)(2,1)S(1)}, bf16[128,256]{1,0:T(8,128)(2,1)S(1)}, u32[]{:S(2)}, u32[]{:S(2)}) collective-permute-start(bf16[128,256]{1,0:T(8,128)(2,1)S(1)} %get-tuple-element.75), channel_id=1, source_target_pairs={{0,24},{8,0},{16,8},{24,16},{1,25},{9,1},{17,9},{25,17},{2,26},{10... | collective-permute-start | bytes 196616 | tf_op jit(solution)/shard_map/ppermute | solution.py:322
  47.7 5.8 %collective-permute-start.12 = (bf16[128,256]{1,0:T(8,128)(2,1)S(1)}, bf16[128,256]{1,0:T(8,128)(2,1)S(1)}, u32[]{:S(2)}, u32[]{:S(2)}) collective-permute-start(bf16[128,256]{1,0:T(8,128)(2,1)S(1)} %get-tuple-element.76), channel_id=1, source_target_pairs={{0,16},{8,24},{16,0},{24,8},{1,17},{9,25},{17,1},{25,9},{2,18},{10... | collective-permute-start | bytes 196616 | tf_op jit(solution)/shard_map/ppermute | solution.py:322
  48.3 5.8 %collective-permute-start.11 = (bf16[128,256]{1,0:T(8,128)(2,1)S(1)}, bf16[128,256]{1,0:T(8,128)(2,1)S(1)}, u32[]{:S(2)}, u32[]{:S(2)}) collective-permute-start(bf16[128,256]{1,0:T(8,128)(2,1)S(1)} %get-tuple-element.74), channel_id=1, source_target_pairs={{0,8},{8,16},{16,24},{24,0},{1,9},{9,17},{17,25},{25,1},{2,10},{10... | collective-permute-start | bytes 196616 | tf_op jit(solution)/shard_map/ppermute | solution.py:322
  115.4 27.1 %copy-start.3 = (f32[4,4,32,256]{3,2,1,0:T(8,128)S(1)}, f32[4,4,32,256]{3,2,1,0:T(8,128)}, u32[]{:S(2)}) copy-start(f32[4,4,32,256]{3,2,1,0:T(8,128)} %param.12) | copy-start | bytes 1572868
  135.5 6.2 %collective-permute-start.16 = (bf16[8,16,256]{2,1,0:T(8,128)(2,1)S(1)}, bf16[8,16,256]{2,1,0:T(8,128)(2,1)S(1)}, u32[]{:S(2)}, u32[]{:S(2)}) collective-permute-start(bf16[8,16,256]{2,1,0:T(8,128)(2,1)S(1)} %all_to_all.52), channel_id=1, source_target_pairs={{0,8},{8,16},{16,24},{24,0},{1,9},{9,17},{17,25},{25,1},{2,10},{10... | collective-permute-start | bytes 196616 | tf_op jit(solution)/shard_map/ppermute | solution.py:400
  135.5 6.2 %collective-permute-start.15 = (bf16[8,16,256]{2,1,0:T(8,128)(2,1)S(1)}, bf16[8,16,256]{2,1,0:T(8,128)(2,1)S(1)}, u32[]{:S(2)}, u32[]{:S(2)}) collective-permute-start(bf16[8,16,256]{2,1,0:T(8,128)(2,1)S(1)} %all_to_all.52), channel_id=1, source_target_pairs={{0,16},{8,24},{16,0},{24,8},{1,17},{9,25},{17,1},{25,9},{2,18},{10... | collective-permute-start | bytes 196616 | tf_op jit(solution)/shard_map/ppermute | solution.py:400
  137.5 5.0 %collective-permute-start.14 = (bf16[8,16,256]{2,1,0:T(8,128)(2,1)S(1)}, bf16[8,16,256]{2,1,0:T(8,128)(2,1)S(1)}, u32[]{:S(2)}, u32[]{:S(2)}) collective-permute-start(bf16[8,16,256]{2,1,0:T(8,128)(2,1)S(1)} %all_to_all.52), channel_id=1, source_target_pairs={{0,24},{8,0},{16,8},{24,16},{1,25},{9,1},{17,9},{25,17},{2,26},{10... | collective-permute-start | bytes 196616 | tf_op jit(solution)/shard_map/ppermute | solution.py:400

commit v3 on v2

--- a/solution.py
+++ b/solution.py
@@ -38,30 +38,30 @@
         level, owner, inner = c // (sn * OWNERS), (c // sn) % OWNERS, c % sn
         rank = count_ref[owner]
         count_ref[owner] = rank + 1
-        plan_ref[0, t] = ring_away(owner, here_ref[0])
+        away = ring_away(owner, here_ref[0])
+        plan_ref[0, t] = away
         plan_ref[1, t] = level * sn + inner
         plan_ref[2, t] = row_ref[t]
-        plan_ref[3, t] = owner
+        plan_ref[3, t] = away
         plan_ref[4, t] = rank
         mark = (level * sn + inner + 1).astype(F32)
-        note[owner, pl.ds(rank, 1), :] = jnp.full((1, note.shape[2]), mark, F32)
+        note[away, pl.ds(rank, 1), :] = jnp.full((1, note.shape[2]), mark, F32)
     note_ref[...] = note[...].astype(BF16)
 
 
 def tile_kernel(n_blocks, core_ref, plan_ref, note_ref, side_ref, a_ref, *refs):
     blocks = refs[:n_blocks]
     core = core_ref[0]
-    res_ref, send_ref, x_all, low_ref, sems, note_sems = refs[n_blocks:]
+    res_ref, out_refs = refs[n_blocks], refs[n_blocks + 1 : n_blocks + 1 + OWNERS]
+    send_ref, x_all, low_ref, sems, note_sems = refs[n_blocks + 1 + OWNERS :]
     tiles = a_ref.shape[0]
     mine = x_all.shape[0] // OWNERS
     half = x_all.shape[1] // 2
     per = send_ref.shape[0] // OWNERS
     copies = [pltpu.make_async_copy(side_ref, res_ref, sems.at[len(blocks)])]
-    own, rest = (2 * X - 2 - 4 * core) * mine, (2 + 4 * core) * mine
-    spots = [0, mine, 4 * mine, 9 * mine // 2, 5 * mine, 11 * mine // 2]
-    spots += [own, own + mine // 2, own + mine, rest, rest + mine, rest + 3 * mine // 2]
+    places = [0, 1, 4, 5] + [2 * X - 2 - 4 * core + i for i in range(2)] + [2 + 4 * core + i for i in range(2)]
     for i, block in enumerate(blocks):
-        target = x_all.at[pl.ds(spots[i], block.shape[0])]
+        target = x_all.at[pl.ds(places[i] * mine, mine)]
         copies.append(pltpu.make_async_copy(block, target, sems.at[i]))
     for copy in copies:
         copy.start()
@@ -80,6 +80,8 @@
         term = dot(low_ref[plan_ref[2, t]], a_ref[t], NN).astype(BF16)
         send_ref[spot] = term[:half]
         send_ref[spot + 1] = term[half:]
+    for o, ref in enumerate(out_refs):
+        ref[...] = send_ref[o * per : (o + 1) * per]
 
 
 def in_hbm(x):
@@ -110,7 +112,7 @@
     parts = tuple(4 if x.shape[0] % 4 == 0 else x.shape[0] for x in operands)
     operands = [in_hbm(x) for x in operands]
     if after is not None:
-        operands.append(in_hbm(after))
+        operands.append(after)
     out_shape = [jax.ShapeDtypeStruct(x.shape, x.dtype) for x in operands]
     return pl.pallas_call(
         functools.partial(near_kernel, n, parts),
@@ -123,9 +125,40 @@
     )(*operands)
 
 
+def pick_kernel(mine, y_ref, *refs):
+    own_hbm, recvs, outs, (own, data, pick, sem) = refs[0], refs[1:OWNERS], refs[OWNERS:-4], refs[-4:]
+    copy = pltpu.make_async_copy(own_hbm, own, sem)
+    copy.start()
+    blocks, size, T = own.shape
+    rows = (blocks - 1) * size
+    K = rows // CAP
+    lane = lax.broadcasted_iota(jnp.int32, (1, 128), 1)
+    marks, codes = [], []
+    for i, ref in enumerate((*recvs, own)):
+        if i == len(recvs):
+            copy.wait()
+        data[i * rows : (i + 1) * rows, :] = ref[: blocks - 1].reshape(rows, T)
+        note = ref[blocks - 1].astype(F32)
+        marks += [note[j : j + 1, :128] for j in range(CAP)]
+    per = 128 // K
+    column = (lane % K).astype(F32)
+    for i in range(0, len(marks), per):
+        mark = marks[i]
+        for j in range(1, per):
+            mark = jnp.where(lane // K == j, marks[i + j], mark)
+        codes.append((mark - 1.0) * K + column)
+    code = jnp.concatenate(codes, axis=1)
+    for step, out in enumerate(outs):
+        at = lax.broadcasted_iota(jnp.int32, (Z * mine, 1), 0)
+        k = at // mine * Y + (y_ref[0] + step) % Y
+        wanted = ((at % mine) * K + k).astype(F32)
+        pick[...] = jnp.where(wanted == code, 1.0, 0.0).astype(BF16)
+        out[...] = dot(pick[...], data[...], NN).astype(BF16)
+
+
 def forward_rows(level, sn, g, look_ref, known_refs, c_ref, d_ref):
     if level > 0:
-        known = jnp.concatenate([ref[...].reshape(-1, ref.shape[2]) for ref in known_refs], axis=0).astype(BF16)
+        known = jnp.concatenate([ref[...].astype(F32).reshape(-1, ref.shape[2]) for ref in known_refs], axis=0).astype(BF16)
         found = dot(look_ref[...], known, NN)
     rows = []
     for j in range(sn):
@@ -160,17 +193,18 @@
 def store_pend(pend, out_ref, rest_refs):
     n, rows, width = out_ref.shape
     base = pend.shape[0] - n * rows
-    out_ref[...] = pend[base:, :].reshape(n, rows, width)
+    out_ref[...] = pend[base:, :].reshape(n, rows, width).astype(out_ref.dtype)
     for ref in rest_refs:
         ref[...] = pend[:base, :]
 
 
 def spread_rows(rows, own_ref, out_ref):
-    out_ref[...] = jnp.zeros_like(out_ref)
     for j, row in enumerate(rows):
         own_ref[j : j + 1, :] = row
-        for o in range(out_ref.shape[0]):
-            out_ref[o, j : j + 1, :] = row
+    filler = jnp.zeros((out_ref.shape[1] - len(rows), out_ref.shape[2]), F32)
+    block = jnp.concatenate(rows + [filler], axis=0).astype(out_ref.dtype)
+    for o in range(out_ref.shape[0]):
+        out_ref[o] = block
 
 
 def first_kernel(sn, parts_ref, d_ref, g_ref, own_ref, out_ref):
@@ -197,9 +231,9 @@
 
 
 def remaining_rows(sn, solved_ref, recv_ref):
-    got = recv_ref[0]
+    got = recv_ref[0].astype(F32)
     for i in range(1, recv_ref.shape[0]):
-        got = got + recv_ref[i]
+        got = got + recv_ref[i].astype(F32)
     return [solved_ref[j : j + 1, :] - got[j : j + 1, :] for j in range(sn)]
 
 
@@ -234,17 +268,17 @@
     e = estimate.astype(BF16).reshape(mine, K, T)
     other = functools.partial(lax.ppermute, axis_name="core", perm=shift(CORE, 1))
 
-    def along(block, way=1):
+    def along(block):
         perm = []
         for x in range(X):
-            perm.append((x * CORE, (x + way) % X * CORE))
-            perm.append((x * CORE + 1, (x - way) % X * CORE + 1))
+            perm.append((x * CORE, (x + 1) % X * CORE))
+            perm.append((x * CORE + 1, (x - 1) % X * CORE + 1))
         return lax.ppermute(block, snode, perm)
 
-    half = mine // 2
-    first = [along(e[:half]), along(e[half:])]
-    second = along(e, -1)
+    first = along(e)
     swapped = other(e)
+    swapped, here = lax.optimization_barrier((swapped, here))
+    second = along(swapped)
     plan, note = pl.pallas_call(
         functools.partial(plan_kernel, sn),
         out_shape=(
@@ -257,24 +291,25 @@
         compiler_params=PARAMS,
         name="plan",
     )(here, in_hbm(tile_col), in_hbm(tile_row))
-    first_lo, first_hi, note = lax.optimization_barrier((*first, note))
-    first = [first_lo, first_hi]
-    far = [along(x) for x in first]
+    third = along(first)
+    cross_first = other(first)
     (a_near,) = bring_near(None, a_tiles)
-    second, a_near = lax.optimization_barrier((second, a_near))
     side = in_hbm(right_side)
-    blocks = [e, swapped] + far + [other(x) for x in far] + first + [other(second), second] + [other(x) for x in first]
+    second, note, a_near = lax.optimization_barrier((second, note, a_near))
+    cross_second, cross_third = other(second), other(third)
+    blocks = [e, swapped, third, cross_third, first, second, cross_second, cross_first]
 
     slot_rows = CAP * K + 16
-    residual, send = pl.pallas_call(
+    residual, *send = pl.pallas_call(
         functools.partial(tile_kernel, len(blocks)),
         out_shape=(
             jax.ShapeDtypeStruct((row_tiles, K, T), F32),
-            pltpu.HBM((OWNERS * slot_rows // 16, 16, T), BF16),
-        ),
+        )
+        + (pltpu.HBM((slot_rows // 16, 16, T), BF16),) * OWNERS,
         in_specs=[SMEM, SMEM, ANY, ANY, VMEM] + [ANY] * len(blocks),
-        out_specs=(VMEM, VMEM),
+        out_specs=(VMEM,) * (1 + OWNERS),
         scratch_shapes=[
+            pltpu.VMEM((OWNERS * slot_rows // 16, 16, T), BF16),
             pltpu.VMEM((OWNERS * mine, K, T), BF16),
             pltpu.VMEM((row_tiles, K, T), BF16),
             pltpu.SemaphoreType.DMA((len(blocks) + 1,)),
@@ -289,7 +324,7 @@
     place = jnp.arange(Y * Z * mine)
     column_k = (place // mine) % Z * Y + (place // (mine * Z) + y) % Y
     place = (place % mine) * K + column_k
-    send, coupling_source = lax.optimization_barrier((send, coupling_source))
+    first_send, coupling_source = lax.optimization_barrier((send[0], coupling_source))
     source = coupling_source.reshape(levels - 1, -1)
     block_rows = 8
     spot_at = source // sn * block_rows + source % sn
@@ -303,23 +338,35 @@
         scatter.append((spots[:, None] == spot_at[level - 1][None, :]).astype(BF16))
     stage = pltpu.VMEM((n_terms + pad_terms, T), F32)
 
-    recv = lax.all_to_all(send, snode, 0, 0, tiled=True)
-    (c_near,) = bring_near(residual, coupling)
-    recv, c_near, look, scatter, to, place = lax.optimization_barrier((recv, c_near, look, scatter, to, place))
-    recv = recv.reshape(OWNERS, slot_rows, T)
-
-    spot = recv[:, CAP * K : CAP * K + CAP, 0].astype(jnp.int32) - 1
-    spot = jnp.pad(jnp.repeat(spot, K, axis=1), ((0, 0), (0, 16)), constant_values=-1).reshape(-1)
-    pick_row = jnp.arange(K * mine)
-    pick_col = jnp.arange(OWNERS * slot_rows) % slot_rows
-    y = lax.axis_index("y")
-    row_k = (pick_row // mine) % Z * Y + (pick_row // (mine * Z) + y) % Y
-    pick = (row_k[:, None] == pick_col[None, :] % K) & (pick_row[:, None] % mine == spot[None, :])
-    part = jnp.dot(pick.astype(BF16), recv.reshape(OWNERS * slot_rows, T), preferred_element_type=F32)
-    part = part.astype(BF16).reshape(Y, Z * mine, T)
+    recv = [first_send]
+    for away in (3, 2, 1, 4, 5, 6, 7):
+        step, swap = away // CORE, away % CORE
+        perm = []
+        for x in range(X):
+            for c in range(CORE):
+                perm.append((x * CORE + c, (x + step) % X * CORE + (c + swap) % CORE))
+        recv.append(lax.ppermute(send[away], snode, perm))
+    recv, look, scatter, to, place = lax.optimization_barrier((recv, look, scatter, to, place))
+    part = pl.pallas_call(
+        functools.partial(pick_kernel, mine),
+        out_shape=(jax.ShapeDtypeStruct((Z * mine, T), BF16),) * Y,
+        in_specs=[SMEM, ANY] + [VMEM] * (OWNERS - 1),
+        out_specs=(VMEM,) * Y,
+        scratch_shapes=[
+            pltpu.VMEM((slot_rows // 16, 16, T), BF16),
+            pltpu.VMEM((OWNERS * CAP * K, T), BF16),
+            pltpu.VMEM((Z * mine, OWNERS * CAP * K), BF16),
+            pltpu.SemaphoreType.DMA(()),
+        ],
+        compiler_params=PARAMS,
+        name="pick",
+    )(y.reshape(1), in_hbm(recv[0]), *recv[1:])
     total = part[0].astype(F32)
-    for s in range(1, Y):
-        total = total + lax.ppermute(part[s], "y", shift(Y, s)).astype(F32)
+    arrived = [lax.ppermute(part[s], "y", shift(Y, s)) for s in (2, 1, 3)]
+    (c_near,) = bring_near(part[0], coupling)
+    arrived, c_near = lax.optimization_barrier((arrived, c_near))
+    for block in arrived:
+        total = total + block.astype(F32)
     parts = lax.all_to_all(total.astype(BF16).reshape(Z, mine, T), "z", 0, 0, tiled=True)
 
     def d_spec(level):
@@ -329,7 +376,7 @@
         return pl.BlockSpec((1, sn, coupling.shape[2], T, T), lambda i: (level - 1, 0, 0, 0, 0))
 
     row4 = jax.ShapeDtypeStruct((sn, T), F32)
-    by_owner = jax.ShapeDtypeStruct((OWNERS, block_rows, T), F32)
+    by_owner = jax.ShapeDtypeStruct((OWNERS, block_rows, T), BF16)
 
     def rest_of(level):
         return (jax.ShapeDtypeStruct(((level - 1) * OWNERS * block_rows, T), F32),) if level > 1 else ()
@@ -397,7 +444,8 @@
                 name="backward_0",
             )(solved[0], arrived, *changes, diag_inverse)
     column = lax.all_to_all(change, "z", 0, 0, tiled=True)
-    pieces = [column] + [lax.ppermute(column, "y", shift(Y, -s % Y)) for s in range(1, Y)]
+    far, ahead, behind = [lax.ppermute(column, "y", shift(Y, -s % Y)) for s in (2, 1, 3)]
+    pieces = [column, ahead, far, behind]
     pieces = jnp.concatenate(pieces, axis=0).reshape(Y * Z * mine, T)
     sort = (to[:, None] == place[None, :]).astype(BF16)
     change = jnp.dot(sort, pieces, preferred_element_type=F32)

time: 145 us -> 139 us (0.959)
  local copies, waits for them, and re-layouts: 3.45 us -> 0.19 us
    ppermute x8 -> x13, starting transfers between devices: 5.8 us -> 14 us  [the longest x7 8.43 us: local(): recv.append(lax.ppermute(send[away], snode, perm))]
    all_to_all x1 -> x0, waiting for transfers between devices: 6.81 us -> none  [local(): recv = lax.all_to_all(send, snode, 0, 0, tiled=True)]
    all_to_all x1 -> x0, starting transfers between devices: 6.71 us -> none  [local(): recv = lax.all_to_all(send, snode, 0, 0, tiled=True)]
    unnamed x13 -> x6, local copies, waits for them, and re-layouts: 2.3 us -> 0.02 us
    ppermute x3, waiting for transfers between devices: 2.99 us -> 5.24 us  [local(): lax.ppermute(column, 'y', shift(Y, -s % Y))]
    ppermute x8 -> x13, waiting for transfers between devices: 6.39 us -> 8.15 us  [the longest x7 6.3 us: local(): recv.append(lax.ppermute(send[away], snode, perm))]
    ppermute x5 -> x3, waiting for transfers between devices: 4.27 us -> 5.92 us  [along(): return lax.ppermute(block, snode, perm)]
    ppermute x5 -> x3, starting transfers between devices: 5.91 us -> 4.3 us  [along(): return lax.ppermute(block, snode, perm)]
  transfers between devices with their start and end apart: 18 -> 20, of which waited for: 12 -> 11; matrix products, arithmetic and copies ran while one was open for 1% -> 0% of each run, Pallas kernels for 4% -> 5%
where the time goes in v3:
time: 139 us
  blocking collectives  75.2 us (54%)
  starting transfers between devices  22.2 us (16%)
  waiting for transfers between devices  19.4 us (14%)
  Pallas kernels  18.5 us (13%)
  other arithmetic  1.44 us (1%)
    all_to_all x3, blocking collectives, local(): known.append(lax.all_to_all(out, snode, 0, 0, tiled=True))  24.2 us
    all_to_all x3, blocking collectives, local(): arrived = lax.all_to_all(out, snode, 0, 0, tiled=True)  23.6 us
    all_to_all x1, blocking collectives, local(): lax.all_to_all(total.astype(BF16).reshape(Z, mine, T), 'z', 0, 0, tiled=T...  16.6 us
    all_to_all x1, blocking collectives, local(): column = lax.all_to_all(change, 'z', 0, 0, tiled=True)  10.8 us
    ppermute x7, starting transfers between devices, local(): recv.append(lax.ppermute(send[away], snode, perm))  8.43 us
    ppermute x7, waiting for transfers between devices, local(): recv.append(lax.ppermute(send[away], snode, perm))  6.3 us
    ppermute x3, waiting for transfers between devices, along(): return lax.ppermute(block, snode, perm)  5.92 us
    ppermute x3, waiting for transfers between devices, local(): lax.ppermute(column, 'y', shift(Y, -s % Y))  5.24 us
  transfers between devices with their start and end apart: 20, of which 11 were waited for; matrix products, arithmetic and copies ran while one was open for 0% of the time, Pallas kernels for 5%

profile of v3, /device:TPU:2, one launch (start us, length us, event | category | flops | bytes accessed | tf_op | source)
XLA Modules:
  0.0 138.9 jit_solution(4332227805825668137)
XLA Ops:
  1.8 1.6 %collective-permute-start.2 = (bf16[16,32,256]{2,1,0:T(8,128)(2,1)S(1)}, bf16[16,32,256]{2,1,0:T(8,128)(2,1)}, u32[]{:S(2)}, u32[]{:S(2)}) collective-permute-start(bf16[16,32,256]{2,1,0:T(8,128)(2,1)S(1)} %bitcast.18), channel_id=1, source_target_pairs={{0,2},{1,7},{2,4},{3,1},{4,6},{5,3},{6,0},{7,5},{8,10},{9,15},{10,... | collective-permute-start | bytes 786440 | tf_op jit(solution)/shard_map/ppermute | solution.py:276
  3.5 1.5 %collective-permute-start.1 = (bf16[16,32,256]{2,1,0:T(8,128)(2,1)}, bf16[16,32,256]{2,1,0:T(8,128)(2,1)}, u32[]{:S(2)}, u32[]{:S(2)}) collective-permute-start(bf16[16,32,256]{2,1,0:T(8,128)(2,1)} %collective-permute-done.refs_1_), channel_id=1, source_target_pairs={{0,2},{1,7},{2,4},{3,1},{4,6},{5,3},{6,0},{7,5},{8,10},{9,15},{10,... | collective-permute-start | bytes 786440 | tf_op jit(solution)/shard_map/ppermute | solution.py:276
  5.0 3.7 %collective-permute-done.2.refs_4_ = bf16[16,32,256]{2,1,0:T(8,128)(2,1)} collective-permute-done((bf16[16,32,256]{2,1,0:T(8,128)(2,1)S(1)}, bf16[16,32,256]{2,1,0:T(8,128)(2,1)}, u32[]{:S(2)}, u32[]{:S(2)}) %collective-permute-start.2) | collective-permute-done | bytes 262176 | tf_op jit(solution)/shard_map/ppermute | solution.py:276
  8.6 1.2 collective-permute-start.3
  9.9 1.9 %bring_near.2.a_ref = bf16[24,256,256]{2,1,0:T(8,128)(2,1)S(1)} custom-call(bf16[24,256,256]{2,1,0:T(8,128)(2,1)} %refs_0_.2), custom_call_target="tpu_custom_call" | custom-call | tf_op jit(solution)/shard_map/bring_near/pallas_call | solution.py:117
  11.8 1.9 %plan.1 = (s32[5,24]{1,0:T(8,128)S(1)}, bf16[8,16,256]{2,1,0:T(8,128)(2,1)}) custom-call(s32[1]{0:T(128)} %bitcast.2.here_ref, s32[24]{0:T(128)} %col_ref.1, s32[24]{0:T(128)} %row_ref.1), custom_call_target="tpu_custom_call" | custom-call | tf_op jit(solution)/shard_map/plan/pallas_call | solution.py:282
  14.3 2.3 %collective-permute-done.3.refs_2_ = bf16[16,32,256]{2,1,0:T(8,128)(2,1)} collective-permute-done((bf16[16,32,256]{2,1,0:T(8,128)(2,1)}, bf16[16,32,256]{2,1,0:T(8,128)(2,1)}, u32[]{:S(2)}, u32[]{:S(2)}) %collective-permute-start.3) | collective-permute-done | bytes 262176 | tf_op jit(solution)/shard_map/ppermute | solution.py:276
  16.5 1.8 %collective-permute-done.4.refs_3_ = bf16[16,32,256]{2,1,0:T(8,128)(2,1)} collective-permute-done((bf16[16,32,256]{2,1,0:T(8,128)(2,1)}, bf16[16,32,256]{2,1,0:T(8,128)(2,1)}, u32[]{:S(2)}, u32[]{:S(2)}) %collective-permute-start.4) | collective-permute-done | bytes 262176 | tf_op jit(solution)/shard_map/ppermute | solution.py:299
  18.4 4.9 %tile_products.1 = (f32[8,32,256]{2,1,0:T(8,128)}, bf16[13,16,256]{2,1,0:T(8,128)(2,1)}, bf16[13,16,256]{2,1,0:T(8,128)(2,1)}, bf16[13,16,256]{2,1,0:T(8,128)(2,...) custom-call(s32[1]{0:T(128)} %bitcast.core_ref, ...), custom_call_target="tpu_custom_call" | custom-call | tf_op jit(solution)/shard_map/tile_products/pallas_call | solution.py:303
  23.5 2.1 %collective-permute-start.10 = (bf16[13,16,256]{2,1,0:T(8,128)(2,1)}, bf16[13,16,256]{2,1,0:T(8,128)(2,1)S(1)}, u32[]{:S(2)}, u32[]{:S(2)}) collective-permute-start(bf16[13,16,256]{2,1,0:T(8,128)(2,1)} %get-tuple-element.71), channel_id=1, source_target_pairs={{0,4},{1,5},{2,6},{3,7},{4,0},{5,1},{6,2},{7,3},{8,12},{9,13},{10,... | collective-permute-start | bytes 319496 | tf_op jit(solution)/shard_map/ppermute | solution.py:348
  26.7 3.2 %collective-permute-start.12 = (bf16[13,16,256]{2,1,0:T(8,128)(2,1)}, bf16[13,16,256]{2,1,0:T(8,128)(2,1)S(1)}, u32[]{:S(2)}, u32[]{:S(2)}) collective-permute-start(bf16[13,16,256]{2,1,0:T(8,128)(2,1)} %get-tuple-element.73), channel_id=1, source_target_pairs={{0,6},{1,7},{2,0},{3,1},{4,2},{5,3},{6,4},{7,5},{8,14},{9,15},{10,... | collective-permute-start | bytes 319496 | tf_op jit(solution)/shard_map/ppermute | solution.py:348
  30.3 1.4 %collective-permute-start.7 = (bf16[13,16,256]{2,1,0:T(8,128)(2,1)}, bf16[13,16,256]{2,1,0:T(8,128)(2,1)S(1)}, u32[]{:S(2)}, u32[]{:S(2)}) collective-permute-start(bf16[13,16,256]{2,1,0:T(8,128)(2,1)} %get-tuple-element.68), channel_id=1, source_target_pairs={{0,3},{1,2},{2,5},{3,4},{4,7},{5,6},{6,1},{7,0},{8,11},{9,10},{10,... | collective-permute-start | bytes 319496 | tf_op jit(solution)/shard_map/ppermute | solution.py:348
  32.8 2.1 %collective-permute-done.12.refs_6_ = bf16[13,16,256]{2,1,0:T(8,128)(2,1)S(1)} collective-permute-done((bf16[13,16,256]{2,1,0:T(8,128)(2,1)}, bf16[13,16,256]{2,1,0:T(8,128)(2,1)S(1)}, u32[]{:S(2)}, u32[]{:S(2)}) %collective-permute-start.12) | collective-permute-done | bytes 106528 | tf_op jit(solution)/shard_map/ppermute | solution.py:348
  34.9 2.2 %collective-permute-done.13.refs_7_ = bf16[13,16,256]{2,1,0:T(8,128)(2,1)S(1)} collective-permute-done((bf16[13,16,256]{2,1,0:T(8,128)(2,1)}, bf16[13,16,256]{2,1,0:T(8,128)(2,1)S(1)}, u32[]{:S(2)}, u32[]{:S(2)}) %collective-permute-start.13) | collective-permute-done | bytes 106528 | tf_op jit(solution)/shard_map/ppermute | solution.py:348
  37.1 1.2 collective-permute-done.8.refs_2_
  38.4 1.5 %pick.1 = (bf16[128,256]{1,0:T(8,128)(2,1)S(1)}, bf16[128,256]{1,0:T(8,128)(2,1)S(1)}, bf16[128,256]{1,0:T(8,128)(2,1)S(1)}, bf16[128,256]{1,0:T(8,128)(2,1)S(1)}) custom-call(s32[1]{0:T(128)} %bitcast.6.y_ref, bf16[13,16,256]{2,1,0:T(8,128)(2,1)} %get-tuple-element.78.refs_0_, bf16[13,16,256]{2,1,0:T(8,128)(2,1)S(1)} %collective-permute-done.7.refs_1_, ...), custom_call_target="tpu_custom_call" | custom-call | tf_op jit(solution)/shard_map/pick/pallas_call | solution.py:350
  39.9 1.7 %collective-permute-start.14 = (bf16[128,256]{1,0:T(8,128)(2,1)S(1)}, bf16[128,256]{1,0:T(8,128)(2,1)S(1)}, u32[]{:S(2)}, u32[]{:S(2)}) collective-permute-start(bf16[128,256]{1,0:T(8,128)(2,1)S(1)} %get-tuple-element.87), channel_id=1, source_target_pairs={{0,16},{8,24},{16,0},{24,8},{1,17},{9,25},{17,1},{25,9},{2,18},{10... | collective-permute-start | bytes 196616 | tf_op jit(solution)/shard_map/ppermute | solution.py:365
  42.3 2.6 %collective-permute-start.16 = (bf16[128,256]{1,0:T(8,128)(2,1)S(1)}, bf16[128,256]{1,0:T(8,128)(2,1)S(1)}, u32[]{:S(2)}, u32[]{:S(2)}) collective-permute-start(bf16[128,256]{1,0:T(8,128)(2,1)S(1)} %get-tuple-element.89), channel_id=1, source_target_pairs={{0,24},{8,0},{16,8},{24,16},{1,25},{9,1},{17,9},{25,17},{2,26},{10... | collective-permute-start | bytes 196616 | tf_op jit(solution)/shard_map/ppermute | solution.py:365
  44.9 2.5 %bring_near.3.refs_1_.refs_2_.refs_3_.c_ref = bf16[3,4,3,256,256]{4,3,2,1,0:T(8,128)(2,1)S(1)} custom-call(bf16[3,4,3,256,256]{4,3,2,1,0:T(8,128)(2,1)} %refs_0_.3, bf16[128,256]{1,0:T(8,128)(2,1)S(1)} %get-tuple-element.86.refs_1_), custom_call_target="tpu_custom_call" | custom-call | tf_op jit(solution)/shard_map/bring_near/pallas_call | solution.py:117
  47.5 16.6 %all_to_all.40.parts_ref = bf16[8,16,256]{2,1,0:T(8,128)(2,1)S(1)} all-to-all(bf16[8,16,256]{2,1,0:T(8,128)(2,1)S(1)} %bitcast.21), channel_id=1, replica_groups=mesh['z'=8,'y'=4,'x'=4,'core'=2] {'z'}, dimensions={0} | all-to-all | bytes 131072 | tf_op jit(solution)/shard_map/all_to_all | solution.py:370
  64.3 8.6 %all_to_all.41.refs_0_ = bf16[8,8,256]{2,1,0:T(8,128)(2,1)S(1)} all-to-all(bf16[8,8,256]{2,1,0:T(8,128)(2,1)S(1)} %get-tuple-element.96), channel_id=1, replica_groups=mesh['z'=8,'y'=4,'x'=4,'core'=2] {'x','core'}, dimensions={0} | all-to-all | bytes 65536 | tf_op jit(solution)/shard_map/all_to_all | solution.py:395
  73.7 7.8 %all_to_all.42.refs_1_ = bf16[8,8,256]{2,1,0:T(8,128)(2,1)S(1)} all-to-all(bf16[8,8,256]{2,1,0:T(8,128)(2,1)S(1)} %get-tuple-element.100), channel_id=1, replica_groups=mesh['z'=8,'y'=4,'x'=4,'core'=2] {'x','core'}, dimensions={0} | all-to-all | bytes 65536 | tf_op jit(solution)/shard_map/all_to_all | solution.py:395
  82.4 7.8 %all_to_all.43.refs_2_ = bf16[8,8,256]{2,1,0:T(8,128)(2,1)S(1)} all-to-all(bf16[8,8,256]{2,1,0:T(8,128)(2,1)S(1)} %get-tuple-element.104), channel_id=1, replica_groups=mesh['z'=8,'y'=4,'x'=4,'core'=2] {'x','core'}, dimensions={0} | all-to-all | bytes 65536 | tf_op jit(solution)/shard_map/all_to_all | solution.py:395
  90.2 1.6 %turn.1 = (f32[4,256]{1,0:T(4,128)S(1)}, bf16[8,8,256]{2,1,0:T(8,128)(2,1)S(1)}, f32[128,256]{1,0:T(8,128)S(1)}) custom-call(f32[16,256]{1,0:T(8,128)S(1)} %get-tuple-element.94.g_ref, bf16[16,192]{1,0:T(8,128)(2,1)S(1)} %fusion.6.look_ref, bf16[192,16]{1,0:T(8,128)(2,1)S(1)} %fusion.3.scatter_ref, bf16[8,8,256]{2,1,0:T(8,128)(2,1)S(1)} %all_to_all.41.refs_0_, ...), custom_call_target="tpu_custom_call" | custom-call | tf_op jit(solution)/shard_map/turn/pallas_call | solution.py:409
  91.8 7.8 %all_to_all.44.recv_ref = bf16[8,8,256]{2,1,0:T(8,128)(2,1)S(1)} all-to-all(bf16[8,8,256]{2,1,0:T(8,128)(2,1)S(1)} %get-tuple-element.105), channel_id=1, replica_groups=mesh['z'=8,'y'=4,'x'=4,'core'=2] {'x','core'}, dimensions={0} | all-to-all | bytes 65536 | tf_op jit(solution)/shard_map/all_to_all | solution.py:421
  100.8 7.8 %all_to_all.45.recv_ref = bf16[8,8,256]{2,1,0:T(8,128)(2,1)S(1)} all-to-all(bf16[8,8,256]{2,1,0:T(8,128)(2,1)S(1)} %get-tuple-element.108), channel_id=1, replica_groups=mesh['z'=8,'y'=4,'x'=4,'core'=2] {'x','core'}, dimensions={0} | all-to-all | bytes 65536 | tf_op jit(solution)/shard_map/all_to_all | solution.py:421
  109.7 7.9 %all_to_all.46.recv_ref = bf16[8,8,256]{2,1,0:T(8,128)(2,1)S(1)} all-to-all(bf16[8,8,256]{2,1,0:T(8,128)(2,1)S(1)} %get-tuple-element.111), channel_id=1, replica_groups=mesh['z'=8,'y'=4,'x'=4,'core'=2] {'x','core'}, dimensions={0} | all-to-all | bytes 65536 | tf_op jit(solution)/shard_map/all_to_all | solution.py:421
  117.9 10.8 %all_to_all.47 = bf16[8,16,256]{2,1,0:T(8,128)(2,1)S(1)} all-to-all(bf16[8,16,256]{2,1,0:T(8,128)(2,1)S(1)} %backward_0.1), channel_id=1, replica_groups=mesh['z'=8,'y'=4,'x'=4,'core'=2] {'z'}, dimensions={0} | all-to-all | bytes 131072 | tf_op jit(solution)/shard_map/all_to_all | solution.py:446
  128.6 2.9 %collective-permute-start.17 = (bf16[8,16,256]{2,1,0:T(8,128)(2,1)S(1)}, bf16[8,16,256]{2,1,0:T(8,128)(2,1)S(1)}, u32[]{:S(2)}, u32[]{:S(2)}) collective-permute-start(bf16[8,16,256]{2,1,0:T(8,128)(2,1)S(1)} %all_to_all.47), channel_id=1, source_target_pairs={{0,24},{8,0},{16,8},{24,16},{1,25},{9,1},{17,9},{25,17},{2,26},{10... | collective-permute-start | bytes 196616 | tf_op jit(solution)/shard_map/ppermute | solution.py:447
  132.5 1.6 %collective-permute-done.17 = bf16[8,16,256]{2,1,0:T(8,128)(2,1)S(1)} collective-permute-done((bf16[8,16,256]{2,1,0:T(8,128)(2,1)S(1)}, bf16[8,16,256]{2,1,0:T(8,128)(2,1)S(1)}, u32[]{:S(2)}, u32[]{:S(2)}) %collective-permute-start.17) | collective-permute-done | bytes 65568 | tf_op jit(solution)/shard_map/ppermute | solution.py:447
  134.0 3.4 %collective-permute-done.18 = bf16[8,16,256]{2,1,0:T(8,128)(2,1)S(1)} collective-permute-done((bf16[8,16,256]{2,1,0:T(8,128)(2,1)S(1)}, bf16[8,16,256]{2,1,0:T(8,128)(2,1)S(1)}, u32[]{:S(2)}, u32[]{:S(2)}) %collective-permute-start.18) | collective-permute-done | bytes 65568 | tf_op jit(solution)/shard_map/ppermute | solution.py:447
  137.7 1.2 convolution_add_fusion
  (50 shorter events, 10.9 us)
Async XLA Ops:
  1.7 1.8 %collective-permute-start = (bf16[16,32,256]{2,1,0:T(8,128)(2,1)S(1)}, bf16[16,32,256]{2,1,0:T(8,128)(2,1)}, u32[]{:S(2)}, u32[]{:S(2)}) collective-permute-start(bf16[16,32,256]{2,1,0:T(8,128)(2,1)S(1)} %bitcast.17), channel_id=1, source_target_pairs={{0,1},{1,0},{2,3},{3,2},{4,5},{5,4},{6,7},{7,6},{8,9},{9,8},{10,11... | collective-permute-start | bytes 786440 | tf_op jit(solution)/shard_map/ppermute | solution.py:279
  1.8 6.8 %collective-permute-start.2 = (bf16[16,32,256]{2,1,0:T(8,128)(2,1)S(1)}, bf16[16,32,256]{2,1,0:T(8,128)(2,1)}, u32[]{:S(2)}, u32[]{:S(2)}) collective-permute-start(bf16[16,32,256]{2,1,0:T(8,128)(2,1)S(1)} %bitcast.18), channel_id=1, source_target_pairs={{0,2},{1,7},{2,4},{3,1},{4,6},{5,3},{6,0},{7,5},{8,10},{9,15},{10,... | collective-permute-start | bytes 786440 | tf_op jit(solution)/shard_map/ppermute | solution.py:276
  3.5 10.3 %collective-permute-start.1 = (bf16[16,32,256]{2,1,0:T(8,128)(2,1)}, bf16[16,32,256]{2,1,0:T(8,128)(2,1)}, u32[]{:S(2)}, u32[]{:S(2)}) collective-permute-start(bf16[16,32,256]{2,1,0:T(8,128)(2,1)} %collective-permute-done.refs_1_), channel_id=1, source_target_pairs={{0,2},{1,7},{2,4},{3,1},{4,6},{5,3},{6,0},{7,5},{8,10},{9,15},{10,... | collective-permute-start | bytes 786440 | tf_op jit(solution)/shard_map/ppermute | solution.py:276
  8.6 7.9 %collective-permute-start.3 = (bf16[16,32,256]{2,1,0:T(8,128)(2,1)}, bf16[16,32,256]{2,1,0:T(8,128)(2,1)}, u32[]{:S(2)}, u32[]{:S(2)}) collective-permute-start(bf16[16,32,256]{2,1,0:T(8,128)(2,1)} %collective-permute-done.2.refs_4_), channel_id=1, source_target_pairs={{0,2},{1,7},{2,4},{3,1},{4,6},{5,3},{6,0},{7,5},{8,10},{9,15},{10,... | collective-permute-start | bytes 786440 | tf_op jit(solution)/shard_map/ppermute | solution.py:276
  11.7 11.5 %copy-start.2 = (s32[3,4,3]{2,1,0:T(4,128)S(1)}, s32[3,4,3]{2,1,0:T(4,128)}, u32[]{:S(2)}) copy-start(s32[3,4,3]{2,1,0:T(4,128)} %param.15) | copy-start | bytes 436
  13.7 2.9 %collective-permute-start.6 = (bf16[16,32,256]{2,1,0:T(8,128)(2,1)}, bf16[16,32,256]{2,1,0:T(8,128)(2,1)}, u32[]{:S(2)}, u32[]{:S(2)}) collective-permute-start(bf16[16,32,256]{2,1,0:T(8,128)(2,1)} %collective-permute-done.2.refs_4_), channel_id=1, source_target_pairs={{0,1},{1,0},{2,3},{3,2},{4,5},{5,4},{6,7},{7,6},{8,9},{9,8},{10,11... | collective-permute-start | bytes 786440 | tf_op jit(solution)/shard_map/ppermute | solution.py:295
  13.8 2.7 %collective-permute-start.5 = (bf16[16,32,256]{2,1,0:T(8,128)(2,1)}, bf16[16,32,256]{2,1,0:T(8,128)(2,1)}, u32[]{:S(2)}, u32[]{:S(2)}) collective-permute-start(bf16[16,32,256]{2,1,0:T(8,128)(2,1)} %collective-permute-done.1.refs_5_), channel_id=1, source_target_pairs={{0,1},{1,0},{2,3},{3,2},{4,5},{5,4},{6,7},{7,6},{8,9},{9,8},{10,11... | collective-permute-start | bytes 786440 | tf_op jit(solution)/shard_map/ppermute | solution.py:299
  16.5 1.9 %collective-permute-start.4 = (bf16[16,32,256]{2,1,0:T(8,128)(2,1)}, bf16[16,32,256]{2,1,0:T(8,128)(2,1)}, u32[]{:S(2)}, u32[]{:S(2)}) collective-permute-start(bf16[16,32,256]{2,1,0:T(8,128)(2,1)} %collective-permute-done.3.refs_2_), channel_id=1, source_target_pairs={{0,1},{1,0},{2,3},{3,2},{4,5},{5,4},{6,7},{7,6},{8,9},{9,8},{10,11... | collective-permute-start | bytes 786440 | tf_op jit(solution)/shard_map/ppermute | solution.py:299
  23.5 8.2 %collective-permute-start.10 = (bf16[13,16,256]{2,1,0:T(8,128)(2,1)}, bf16[13,16,256]{2,1,0:T(8,128)(2,1)S(1)}, u32[]{:S(2)}, u32[]{:S(2)}) collective-permute-start(bf16[13,16,256]{2,1,0:T(8,128)(2,1)} %get-tuple-element.71), channel_id=1, source_target_pairs={{0,4},{1,5},{2,6},{3,7},{4,0},{5,1},{6,2},{7,3},{8,12},{9,13},{10,... | collective-permute-start | bytes 319496 | tf_op jit(solution)/shard_map/ppermute | solution.py:348
  25.6 7.0 %collective-permute-start.11 = (bf16[13,16,256]{2,1,0:T(8,128)(2,1)}, bf16[13,16,256]{2,1,0:T(8,128)(2,1)S(1)}, u32[]{:S(2)}, u32[]{:S(2)}) collective-permute-start(bf16[13,16,256]{2,1,0:T(8,128)(2,1)} %get-tuple-element.72), channel_id=1, source_target_pairs={{0,5},{1,4},{2,7},{3,6},{4,1},{5,0},{6,3},{7,2},{8,13},{9,12},{10,... | collective-permute-start | bytes 319496 | tf_op jit(solution)/shard_map/ppermute | solution.py:348
  26.7 8.2 %collective-permute-start.12 = (bf16[13,16,256]{2,1,0:T(8,128)(2,1)}, bf16[13,16,256]{2,1,0:T(8,128)(2,1)S(1)}, u32[]{:S(2)}, u32[]{:S(2)}) collective-permute-start(bf16[13,16,256]{2,1,0:T(8,128)(2,1)} %get-tuple-element.73), channel_id=1, source_target_pairs={{0,6},{1,7},{2,0},{3,1},{4,2},{5,3},{6,4},{7,5},{8,14},{9,15},{10,... | collective-permute-start | bytes 319496 | tf_op jit(solution)/shard_map/ppermute | solution.py:348
  29.9 7.2 %collective-permute-start.13 = (bf16[13,16,256]{2,1,0:T(8,128)(2,1)}, bf16[13,16,256]{2,1,0:T(8,128)(2,1)S(1)}, u32[]{:S(2)}, u32[]{:S(2)}) collective-permute-start(bf16[13,16,256]{2,1,0:T(8,128)(2,1)} %get-tuple-element.74), channel_id=1, source_target_pairs={{0,7},{1,6},{2,1},{3,0},{4,3},{5,2},{6,5},{7,4},{8,15},{9,14},{10,... | collective-permute-start | bytes 319496 | tf_op jit(solution)/shard_map/ppermute | solution.py:348
  30.3 6.9 %collective-permute-start.7 = (bf16[13,16,256]{2,1,0:T(8,128)(2,1)}, bf16[13,16,256]{2,1,0:T(8,128)(2,1)S(1)}, u32[]{:S(2)}, u32[]{:S(2)}) collective-permute-start(bf16[13,16,256]{2,1,0:T(8,128)(2,1)} %get-tuple-element.68), channel_id=1, source_target_pairs={{0,3},{1,2},{2,5},{3,4},{4,7},{5,6},{6,1},{7,0},{8,11},{9,10},{10,... | collective-permute-start | bytes 319496 | tf_op jit(solution)/shard_map/ppermute | solution.py:348
  31.7 6.7 %collective-permute-start.8 = (bf16[13,16,256]{2,1,0:T(8,128)(2,1)}, bf16[13,16,256]{2,1,0:T(8,128)(2,1)S(1)}, u32[]{:S(2)}, u32[]{:S(2)}) collective-permute-start(bf16[13,16,256]{2,1,0:T(8,128)(2,1)} %get-tuple-element.69), channel_id=1, source_target_pairs={{0,2},{1,3},{2,4},{3,5},{4,6},{5,7},{6,0},{7,1},{8,10},{9,11},{10,... | collective-permute-start | bytes 319496 | tf_op jit(solution)/shard_map/ppermute | solution.py:348
  32.7 5.7 %collective-permute-start.9 = (bf16[13,16,256]{2,1,0:T(8,128)(2,1)}, bf16[13,16,256]{2,1,0:T(8,128)(2,1)S(1)}, u32[]{:S(2)}, u32[]{:S(2)}) collective-permute-start(bf16[13,16,256]{2,1,0:T(8,128)(2,1)} %get-tuple-element.70), channel_id=1, source_target_pairs={{0,1},{1,0},{2,3},{3,2},{4,5},{5,4},{6,7},{7,6},{8,9},{9,8},{10,11... | collective-permute-start | bytes 319496 | tf_op jit(solution)/shard_map/ppermute | solution.py:348
  39.9 7.5 %collective-permute-start.14 = (bf16[128,256]{1,0:T(8,128)(2,1)S(1)}, bf16[128,256]{1,0:T(8,128)(2,1)S(1)}, u32[]{:S(2)}, u32[]{:S(2)}) collective-permute-start(bf16[128,256]{1,0:T(8,128)(2,1)S(1)} %get-tuple-element.87), channel_id=1, source_target_pairs={{0,16},{8,24},{16,0},{24,8},{1,17},{9,25},{17,1},{25,9},{2,18},{10... | collective-permute-start | bytes 196616 | tf_op jit(solution)/shard_map/ppermute | solution.py:365
  41.6 5.8 %collective-permute-start.15 = (bf16[128,256]{1,0:T(8,128)(2,1)S(1)}, bf16[128,256]{1,0:T(8,128)(2,1)S(1)}, u32[]{:S(2)}, u32[]{:S(2)}) collective-permute-start(bf16[128,256]{1,0:T(8,128)(2,1)S(1)} %get-tuple-element.88), channel_id=1, source_target_pairs={{0,8},{8,16},{16,24},{24,0},{1,9},{9,17},{17,25},{25,1},{2,10},{10... | collective-permute-start | bytes 196616 | tf_op jit(solution)/shard_map/ppermute | solution.py:365
  42.3 5.1 %collective-permute-start.16 = (bf16[128,256]{1,0:T(8,128)(2,1)S(1)}, bf16[128,256]{1,0:T(8,128)(2,1)S(1)}, u32[]{:S(2)}, u32[]{:S(2)}) collective-permute-start(bf16[128,256]{1,0:T(8,128)(2,1)S(1)} %get-tuple-element.89), channel_id=1, source_target_pairs={{0,24},{8,0},{16,8},{24,16},{1,25},{9,1},{17,9},{25,17},{2,26},{10... | collective-permute-start | bytes 196616 | tf_op jit(solution)/shard_map/ppermute | solution.py:365
  44.9 19.3 %copy-start = (bf16[4,4,256,256]{3,2,1,0:T(8,128)(2,1)S(1)}, bf16[4,4,256,256]{3,2,1,0:T(8,128)(2,1)}, u32[]{:S(2)}) copy-start(bf16[4,4,256,256]{3,2,1,0:T(8,128)(2,1)} %d_ref.7) | copy-start | bytes 6291460
  109.6 28.1 %copy-start.1 = (f32[4,4,32,256]{3,2,1,0:T(8,128)S(1)}, f32[4,4,32,256]{3,2,1,0:T(8,128)}, u32[]{:S(2)}) copy-start(f32[4,4,32,256]{3,2,1,0:T(8,128)} %param.12) | copy-start | bytes 1572868
  128.6 5.4 %collective-permute-start.17 = (bf16[8,16,256]{2,1,0:T(8,128)(2,1)S(1)}, bf16[8,16,256]{2,1,0:T(8,128)(2,1)S(1)}, u32[]{:S(2)}, u32[]{:S(2)}) collective-permute-start(bf16[8,16,256]{2,1,0:T(8,128)(2,1)S(1)} %all_to_all.47), channel_id=1, source_target_pairs={{0,24},{8,0},{16,8},{24,16},{1,25},{9,1},{17,9},{25,17},{2,26},{10... | collective-permute-start | bytes 196616 | tf_op jit(solution)/shard_map/ppermute | solution.py:447
  131.5 5.9 %collective-permute-start.18 = (bf16[8,16,256]{2,1,0:T(8,128)(2,1)S(1)}, bf16[8,16,256]{2,1,0:T(8,128)(2,1)S(1)}, u32[]{:S(2)}, u32[]{:S(2)}) collective-permute-start(bf16[8,16,256]{2,1,0:T(8,128)(2,1)S(1)} %all_to_all.47), channel_id=1, source_target_pairs={{0,16},{8,24},{16,0},{24,8},{1,17},{9,25},{17,1},{25,9},{2,18},{10... | collective-permute-start | bytes 196616 | tf_op jit(solution)/shard_map/ppermute | solution.py:447
  131.5 6.2 %collective-permute-start.19 = (bf16[8,16,256]{2,1,0:T(8,128)(2,1)S(1)}, bf16[8,16,256]{2,1,0:T(8,128)(2,1)S(1)}, u32[]{:S(2)}, u32[]{:S(2)}) collective-permute-start(bf16[8,16,256]{2,1,0:T(8,128)(2,1)S(1)} %all_to_all.47), channel_id=1, source_target_pairs={{0,8},{8,16},{16,24},{24,0},{1,9},{9,17},{17,25},{25,1},{2,10},{10... | collective-permute-start | bytes 196616 | tf_op jit(solution)/shard_map/ppermute | solution.py:447

commit v4 on v3

--- a/solution.py
+++ b/solution.py
@@ -52,8 +52,8 @@
 def tile_kernel(n_blocks, core_ref, plan_ref, note_ref, side_ref, a_ref, *refs):
     blocks = refs[:n_blocks]
     core = core_ref[0]
-    res_ref, out_refs = refs[n_blocks], refs[n_blocks + 1 : n_blocks + 1 + OWNERS]
-    send_ref, x_all, low_ref, sems, note_sems = refs[n_blocks + 1 + OWNERS :]
+    res_ref, out_refs = refs[n_blocks], refs[n_blocks + 1 : n_blocks + 2 + X]
+    send_ref, x_all, low_ref, sems, note_sems = refs[n_blocks + 2 + X :]
     tiles = a_ref.shape[0]
     mine = x_all.shape[0] // OWNERS
     half = x_all.shape[1] // 2
@@ -80,8 +80,10 @@
         term = dot(low_ref[plan_ref[2, t]], a_ref[t], NN).astype(BF16)
         send_ref[spot] = term[:half]
         send_ref[spot + 1] = term[half:]
-    for o, ref in enumerate(out_refs):
-        ref[...] = send_ref[o * per : (o + 1) * per]
+    at = 0
+    for ref in out_refs:
+        ref[...] = send_ref[at : at + ref.shape[0]]
+        at += ref.shape[0]
 
 
 def in_hbm(x):
@@ -126,17 +128,13 @@
 
 
 def pick_kernel(mine, y_ref, *refs):
-    own_hbm, recvs, outs, (own, data, pick, sem) = refs[0], refs[1:OWNERS], refs[OWNERS:-4], refs[-4:]
-    copy = pltpu.make_async_copy(own_hbm, own, sem)
-    copy.start()
-    blocks, size, T = own.shape
+    recvs, outs, (data, pick) = refs[:OWNERS], refs[OWNERS:-2], refs[-2:]
+    blocks, size, T = recvs[0].shape
     rows = (blocks - 1) * size
     K = rows // CAP
     lane = lax.broadcasted_iota(jnp.int32, (1, 128), 1)
     marks, codes = [], []
-    for i, ref in enumerate((*recvs, own)):
-        if i == len(recvs):
-            copy.wait()
+    for i, ref in enumerate(recvs):
         data[i * rows : (i + 1) * rows, :] = ref[: blocks - 1].reshape(rows, T)
         note = ref[blocks - 1].astype(F32)
         marks += [note[j : j + 1, :128] for j in range(CAP)]
@@ -305,9 +303,11 @@
         out_shape=(
             jax.ShapeDtypeStruct((row_tiles, K, T), F32),
         )
-        + (pltpu.HBM((slot_rows // 16, 16, T), BF16),) * OWNERS,
+        + (jax.ShapeDtypeStruct((slot_rows // 16, 16, T), BF16),)
+        + (pltpu.HBM((slot_rows // 16, 16, T), BF16),)
+        + (pltpu.HBM((CORE * slot_rows // 16, 16, T), BF16),) * (X - 1),
         in_specs=[SMEM, SMEM, ANY, ANY, VMEM] + [ANY] * len(blocks),
-        out_specs=(VMEM,) * (1 + OWNERS),
+        out_specs=(VMEM,) * (2 + X),
         scratch_shapes=[
             pltpu.VMEM((OWNERS * slot_rows // 16, 16, T), BF16),
             pltpu.VMEM((OWNERS * mine, K, T), BF16),
@@ -338,29 +338,22 @@
         scatter.append((spots[:, None] == spot_at[level - 1][None, :]).astype(BF16))
     stage = pltpu.VMEM((n_terms + pad_terms, T), F32)
 
-    recv = [first_send]
-    for away in (3, 2, 1, 4, 5, 6, 7):
-        step, swap = away // CORE, away % CORE
-        perm = []
-        for x in range(X):
-            for c in range(CORE):
-                perm.append((x * CORE + c, (x + step) % X * CORE + (c + swap) % CORE))
-        recv.append(lax.ppermute(send[away], snode, perm))
+    arrived = {step: lax.ppermute(send[1 + step], "x", shift(X, step)) for step in (2, 1, 3)}
+    n = slot_rows // 16
+    recv = [first_send, other(send[1])] + [other(arrived[step][n:]) for step in (2, 1, 3)] + [arrived[step] for step in (2, 1, 3)]
     recv, look, scatter, to, place = lax.optimization_barrier((recv, look, scatter, to, place))
     part = pl.pallas_call(
         functools.partial(pick_kernel, mine),
         out_shape=(jax.ShapeDtypeStruct((Z * mine, T), BF16),) * Y,
-        in_specs=[SMEM, ANY] + [VMEM] * (OWNERS - 1),
+        in_specs=[SMEM] + [VMEM] * OWNERS,
         out_specs=(VMEM,) * Y,
         scratch_shapes=[
-            pltpu.VMEM((slot_rows // 16, 16, T), BF16),
             pltpu.VMEM((OWNERS * CAP * K, T), BF16),
             pltpu.VMEM((Z * mine, OWNERS * CAP * K), BF16),
-            pltpu.SemaphoreType.DMA(()),
         ],
         compiler_params=PARAMS,
         name="pick",
-    )(y.reshape(1), in_hbm(recv[0]), *recv[1:])
+    )(y.reshape(1), *recv)
     total = part[0].astype(F32)
     arrived = [lax.ppermute(part[s], "y", shift(Y, s)) for s in (2, 1, 3)]
     (c_near,) = bring_near(part[0], coupling)

time: 139 us -> 141 us (1.014)
  waiting for transfers between devices: 19.4 us -> 23.6 us
  starting transfers between devices: 22.2 us -> 19.7 us
    ppermute x7, waiting for transfers between devices: 6.3 us -> 10.5 us  [the longest x3 9.25 us: local(): lax.ppermute(send[1 + step], 'x', shift(X, step))]
    ppermute x7, starting transfers between devices: 8.43 us -> 6.15 us  [the longest x3 5.39 us: local(): lax.ppermute(send[1 + step], 'x', shift(X, step))]
  transfers between devices with their start and end apart: 20 -> 20, of which waited for: 11 -> 10; matrix products, arithmetic and copies ran while one was open for 0% -> 0% of each run, Pallas kernels for 5% -> 4%
where the time goes in v4:
time: 141 us
  blocking collectives  76.1 us (54%)
  waiting for transfers between devices  23.6 us (17%)
  starting transfers between devices  19.7 us (14%)
  Pallas kernels  17.6 us (12%)
  other arithmetic  1.43 us (1%)
    all_to_all x3, blocking collectives, local(): known.append(lax.all_to_all(out, snode, 0, 0, tiled=True))  25.1 us
    all_to_all x3, blocking collectives, local(): arrived = lax.all_to_all(out, snode, 0, 0, tiled=True)  23.6 us
    all_to_all x1, blocking collectives, local(): lax.all_to_all(total.astype(BF16).reshape(Z, mine, T), 'z', 0, 0, tiled=T...  16.7 us
    all_to_all x1, blocking collectives, local(): column = lax.all_to_all(change, 'z', 0, 0, tiled=True)  10.8 us
    ppermute x3, waiting for transfers between devices, local(): lax.ppermute(send[1 + step], 'x', shift(X, step))  9.25 us
    ppermute x3, waiting for transfers between devices, along(): return lax.ppermute(block, snode, perm)  5.92 us
    ppermute x3, starting transfers between devices, local(): lax.ppermute(send[1 + step], 'x', shift(X, step))  5.39 us
    ppermute x3, waiting for transfers between devices, local(): lax.ppermute(column, 'y', shift(Y, -s % Y))  5.24 us
  transfers between devices with their start and end apart: 20, of which 10 were waited for; matrix products, arithmetic and copies ran while one was open for 0% of the time, Pallas kernels for 4%

profile of v4, /device:TPU:2, one launch (start us, length us, event | category | flops | bytes accessed | tf_op | source)
XLA Modules:
  0.0 140.6 jit_solution(12882803415170982143)
XLA Ops:
  0.6 1.1 convert_element_type.37
  1.8 1.6 %collective-permute-start.2 = (bf16[16,32,256]{2,1,0:T(8,128)(2,1)S(1)}, bf16[16,32,256]{2,1,0:T(8,128)(2,1)}, u32[]{:S(2)}, u32[]{:S(2)}) collective-permute-start(bf16[16,32,256]{2,1,0:T(8,128)(2,1)S(1)} %bitcast.18), channel_id=1, source_target_pairs={{0,2},{1,7},{2,4},{3,1},{4,6},{5,3},{6,0},{7,5},{8,10},{9,15},{10,... | collective-permute-start | bytes 786440 | tf_op jit(solution)/shard_map/ppermute | solution.py:274
  3.5 1.5 %collective-permute-start.1 = (bf16[16,32,256]{2,1,0:T(8,128)(2,1)}, bf16[16,32,256]{2,1,0:T(8,128)(2,1)}, u32[]{:S(2)}, u32[]{:S(2)}) collective-permute-start(bf16[16,32,256]{2,1,0:T(8,128)(2,1)} %collective-permute-done.refs_1_), channel_id=1, source_target_pairs={{0,2},{1,7},{2,4},{3,1},{4,6},{5,3},{6,0},{7,5},{8,10},{9,15},{10,... | collective-permute-start | bytes 786440 | tf_op jit(solution)/shard_map/ppermute | solution.py:274
  5.0 3.7 %collective-permute-done.2.refs_4_ = bf16[16,32,256]{2,1,0:T(8,128)(2,1)} collective-permute-done((bf16[16,32,256]{2,1,0:T(8,128)(2,1)S(1)}, bf16[16,32,256]{2,1,0:T(8,128)(2,1)}, u32[]{:S(2)}, u32[]{:S(2)}) %collective-permute-start.2) | collective-permute-done | bytes 262176 | tf_op jit(solution)/shard_map/ppermute | solution.py:274
  8.6 1.2 collective-permute-start.3
  9.9 1.9 %bring_near.2.a_ref = bf16[24,256,256]{2,1,0:T(8,128)(2,1)S(1)} custom-call(bf16[24,256,256]{2,1,0:T(8,128)(2,1)} %refs_0_.2), custom_call_target="tpu_custom_call" | custom-call | tf_op jit(solution)/shard_map/bring_near/pallas_call | solution.py:119
  11.8 1.9 %plan.1 = (s32[5,24]{1,0:T(8,128)S(1)}, bf16[8,16,256]{2,1,0:T(8,128)(2,1)}) custom-call(s32[1]{0:T(128)} %bitcast.2.here_ref, s32[24]{0:T(128)} %col_ref.1, s32[24]{0:T(128)} %row_ref.1), custom_call_target="tpu_custom_call" | custom-call | tf_op jit(solution)/shard_map/plan/pallas_call | solution.py:280
  14.3 2.3 %collective-permute-done.3.refs_2_ = bf16[16,32,256]{2,1,0:T(8,128)(2,1)} collective-permute-done((bf16[16,32,256]{2,1,0:T(8,128)(2,1)}, bf16[16,32,256]{2,1,0:T(8,128)(2,1)}, u32[]{:S(2)}, u32[]{:S(2)}) %collective-permute-start.3) | collective-permute-done | bytes 262176 | tf_op jit(solution)/shard_map/ppermute | solution.py:274
  16.5 1.8 %collective-permute-done.4.refs_3_ = bf16[16,32,256]{2,1,0:T(8,128)(2,1)} collective-permute-done((bf16[16,32,256]{2,1,0:T(8,128)(2,1)}, bf16[16,32,256]{2,1,0:T(8,128)(2,1)}, u32[]{:S(2)}, u32[]{:S(2)}) %collective-permute-start.4) | collective-permute-done | bytes 262176 | tf_op jit(solution)/shard_map/ppermute | solution.py:297
  18.4 4.8 %tile_products.1 = (f32[8,32,256]{2,1,0:T(8,128)}, bf16[13,16,256]{2,1,0:T(8,128)(2,1)S(1)}, bf16[13,16,256]{2,1,0:T(8,128)(2,1)}, bf16[26,16,256]{2,1,0:T(8,128...) custom-call(s32[1]{0:T(128)} %bitcast.core_ref, s32[5,24]{1,0:T(8,128)S(1)} %get-tuple-element.57.plan_ref, ...), custom_call_target="tpu_custom_call" | custom-call | tf_op jit(solution)/shard_map/tile_products/pallas_call | solution.py:301
  23.6 3.3 %collective-permute-start.12 = (bf16[26,16,256]{2,1,0:T(8,128)(2,1)}, bf16[26,16,256]{2,1,0:T(8,128)(2,1)S(1)}, u32[]{:S(2)}, u32[]{:S(2)}) collective-permute-start(bf16[26,16,256]{2,1,0:T(8,128)(2,1)} %get-tuple-element.68), channel_id=1, source_target_pairs={{0,6},{2,0},{4,2},{6,4},{1,7},{3,1},{5,3},{7,5},{8,14},{10,8},{12,... | collective-permute-start | bytes 638984 | tf_op jit(solution)/shard_map/ppermute | solution.py:341
  26.9 2.0 %collective-permute-start.8 = (bf16[26,16,256]{2,1,0:T(8,128)(2,1)}, bf16[26,16,256]{2,1,0:T(8,128)(2,1)S(1)}, u32[]{:S(2)}, u32[]{:S(2)}) collective-permute-start(bf16[26,16,256]{2,1,0:T(8,128)(2,1)} %get-tuple-element.66), channel_id=1, source_target_pairs={{0,4},{2,6},{4,0},{6,2},{1,5},{3,7},{5,1},{7,3},{8,12},{10,14},{12... | collective-permute-start | bytes 638984 | tf_op jit(solution)/shard_map/ppermute | solution.py:341
  29.0 4.1 %collective-permute-done.10.refs_6_ = bf16[26,16,256]{2,1,0:T(8,128)(2,1)S(1)} collective-permute-done((bf16[26,16,256]{2,1,0:T(8,128)(2,1)}, bf16[26,16,256]{2,1,0:T(8,128)(2,1)S(1)}, u32[]{:S(2)}, u32[]{:S(2)}) %collective-permute-start.10) | collective-permute-done | bytes 213024 | tf_op jit(solution)/shard_map/ppermute | solution.py:341
  33.8 5.1 %collective-permute-done.8.refs_5_ = bf16[26,16,256]{2,1,0:T(8,128)(2,1)S(1)} collective-permute-done((bf16[26,16,256]{2,1,0:T(8,128)(2,1)}, bf16[26,16,256]{2,1,0:T(8,128)(2,1)S(1)}, u32[]{:S(2)}, u32[]{:S(2)}) %collective-permute-start.8) | collective-permute-done | bytes 213024 | tf_op jit(solution)/shard_map/ppermute | solution.py:341
  39.1 1.2 collective-permute-done.9.refs_2_
  40.9 1.5 %collective-permute-start.14 = (bf16[128,256]{1,0:T(8,128)(2,1)S(1)}, bf16[128,256]{1,0:T(8,128)(2,1)S(1)}, u32[]{:S(2)}, u32[]{:S(2)}) collective-permute-start(bf16[128,256]{1,0:T(8,128)(2,1)S(1)} %get-tuple-element.81), channel_id=1, source_target_pairs={{0,16},{8,24},{16,0},{24,8},{1,17},{9,25},{17,1},{25,9},{2,18},{10... | collective-permute-start | bytes 196616 | tf_op jit(solution)/shard_map/ppermute | solution.py:358
  43.1 2.6 %collective-permute-start.16 = (bf16[128,256]{1,0:T(8,128)(2,1)S(1)}, bf16[128,256]{1,0:T(8,128)(2,1)S(1)}, u32[]{:S(2)}, u32[]{:S(2)}) collective-permute-start(bf16[128,256]{1,0:T(8,128)(2,1)S(1)} %get-tuple-element.83), channel_id=1, source_target_pairs={{0,24},{8,0},{16,8},{24,16},{1,25},{9,1},{17,9},{25,17},{2,26},{10... | collective-permute-start | bytes 196616 | tf_op jit(solution)/shard_map/ppermute | solution.py:358
  45.7 2.5 %bring_near.3.refs_1_.refs_2_.refs_3_.c_ref = bf16[3,4,3,256,256]{4,3,2,1,0:T(8,128)(2,1)S(1)} custom-call(bf16[3,4,3,256,256]{4,3,2,1,0:T(8,128)(2,1)} %refs_0_.3, bf16[128,256]{1,0:T(8,128)(2,1)S(1)} %get-tuple-element.80.refs_1_), custom_call_target="tpu_custom_call" | custom-call | tf_op jit(solution)/shard_map/bring_near/pallas_call | solution.py:119
  48.3 16.7 %all_to_all.40.parts_ref = bf16[8,16,256]{2,1,0:T(8,128)(2,1)S(1)} all-to-all(bf16[8,16,256]{2,1,0:T(8,128)(2,1)S(1)} %bitcast.21), channel_id=1, replica_groups=mesh['z'=8,'y'=4,'x'=4,'core'=2] {'z'}, dimensions={0} | all-to-all | bytes 131072 | tf_op jit(solution)/shard_map/all_to_all | solution.py:363
  65.2 9.4 %all_to_all.41.refs_0_ = bf16[8,8,256]{2,1,0:T(8,128)(2,1)S(1)} all-to-all(bf16[8,8,256]{2,1,0:T(8,128)(2,1)S(1)} %get-tuple-element.90), channel_id=1, replica_groups=mesh['z'=8,'y'=4,'x'=4,'core'=2] {'x','core'}, dimensions={0} | all-to-all | bytes 65536 | tf_op jit(solution)/shard_map/all_to_all | solution.py:388
  75.4 7.8 %all_to_all.42.refs_1_ = bf16[8,8,256]{2,1,0:T(8,128)(2,1)S(1)} all-to-all(bf16[8,8,256]{2,1,0:T(8,128)(2,1)S(1)} %get-tuple-element.94), channel_id=1, replica_groups=mesh['z'=8,'y'=4,'x'=4,'core'=2] {'x','core'}, dimensions={0} | all-to-all | bytes 65536 | tf_op jit(solution)/shard_map/all_to_all | solution.py:388
  84.1 7.8 %all_to_all.43.refs_2_ = bf16[8,8,256]{2,1,0:T(8,128)(2,1)S(1)} all-to-all(bf16[8,8,256]{2,1,0:T(8,128)(2,1)S(1)} %get-tuple-element.98), channel_id=1, replica_groups=mesh['z'=8,'y'=4,'x'=4,'core'=2] {'x','core'}, dimensions={0} | all-to-all | bytes 65536 | tf_op jit(solution)/shard_map/all_to_all | solution.py:388
  91.9 1.6 %turn.1 = (f32[4,256]{1,0:T(4,128)S(1)}, bf16[8,8,256]{2,1,0:T(8,128)(2,1)S(1)}, f32[128,256]{1,0:T(8,128)S(1)}) custom-call(f32[16,256]{1,0:T(8,128)S(1)} %get-tuple-element.88.g_ref, bf16[16,192]{1,0:T(8,128)(2,1)S(1)} %fusion.6.look_ref, bf16[192,16]{1,0:T(8,128)(2,1)S(1)} %fusion.3.scatter_ref, bf16[8,8,256]{2,1,0:T(8,128)(2,1)S(1)} %all_to_all.41.refs_0_, ...), custom_call_target="tpu_custom_call" | custom-call | tf_op jit(solution)/shard_map/turn/pallas_call | solution.py:402
  93.6 7.8 %all_to_all.44.recv_ref = bf16[8,8,256]{2,1,0:T(8,128)(2,1)S(1)} all-to-all(bf16[8,8,256]{2,1,0:T(8,128)(2,1)S(1)} %get-tuple-element.99), channel_id=1, replica_groups=mesh['z'=8,'y'=4,'x'=4,'core'=2] {'x','core'}, dimensions={0} | all-to-all | bytes 65536 | tf_op jit(solution)/shard_map/all_to_all | solution.py:414
  101.4 1.1 backward_2.1
  102.5 7.8 %all_to_all.45.recv_ref = bf16[8,8,256]{2,1,0:T(8,128)(2,1)S(1)} all-to-all(bf16[8,8,256]{2,1,0:T(8,128)(2,1)S(1)} %get-tuple-element.102), channel_id=1, replica_groups=mesh['z'=8,'y'=4,'x'=4,'core'=2] {'x','core'}, dimensions={0} | all-to-all | bytes 65536 | tf_op jit(solution)/shard_map/all_to_all | solution.py:414
  111.4 7.9 %all_to_all.46.recv_ref = bf16[8,8,256]{2,1,0:T(8,128)(2,1)S(1)} all-to-all(bf16[8,8,256]{2,1,0:T(8,128)(2,1)S(1)} %get-tuple-element.105), channel_id=1, replica_groups=mesh['z'=8,'y'=4,'x'=4,'core'=2] {'x','core'}, dimensions={0} | all-to-all | bytes 65536 | tf_op jit(solution)/shard_map/all_to_all | solution.py:414
  119.6 10.8 %all_to_all.47 = bf16[8,16,256]{2,1,0:T(8,128)(2,1)S(1)} all-to-all(bf16[8,16,256]{2,1,0:T(8,128)(2,1)S(1)} %backward_0.1), channel_id=1, replica_groups=mesh['z'=8,'y'=4,'x'=4,'core'=2] {'z'}, dimensions={0} | all-to-all | bytes 131072 | tf_op jit(solution)/shard_map/all_to_all | solution.py:439
  130.3 2.9 %collective-permute-start.17 = (bf16[8,16,256]{2,1,0:T(8,128)(2,1)S(1)}, bf16[8,16,256]{2,1,0:T(8,128)(2,1)S(1)}, u32[]{:S(2)}, u32[]{:S(2)}) collective-permute-start(bf16[8,16,256]{2,1,0:T(8,128)(2,1)S(1)} %all_to_all.47), channel_id=1, source_target_pairs={{0,24},{8,0},{16,8},{24,16},{1,25},{9,1},{17,9},{25,17},{2,26},{10... | collective-permute-start | bytes 196616 | tf_op jit(solution)/shard_map/ppermute | solution.py:440
  134.2 1.6 %collective-permute-done.17 = bf16[8,16,256]{2,1,0:T(8,128)(2,1)S(1)} collective-permute-done((bf16[8,16,256]{2,1,0:T(8,128)(2,1)S(1)}, bf16[8,16,256]{2,1,0:T(8,128)(2,1)S(1)}, u32[]{:S(2)}, u32[]{:S(2)}) %collective-permute-start.17) | collective-permute-done | bytes 65568 | tf_op jit(solution)/shard_map/ppermute | solution.py:440
  135.7 3.4 %collective-permute-done.18 = bf16[8,16,256]{2,1,0:T(8,128)(2,1)S(1)} collective-permute-done((bf16[8,16,256]{2,1,0:T(8,128)(2,1)S(1)}, bf16[8,16,256]{2,1,0:T(8,128)(2,1)S(1)}, u32[]{:S(2)}, u32[]{:S(2)}) %collective-permute-start.18) | collective-permute-done | bytes 65568 | tf_op jit(solution)/shard_map/ppermute | solution.py:440
  139.5 1.2 convolution_add_fusion
  (53 shorter events, 7.9 us)
Async XLA Ops:
  1.7 1.8 %collective-permute-start = (bf16[16,32,256]{2,1,0:T(8,128)(2,1)S(1)}, bf16[16,32,256]{2,1,0:T(8,128)(2,1)}, u32[]{:S(2)}, u32[]{:S(2)}) collective-permute-start(bf16[16,32,256]{2,1,0:T(8,128)(2,1)S(1)} %bitcast.17), channel_id=1, source_target_pairs={{0,1},{1,0},{2,3},{3,2},{4,5},{5,4},{6,7},{7,6},{8,9},{9,8},{10,11... | collective-permute-start | bytes 786440 | tf_op jit(solution)/shard_map/ppermute | solution.py:277
  1.8 6.8 %collective-permute-start.2 = (bf16[16,32,256]{2,1,0:T(8,128)(2,1)S(1)}, bf16[16,32,256]{2,1,0:T(8,128)(2,1)}, u32[]{:S(2)}, u32[]{:S(2)}) collective-permute-start(bf16[16,32,256]{2,1,0:T(8,128)(2,1)S(1)} %bitcast.18), channel_id=1, source_target_pairs={{0,2},{1,7},{2,4},{3,1},{4,6},{5,3},{6,0},{7,5},{8,10},{9,15},{10,... | collective-permute-start | bytes 786440 | tf_op jit(solution)/shard_map/ppermute | solution.py:274
  3.5 10.3 %collective-permute-start.1 = (bf16[16,32,256]{2,1,0:T(8,128)(2,1)}, bf16[16,32,256]{2,1,0:T(8,128)(2,1)}, u32[]{:S(2)}, u32[]{:S(2)}) collective-permute-start(bf16[16,32,256]{2,1,0:T(8,128)(2,1)} %collective-permute-done.refs_1_), channel_id=1, source_target_pairs={{0,2},{1,7},{2,4},{3,1},{4,6},{5,3},{6,0},{7,5},{8,10},{9,15},{10,... | collective-permute-start | bytes 786440 | tf_op jit(solution)/shard_map/ppermute | solution.py:274
  8.6 7.9 %collective-permute-start.3 = (bf16[16,32,256]{2,1,0:T(8,128)(2,1)}, bf16[16,32,256]{2,1,0:T(8,128)(2,1)}, u32[]{:S(2)}, u32[]{:S(2)}) collective-permute-start(bf16[16,32,256]{2,1,0:T(8,128)(2,1)} %collective-permute-done.2.refs_4_), channel_id=1, source_target_pairs={{0,2},{1,7},{2,4},{3,1},{4,6},{5,3},{6,0},{7,5},{8,10},{9,15},{10,... | collective-permute-start | bytes 786440 | tf_op jit(solution)/shard_map/ppermute | solution.py:274
  11.7 11.5 %copy-start.2 = (s32[3,4,3]{2,1,0:T(4,128)S(1)}, s32[3,4,3]{2,1,0:T(4,128)}, u32[]{:S(2)}) copy-start(s32[3,4,3]{2,1,0:T(4,128)} %param.15) | copy-start | bytes 436
  13.7 2.9 %collective-permute-start.6 = (bf16[16,32,256]{2,1,0:T(8,128)(2,1)}, bf16[16,32,256]{2,1,0:T(8,128)(2,1)}, u32[]{:S(2)}, u32[]{:S(2)}) collective-permute-start(bf16[16,32,256]{2,1,0:T(8,128)(2,1)} %collective-permute-done.2.refs_4_), channel_id=1, source_target_pairs={{0,1},{1,0},{2,3},{3,2},{4,5},{5,4},{6,7},{7,6},{8,9},{9,8},{10,11... | collective-permute-start | bytes 786440 | tf_op jit(solution)/shard_map/ppermute | solution.py:293
  13.8 2.7 %collective-permute-start.5 = (bf16[16,32,256]{2,1,0:T(8,128)(2,1)}, bf16[16,32,256]{2,1,0:T(8,128)(2,1)}, u32[]{:S(2)}, u32[]{:S(2)}) collective-permute-start(bf16[16,32,256]{2,1,0:T(8,128)(2,1)} %collective-permute-done.1.refs_5_), channel_id=1, source_target_pairs={{0,1},{1,0},{2,3},{3,2},{4,5},{5,4},{6,7},{7,6},{8,9},{9,8},{10,11... | collective-permute-start | bytes 786440 | tf_op jit(solution)/shard_map/ppermute | solution.py:297
  16.5 1.9 %collective-permute-start.4 = (bf16[16,32,256]{2,1,0:T(8,128)(2,1)}, bf16[16,32,256]{2,1,0:T(8,128)(2,1)}, u32[]{:S(2)}, u32[]{:S(2)}) collective-permute-start(bf16[16,32,256]{2,1,0:T(8,128)(2,1)} %collective-permute-done.3.refs_2_), channel_id=1, source_target_pairs={{0,1},{1,0},{2,3},{3,2},{4,5},{5,4},{6,7},{7,6},{8,9},{9,8},{10,11... | collective-permute-start | bytes 786440 | tf_op jit(solution)/shard_map/ppermute | solution.py:297
  23.5 9.6 %collective-permute-start.10 = (bf16[26,16,256]{2,1,0:T(8,128)(2,1)}, bf16[26,16,256]{2,1,0:T(8,128)(2,1)S(1)}, u32[]{:S(2)}, u32[]{:S(2)}) collective-permute-start(bf16[26,16,256]{2,1,0:T(8,128)(2,1)} %get-tuple-element.67), channel_id=1, source_target_pairs={{0,2},{2,4},{4,6},{6,0},{1,3},{3,5},{5,7},{7,1},{8,10},{10,12},{12... | collective-permute-start | bytes 638984 | tf_op jit(solution)/shard_map/ppermute | solution.py:341
  23.6 9.6 %collective-permute-start.12 = (bf16[26,16,256]{2,1,0:T(8,128)(2,1)}, bf16[26,16,256]{2,1,0:T(8,128)(2,1)S(1)}, u32[]{:S(2)}, u32[]{:S(2)}) collective-permute-start(bf16[26,16,256]{2,1,0:T(8,128)(2,1)} %get-tuple-element.68), channel_id=1, source_target_pairs={{0,6},{2,0},{4,2},{6,4},{1,7},{3,1},{5,3},{7,5},{8,14},{10,8},{12,... | collective-permute-start | bytes 638984 | tf_op jit(solution)/shard_map/ppermute | solution.py:341
  26.9 12.0 %collective-permute-start.8 = (bf16[26,16,256]{2,1,0:T(8,128)(2,1)}, bf16[26,16,256]{2,1,0:T(8,128)(2,1)S(1)}, u32[]{:S(2)}, u32[]{:S(2)}) collective-permute-start(bf16[26,16,256]{2,1,0:T(8,128)(2,1)} %get-tuple-element.66), channel_id=1, source_target_pairs={{0,4},{2,6},{4,0},{6,2},{1,5},{3,7},{5,1},{7,3},{8,12},{10,14},{12... | collective-permute-start | bytes 638984 | tf_op jit(solution)/shard_map/ppermute | solution.py:341
  28.9 10.2 %collective-permute-start.7 = (bf16[13,16,256]{2,1,0:T(8,128)(2,1)}, bf16[13,16,256]{2,1,0:T(8,128)(2,1)S(1)}, u32[]{:S(2)}, u32[]{:S(2)}) collective-permute-start(bf16[13,16,256]{2,1,0:T(8,128)(2,1)} %get-tuple-element.65), channel_id=1, source_target_pairs={{0,1},{1,0},{2,3},{3,2},{4,5},{5,4},{6,7},{7,6},{8,9},{9,8},{10,11... | collective-permute-start | bytes 319496 | tf_op jit(solution)/shard_map/ppermute | solution.py:343
  33.1 6.0 %collective-permute-start.11 = (bf16[13,16,256]{2,1,0:T(8,128)(2,1)S(1)}, bf16[13,16,256]{2,1,0:T(8,128)(2,1)S(1)}, u32[]{:S(2)}, u32[]{:S(2)}) collective-permute-start(bf16[13,16,256]{2,1,0:T(8,128)(2,1)S(1)} %slice.28), channel_id=1, source_target_pairs={{0,1},{1,0},{2,3},{3,2},{4,5},{5,4},{6,7},{7,6},{8,9},{9,8},{10,11... | collective-permute-start | bytes 319496 | tf_op jit(solution)/shard_map/ppermute | solution.py:343
  33.2 5.9 %collective-permute-start.13 = (bf16[13,16,256]{2,1,0:T(8,128)(2,1)S(1)}, bf16[13,16,256]{2,1,0:T(8,128)(2,1)S(1)}, u32[]{:S(2)}, u32[]{:S(2)}) collective-permute-start(bf16[13,16,256]{2,1,0:T(8,128)(2,1)S(1)} %slice.29), channel_id=1, source_target_pairs={{0,1},{1,0},{2,3},{3,2},{4,5},{5,4},{6,7},{7,6},{8,9},{9,8},{10,11... | collective-permute-start | bytes 319496 | tf_op jit(solution)/shard_map/ppermute | solution.py:343
  38.9 1.4 collective-permute-start.9
  40.9 7.3 %collective-permute-start.14 = (bf16[128,256]{1,0:T(8,128)(2,1)S(1)}, bf16[128,256]{1,0:T(8,128)(2,1)S(1)}, u32[]{:S(2)}, u32[]{:S(2)}) collective-permute-start(bf16[128,256]{1,0:T(8,128)(2,1)S(1)} %get-tuple-element.81), channel_id=1, source_target_pairs={{0,16},{8,24},{16,0},{24,8},{1,17},{9,25},{17,1},{25,9},{2,18},{10... | collective-permute-start | bytes 196616 | tf_op jit(solution)/shard_map/ppermute | solution.py:358
  42.5 5.8 %collective-permute-start.15 = (bf16[128,256]{1,0:T(8,128)(2,1)S(1)}, bf16[128,256]{1,0:T(8,128)(2,1)S(1)}, u32[]{:S(2)}, u32[]{:S(2)}) collective-permute-start(bf16[128,256]{1,0:T(8,128)(2,1)S(1)} %get-tuple-element.82), channel_id=1, source_target_pairs={{0,8},{8,16},{16,24},{24,0},{1,9},{9,17},{17,25},{25,1},{2,10},{10... | collective-permute-start | bytes 196616 | tf_op jit(solution)/shard_map/ppermute | solution.py:358
  43.1 5.1 %collective-permute-start.16 = (bf16[128,256]{1,0:T(8,128)(2,1)S(1)}, bf16[128,256]{1,0:T(8,128)(2,1)S(1)}, u32[]{:S(2)}, u32[]{:S(2)}) collective-permute-start(bf16[128,256]{1,0:T(8,128)(2,1)S(1)} %get-tuple-element.83), channel_id=1, source_target_pairs={{0,24},{8,0},{16,8},{24,16},{1,25},{9,1},{17,9},{25,17},{2,26},{10... | collective-permute-start | bytes 196616 | tf_op jit(solution)/shard_map/ppermute | solution.py:358
  45.7 19.3 %copy-start = (bf16[4,4,256,256]{3,2,1,0:T(8,128)(2,1)S(1)}, bf16[4,4,256,256]{3,2,1,0:T(8,128)(2,1)}, u32[]{:S(2)}) copy-start(bf16[4,4,256,256]{3,2,1,0:T(8,128)(2,1)} %d_ref.7) | copy-start | bytes 6291460
  111.4 28.1 %copy-start.1 = (f32[4,4,32,256]{3,2,1,0:T(8,128)S(1)}, f32[4,4,32,256]{3,2,1,0:T(8,128)}, u32[]{:S(2)}) copy-start(f32[4,4,32,256]{3,2,1,0:T(8,128)} %param.12) | copy-start | bytes 1572868
  130.3 5.4 %collective-permute-start.17 = (bf16[8,16,256]{2,1,0:T(8,128)(2,1)S(1)}, bf16[8,16,256]{2,1,0:T(8,128)(2,1)S(1)}, u32[]{:S(2)}, u32[]{:S(2)}) collective-permute-start(bf16[8,16,256]{2,1,0:T(8,128)(2,1)S(1)} %all_to_all.47), channel_id=1, source_target_pairs={{0,24},{8,0},{16,8},{24,16},{1,25},{9,1},{17,9},{25,17},{2,26},{10... | collective-permute-start | bytes 196616 | tf_op jit(solution)/shard_map/ppermute | solution.py:440
  133.2 5.9 %collective-permute-start.18 = (bf16[8,16,256]{2,1,0:T(8,128)(2,1)S(1)}, bf16[8,16,256]{2,1,0:T(8,128)(2,1)S(1)}, u32[]{:S(2)}, u32[]{:S(2)}) collective-permute-start(bf16[8,16,256]{2,1,0:T(8,128)(2,1)S(1)} %all_to_all.47), channel_id=1, source_target_pairs={{0,16},{8,24},{16,0},{24,8},{1,17},{9,25},{17,1},{25,9},{2,18},{10... | collective-permute-start | bytes 196616 | tf_op jit(solution)/shard_map/ppermute | solution.py:440
  133.2 6.2 %collective-permute-start.19 = (bf16[8,16,256]{2,1,0:T(8,128)(2,1)S(1)}, bf16[8,16,256]{2,1,0:T(8,128)(2,1)S(1)}, u32[]{:S(2)}, u32[]{:S(2)}) collective-permute-start(bf16[8,16,256]{2,1,0:T(8,128)(2,1)S(1)} %all_to_all.47), channel_id=1, source_target_pairs={{0,8},{8,16},{16,24},{24,0},{1,9},{9,17},{17,25},{25,1},{2,10},{10... | collective-permute-start | bytes 196616 | tf_op jit(solution)/shard_map/ppermute | solution.py:440

commit v5 on v3

--- a/solution.py
+++ b/solution.py
@@ -126,17 +126,13 @@
 
 
 def pick_kernel(mine, y_ref, *refs):
-    own_hbm, recvs, outs, (own, data, pick, sem) = refs[0], refs[1:OWNERS], refs[OWNERS:-4], refs[-4:]
-    copy = pltpu.make_async_copy(own_hbm, own, sem)
-    copy.start()
-    blocks, size, T = own.shape
+    recvs, outs, (data, pick) = refs[:OWNERS], refs[OWNERS:-2], refs[-2:]
+    blocks, size, T = recvs[0].shape
     rows = (blocks - 1) * size
     K = rows // CAP
     lane = lax.broadcasted_iota(jnp.int32, (1, 128), 1)
     marks, codes = [], []
-    for i, ref in enumerate((*recvs, own)):
-        if i == len(recvs):
-            copy.wait()
+    for i, ref in enumerate(recvs):
         data[i * rows : (i + 1) * rows, :] = ref[: blocks - 1].reshape(rows, T)
         note = ref[blocks - 1].astype(F32)
         marks += [note[j : j + 1, :128] for j in range(CAP)]
@@ -305,7 +301,8 @@
         out_shape=(
             jax.ShapeDtypeStruct((row_tiles, K, T), F32),
         )
-        + (pltpu.HBM((slot_rows // 16, 16, T), BF16),) * OWNERS,
+        + (jax.ShapeDtypeStruct((slot_rows // 16, 16, T), BF16),)
+        + (pltpu.HBM((slot_rows // 16, 16, T), BF16),) * (OWNERS - 1),
         in_specs=[SMEM, SMEM, ANY, ANY, VMEM] + [ANY] * len(blocks),
         out_specs=(VMEM,) * (1 + OWNERS),
         scratch_shapes=[
@@ -327,7 +324,9 @@
     first_send, coupling_source = lax.optimization_barrier((send[0], coupling_source))
     source = coupling_source.reshape(levels - 1, -1)
     block_rows = 8
-    spot_at = source // sn * block_rows + source % sn
+    owner = source // sn % OWNERS
+    block = source // width * OWNERS + owner % CORE * X + owner // CORE
+    spot_at = block * block_rows + source % sn
     n_terms = source.shape[1]
     pad_terms = -n_terms % 16
     spot_at = jnp.pad(spot_at, ((0, 0), (0, pad_terms)), constant_values=-1)
@@ -350,17 +349,15 @@
     part = pl.pallas_call(
         functools.partial(pick_kernel, mine),
         out_shape=(jax.ShapeDtypeStruct((Z * mine, T), BF16),) * Y,
-        in_specs=[SMEM, ANY] + [VMEM] * (OWNERS - 1),
+        in_specs=[SMEM] + [VMEM] * OWNERS,
         out_specs=(VMEM,) * Y,
         scratch_shapes=[
-            pltpu.VMEM((slot_rows // 16, 16, T), BF16),
             pltpu.VMEM((OWNERS * CAP * K, T), BF16),
             pltpu.VMEM((Z * mine, OWNERS * CAP * K), BF16),
-            pltpu.SemaphoreType.DMA(()),
         ],
         compiler_params=PARAMS,
         name="pick",
-    )(y.reshape(1), in_hbm(recv[0]), *recv[1:])
+    )(y.reshape(1), *recv)
     total = part[0].astype(F32)
     arrived = [lax.ppermute(part[s], "y", shift(Y, s)) for s in (2, 1, 3)]
     (c_near,) = bring_near(part[0], coupling)
@@ -392,7 +389,7 @@
     )(parts, diag_inverse)
     known, solved = [], [value]
     for level in range(1, levels):
-        known.append(lax.all_to_all(out, snode, 0, 0, tiled=True))
+        known.append(lax.all_to_all(out, ("core", "x"), 0, 0, tiled=True))
         if level < levels - 1:
             value, out = pl.pallas_call(
                 functools.partial(forward_kernel, level, sn),
@@ -418,7 +415,7 @@
             )(g, look[level - 1], scatter[level - 1], *known, c_near, diag_inverse)
     changes = [change]
     for level in reversed(range(levels - 1)):
-        arrived = lax.all_to_all(out, snode, 0, 0, tiled=True)
+        arrived = lax.all_to_all(out, ("core", "x"), 0, 0, tiled=True)
         if level > 0:
             out_shape = (row4, by_owner) + rest_of(level)
             change, out, *rest = pl.pallas_call(

time: 139 us -> 138 us (level)
  no operation moved by 1% of the time
where the time goes in v5:
time: 138 us; the launch traced here: 137 us
  blocking collectives  74.5 us (54%)
  starting transfers between devices  22.1 us (16%)
  waiting for transfers between devices  19.4 us (14%)
  Pallas kernels  17.6 us (13%)
  other arithmetic  1.45 us (1%)
    all_to_all x3, blocking collectives, local(): known.append(lax.all_to_all(out, ('core', 'x'), 0, 0, tiled=True))  23.9 us
    all_to_all x3, blocking collectives, local(): arrived = lax.all_to_all(out, ('core', 'x'), 0, 0, tiled=True)  23.2 us
    all_to_all x1, blocking collectives, local(): lax.all_to_all(total.astype(BF16).reshape(Z, mine, T), 'z', 0, 0, tiled=T...  16.6 us
    all_to_all x1, blocking collectives, local(): column = lax.all_to_all(change, 'z', 0, 0, tiled=True)  10.8 us
    ppermute x7, starting transfers between devices, local(): recv.append(lax.ppermute(send[away], snode, perm))  8.43 us
    ppermute x7, waiting for transfers between devices, local(): recv.append(lax.ppermute(send[away], snode, perm))  6.29 us
    ppermute x3, waiting for transfers between devices, along(): return lax.ppermute(block, snode, perm)  5.92 us
    ppermute x3, waiting for transfers between devices, local(): lax.ppermute(column, 'y', shift(Y, -s % Y))  5.24 us
  transfers between devices with their start and end apart: 20, of which 11 were waited for; matrix products, arithmetic and copies ran while one was open for 0% of the time, Pallas kernels for 5%

profile of v5, /device:TPU:2, one launch (start us, length us, event | category | flops | bytes accessed | tf_op | source)
XLA Modules:
  0.0 137.3 jit_solution(1461235990293668757)
XLA Ops:
  1.8 1.6 %collective-permute-start.2 = (bf16[16,32,256]{2,1,0:T(8,128)(2,1)S(1)}, bf16[16,32,256]{2,1,0:T(8,128)(2,1)}, u32[]{:S(2)}, u32[]{:S(2)}) collective-permute-start(bf16[16,32,256]{2,1,0:T(8,128)(2,1)S(1)} %bitcast.18), channel_id=1, source_target_pairs={{0,2},{1,7},{2,4},{3,1},{4,6},{5,3},{6,0},{7,5},{8,10},{9,15},{10,... | collective-permute-start | bytes 786440 | tf_op jit(solution)/shard_map/ppermute | solution.py:272
  3.5 1.5 %collective-permute-start.1 = (bf16[16,32,256]{2,1,0:T(8,128)(2,1)}, bf16[16,32,256]{2,1,0:T(8,128)(2,1)}, u32[]{:S(2)}, u32[]{:S(2)}) collective-permute-start(bf16[16,32,256]{2,1,0:T(8,128)(2,1)} %collective-permute-done.refs_1_), channel_id=1, source_target_pairs={{0,2},{1,7},{2,4},{3,1},{4,6},{5,3},{6,0},{7,5},{8,10},{9,15},{10,... | collective-permute-start | bytes 786440 | tf_op jit(solution)/shard_map/ppermute | solution.py:272
  5.0 3.7 %collective-permute-done.2.refs_4_ = bf16[16,32,256]{2,1,0:T(8,128)(2,1)} collective-permute-done((bf16[16,32,256]{2,1,0:T(8,128)(2,1)S(1)}, bf16[16,32,256]{2,1,0:T(8,128)(2,1)}, u32[]{:S(2)}, u32[]{:S(2)}) %collective-permute-start.2) | collective-permute-done | bytes 262176 | tf_op jit(solution)/shard_map/ppermute | solution.py:272
  8.6 1.2 collective-permute-start.3
  9.9 1.9 %bring_near.2.a_ref = bf16[24,256,256]{2,1,0:T(8,128)(2,1)S(1)} custom-call(bf16[24,256,256]{2,1,0:T(8,128)(2,1)} %refs_0_.2), custom_call_target="tpu_custom_call" | custom-call | tf_op jit(solution)/shard_map/bring_near/pallas_call | solution.py:117
  11.8 1.9 %plan.1 = (s32[5,24]{1,0:T(8,128)S(1)}, bf16[8,16,256]{2,1,0:T(8,128)(2,1)}) custom-call(s32[1]{0:T(128)} %bitcast.2.here_ref, s32[24]{0:T(128)} %col_ref.1, s32[24]{0:T(128)} %row_ref.1), custom_call_target="tpu_custom_call" | custom-call | tf_op jit(solution)/shard_map/plan/pallas_call | solution.py:278
  14.3 2.3 %collective-permute-done.3.refs_2_ = bf16[16,32,256]{2,1,0:T(8,128)(2,1)} collective-permute-done((bf16[16,32,256]{2,1,0:T(8,128)(2,1)}, bf16[16,32,256]{2,1,0:T(8,128)(2,1)}, u32[]{:S(2)}, u32[]{:S(2)}) %collective-permute-start.3) | collective-permute-done | bytes 262176 | tf_op jit(solution)/shard_map/ppermute | solution.py:272
  16.6 1.8 %collective-permute-done.4.refs_3_ = bf16[16,32,256]{2,1,0:T(8,128)(2,1)} collective-permute-done((bf16[16,32,256]{2,1,0:T(8,128)(2,1)}, bf16[16,32,256]{2,1,0:T(8,128)(2,1)}, u32[]{:S(2)}, u32[]{:S(2)}) %collective-permute-start.4) | collective-permute-done | bytes 262176 | tf_op jit(solution)/shard_map/ppermute | solution.py:295
  18.4 4.8 %tile_products.1 = (f32[8,32,256]{2,1,0:T(8,128)}, bf16[13,16,256]{2,1,0:T(8,128)(2,1)S(1)}, bf16[13,16,256]{2,1,0:T(8,128)(2,1)}, bf16[13,16,256]{2,1,0:T(8,128...) custom-call(s32[1]{0:T(128)} %bitcast.core_ref, ...), custom_call_target="tpu_custom_call" | custom-call | tf_op jit(solution)/shard_map/tile_products/pallas_call | solution.py:299
  23.5 2.1 %collective-permute-start.10 = (bf16[13,16,256]{2,1,0:T(8,128)(2,1)}, bf16[13,16,256]{2,1,0:T(8,128)(2,1)S(1)}, u32[]{:S(2)}, u32[]{:S(2)}) collective-permute-start(bf16[13,16,256]{2,1,0:T(8,128)(2,1)} %get-tuple-element.71), channel_id=1, source_target_pairs={{0,4},{1,5},{2,6},{3,7},{4,0},{5,1},{6,2},{7,3},{8,12},{9,13},{10,... | collective-permute-start | bytes 319496 | tf_op jit(solution)/shard_map/ppermute | solution.py:347
  26.7 3.2 %collective-permute-start.12 = (bf16[13,16,256]{2,1,0:T(8,128)(2,1)}, bf16[13,16,256]{2,1,0:T(8,128)(2,1)S(1)}, u32[]{:S(2)}, u32[]{:S(2)}) collective-permute-start(bf16[13,16,256]{2,1,0:T(8,128)(2,1)} %get-tuple-element.73), channel_id=1, source_target_pairs={{0,6},{1,7},{2,0},{3,1},{4,2},{5,3},{6,4},{7,5},{8,14},{9,15},{10,... | collective-permute-start | bytes 319496 | tf_op jit(solution)/shard_map/ppermute | solution.py:347
  30.2 1.4 %collective-permute-start.7 = (bf16[13,16,256]{2,1,0:T(8,128)(2,1)}, bf16[13,16,256]{2,1,0:T(8,128)(2,1)S(1)}, u32[]{:S(2)}, u32[]{:S(2)}) collective-permute-start(bf16[13,16,256]{2,1,0:T(8,128)(2,1)} %get-tuple-element.68), channel_id=1, source_target_pairs={{0,3},{1,2},{2,5},{3,4},{4,7},{5,6},{6,1},{7,0},{8,11},{9,10},{10,... | collective-permute-start | bytes 319496 | tf_op jit(solution)/shard_map/ppermute | solution.py:347
  32.8 2.1 %collective-permute-done.12.refs_6_ = bf16[13,16,256]{2,1,0:T(8,128)(2,1)S(1)} collective-permute-done((bf16[13,16,256]{2,1,0:T(8,128)(2,1)}, bf16[13,16,256]{2,1,0:T(8,128)(2,1)S(1)}, u32[]{:S(2)}, u32[]{:S(2)}) %collective-permute-start.12) | collective-permute-done | bytes 106528 | tf_op jit(solution)/shard_map/ppermute | solution.py:347
  34.9 2.2 %collective-permute-done.13.refs_7_ = bf16[13,16,256]{2,1,0:T(8,128)(2,1)S(1)} collective-permute-done((bf16[13,16,256]{2,1,0:T(8,128)(2,1)}, bf16[13,16,256]{2,1,0:T(8,128)(2,1)S(1)}, u32[]{:S(2)}, u32[]{:S(2)}) %collective-permute-start.13) | collective-permute-done | bytes 106528 | tf_op jit(solution)/shard_map/ppermute | solution.py:347
  37.1 1.2 collective-permute-done.8.refs_2_
  39.0 1.7 %collective-permute-start.14 = (bf16[128,256]{1,0:T(8,128)(2,1)S(1)}, bf16[128,256]{1,0:T(8,128)(2,1)S(1)}, u32[]{:S(2)}, u32[]{:S(2)}) collective-permute-start(bf16[128,256]{1,0:T(8,128)(2,1)S(1)} %get-tuple-element.87), channel_id=1, source_target_pairs={{0,16},{8,24},{16,0},{24,8},{1,17},{9,25},{17,1},{25,9},{2,18},{10... | collective-permute-start | bytes 196616 | tf_op jit(solution)/shard_map/ppermute | solution.py:362
  41.4 2.6 %collective-permute-start.16 = (bf16[128,256]{1,0:T(8,128)(2,1)S(1)}, bf16[128,256]{1,0:T(8,128)(2,1)S(1)}, u32[]{:S(2)}, u32[]{:S(2)}) collective-permute-start(bf16[128,256]{1,0:T(8,128)(2,1)S(1)} %get-tuple-element.89), channel_id=1, source_target_pairs={{0,24},{8,0},{16,8},{24,16},{1,25},{9,1},{17,9},{25,17},{2,26},{10... | collective-permute-start | bytes 196616 | tf_op jit(solution)/shard_map/ppermute | solution.py:362
  43.9 2.5 %bring_near.3.refs_1_.refs_2_.refs_3_.c_ref = bf16[3,4,3,256,256]{4,3,2,1,0:T(8,128)(2,1)S(1)} custom-call(bf16[3,4,3,256,256]{4,3,2,1,0:T(8,128)(2,1)} %refs_0_.3, bf16[128,256]{1,0:T(8,128)(2,1)S(1)} %get-tuple-element.86.refs_1_), custom_call_target="tpu_custom_call" | custom-call | tf_op jit(solution)/shard_map/bring_near/pallas_call | solution.py:117
  46.5 16.6 %all_to_all.40.parts_ref = bf16[8,16,256]{2,1,0:T(8,128)(2,1)S(1)} all-to-all(bf16[8,16,256]{2,1,0:T(8,128)(2,1)S(1)} %bitcast.21), channel_id=1, replica_groups=mesh['z'=8,'y'=4,'x'=4,'core'=2] {'z'}, dimensions={0} | all-to-all | bytes 131072 | tf_op jit(solution)/shard_map/all_to_all | solution.py:367
  63.4 8.5 %all_to_all.41.refs_0_ = bf16[8,8,256]{2,1,0:T(8,128)(2,1)S(1)} all-to-all(bf16[8,8,256]{2,1,0:T(8,128)(2,1)S(1)} %get-tuple-element.96), channel_id=1, replica_groups=mesh['z'=8,'y'=4,'x'=4,'core'=2] {'core','x'}, dimensions={0} | all-to-all | bytes 65536 | tf_op jit(solution)/shard_map/all_to_all | solution.py:392
  72.8 7.7 %all_to_all.42.refs_1_ = bf16[8,8,256]{2,1,0:T(8,128)(2,1)S(1)} all-to-all(bf16[8,8,256]{2,1,0:T(8,128)(2,1)S(1)} %get-tuple-element.100), channel_id=1, replica_groups=mesh['z'=8,'y'=4,'x'=4,'core'=2] {'core','x'}, dimensions={0} | all-to-all | bytes 65536 | tf_op jit(solution)/shard_map/all_to_all | solution.py:392
  81.3 7.7 %all_to_all.43.refs_2_ = bf16[8,8,256]{2,1,0:T(8,128)(2,1)S(1)} all-to-all(bf16[8,8,256]{2,1,0:T(8,128)(2,1)S(1)} %get-tuple-element.104), channel_id=1, replica_groups=mesh['z'=8,'y'=4,'x'=4,'core'=2] {'core','x'}, dimensions={0} | all-to-all | bytes 65536 | tf_op jit(solution)/shard_map/all_to_all | solution.py:392
  89.0 1.6 %turn.1 = (f32[4,256]{1,0:T(4,128)S(1)}, bf16[8,8,256]{2,1,0:T(8,128)(2,1)S(1)}, f32[128,256]{1,0:T(8,128)S(1)}) custom-call(f32[16,256]{1,0:T(8,128)S(1)} %get-tuple-element.94.g_ref, bf16[16,192]{1,0:T(8,128)(2,1)S(1)} %fusion.6.look_ref, bf16[192,16]{1,0:T(8,128)(2,1)S(1)} %fusion.3.scatter_ref, bf16[8,8,256]{2,1,0:T(8,128)(2,1)S(1)} %all_to_all.41.refs_0_, ...), custom_call_target="tpu_custom_call" | custom-call | tf_op jit(solution)/shard_map/turn/pallas_call | solution.py:406
  90.6 7.7 %all_to_all.44.recv_ref = bf16[8,8,256]{2,1,0:T(8,128)(2,1)S(1)} all-to-all(bf16[8,8,256]{2,1,0:T(8,128)(2,1)S(1)} %get-tuple-element.105), channel_id=1, replica_groups=mesh['z'=8,'y'=4,'x'=4,'core'=2] {'core','x'}, dimensions={0} | all-to-all | bytes 65536 | tf_op jit(solution)/shard_map/all_to_all | solution.py:418
  98.3 1.1 backward_2.1
  99.4 7.7 %all_to_all.45.recv_ref = bf16[8,8,256]{2,1,0:T(8,128)(2,1)S(1)} all-to-all(bf16[8,8,256]{2,1,0:T(8,128)(2,1)S(1)} %get-tuple-element.108), channel_id=1, replica_groups=mesh['z'=8,'y'=4,'x'=4,'core'=2] {'core','x'}, dimensions={0} | all-to-all | bytes 65536 | tf_op jit(solution)/shard_map/all_to_all | solution.py:418
  108.2 7.8 %all_to_all.46.recv_ref = bf16[8,8,256]{2,1,0:T(8,128)(2,1)S(1)} all-to-all(bf16[8,8,256]{2,1,0:T(8,128)(2,1)S(1)} %get-tuple-element.111), channel_id=1, replica_groups=mesh['z'=8,'y'=4,'x'=4,'core'=2] {'core','x'}, dimensions={0} | all-to-all | bytes 65536 | tf_op jit(solution)/shard_map/all_to_all | solution.py:418
  116.2 10.8 %all_to_all.47 = bf16[8,16,256]{2,1,0:T(8,128)(2,1)S(1)} all-to-all(bf16[8,16,256]{2,1,0:T(8,128)(2,1)S(1)} %backward_0.1), channel_id=1, replica_groups=mesh['z'=8,'y'=4,'x'=4,'core'=2] {'z'}, dimensions={0} | all-to-all | bytes 131072 | tf_op jit(solution)/shard_map/all_to_all | solution.py:443
  127.0 2.9 %collective-permute-start.17 = (bf16[8,16,256]{2,1,0:T(8,128)(2,1)S(1)}, bf16[8,16,256]{2,1,0:T(8,128)(2,1)S(1)}, u32[]{:S(2)}, u32[]{:S(2)}) collective-permute-start(bf16[8,16,256]{2,1,0:T(8,128)(2,1)S(1)} %all_to_all.47), channel_id=1, source_target_pairs={{0,24},{8,0},{16,8},{24,16},{1,25},{9,1},{17,9},{25,17},{2,26},{10... | collective-permute-start | bytes 196616 | tf_op jit(solution)/shard_map/ppermute | solution.py:444
  130.9 1.6 %collective-permute-done.17 = bf16[8,16,256]{2,1,0:T(8,128)(2,1)S(1)} collective-permute-done((bf16[8,16,256]{2,1,0:T(8,128)(2,1)S(1)}, bf16[8,16,256]{2,1,0:T(8,128)(2,1)S(1)}, u32[]{:S(2)}, u32[]{:S(2)}) %collective-permute-start.17) | collective-permute-done | bytes 65568 | tf_op jit(solution)/shard_map/ppermute | solution.py:444
  132.4 3.4 %collective-permute-done.18 = bf16[8,16,256]{2,1,0:T(8,128)(2,1)S(1)} collective-permute-done((bf16[8,16,256]{2,1,0:T(8,128)(2,1)S(1)}, bf16[8,16,256]{2,1,0:T(8,128)(2,1)S(1)}, u32[]{:S(2)}, u32[]{:S(2)}) %collective-permute-start.18) | collective-permute-done | bytes 65568 | tf_op jit(solution)/shard_map/ppermute | solution.py:444
  136.1 1.2 convolution_add_fusion
  (50 shorter events, 10.4 us)
Async XLA Ops:
  1.7 1.8 %collective-permute-start = (bf16[16,32,256]{2,1,0:T(8,128)(2,1)S(1)}, bf16[16,32,256]{2,1,0:T(8,128)(2,1)}, u32[]{:S(2)}, u32[]{:S(2)}) collective-permute-start(bf16[16,32,256]{2,1,0:T(8,128)(2,1)S(1)} %bitcast.17), channel_id=1, source_target_pairs={{0,1},{1,0},{2,3},{3,2},{4,5},{5,4},{6,7},{7,6},{8,9},{9,8},{10,11... | collective-permute-start | bytes 786440 | tf_op jit(solution)/shard_map/ppermute | solution.py:275
  1.8 6.8 %collective-permute-start.2 = (bf16[16,32,256]{2,1,0:T(8,128)(2,1)S(1)}, bf16[16,32,256]{2,1,0:T(8,128)(2,1)}, u32[]{:S(2)}, u32[]{:S(2)}) collective-permute-start(bf16[16,32,256]{2,1,0:T(8,128)(2,1)S(1)} %bitcast.18), channel_id=1, source_target_pairs={{0,2},{1,7},{2,4},{3,1},{4,6},{5,3},{6,0},{7,5},{8,10},{9,15},{10,... | collective-permute-start | bytes 786440 | tf_op jit(solution)/shard_map/ppermute | solution.py:272
  3.5 10.3 %collective-permute-start.1 = (bf16[16,32,256]{2,1,0:T(8,128)(2,1)}, bf16[16,32,256]{2,1,0:T(8,128)(2,1)}, u32[]{:S(2)}, u32[]{:S(2)}) collective-permute-start(bf16[16,32,256]{2,1,0:T(8,128)(2,1)} %collective-permute-done.refs_1_), channel_id=1, source_target_pairs={{0,2},{1,7},{2,4},{3,1},{4,6},{5,3},{6,0},{7,5},{8,10},{9,15},{10,... | collective-permute-start | bytes 786440 | tf_op jit(solution)/shard_map/ppermute | solution.py:272
  8.6 7.9 %collective-permute-start.3 = (bf16[16,32,256]{2,1,0:T(8,128)(2,1)}, bf16[16,32,256]{2,1,0:T(8,128)(2,1)}, u32[]{:S(2)}, u32[]{:S(2)}) collective-permute-start(bf16[16,32,256]{2,1,0:T(8,128)(2,1)} %collective-permute-done.2.refs_4_), channel_id=1, source_target_pairs={{0,2},{1,7},{2,4},{3,1},{4,6},{5,3},{6,0},{7,5},{8,10},{9,15},{10,... | collective-permute-start | bytes 786440 | tf_op jit(solution)/shard_map/ppermute | solution.py:272
  11.7 11.5 %copy-start.2 = (s32[3,4,3]{2,1,0:T(4,128)S(1)}, s32[3,4,3]{2,1,0:T(4,128)}, u32[]{:S(2)}) copy-start(s32[3,4,3]{2,1,0:T(4,128)} %param.15) | copy-start | bytes 436
  13.7 2.9 %collective-permute-start.6 = (bf16[16,32,256]{2,1,0:T(8,128)(2,1)}, bf16[16,32,256]{2,1,0:T(8,128)(2,1)}, u32[]{:S(2)}, u32[]{:S(2)}) collective-permute-start(bf16[16,32,256]{2,1,0:T(8,128)(2,1)} %collective-permute-done.2.refs_4_), channel_id=1, source_target_pairs={{0,1},{1,0},{2,3},{3,2},{4,5},{5,4},{6,7},{7,6},{8,9},{9,8},{10,11... | collective-permute-start | bytes 786440 | tf_op jit(solution)/shard_map/ppermute | solution.py:291
  13.8 2.7 %collective-permute-start.5 = (bf16[16,32,256]{2,1,0:T(8,128)(2,1)}, bf16[16,32,256]{2,1,0:T(8,128)(2,1)}, u32[]{:S(2)}, u32[]{:S(2)}) collective-permute-start(bf16[16,32,256]{2,1,0:T(8,128)(2,1)} %collective-permute-done.1.refs_5_), channel_id=1, source_target_pairs={{0,1},{1,0},{2,3},{3,2},{4,5},{5,4},{6,7},{7,6},{8,9},{9,8},{10,11... | collective-permute-start | bytes 786440 | tf_op jit(solution)/shard_map/ppermute | solution.py:295
  16.5 1.9 %collective-permute-start.4 = (bf16[16,32,256]{2,1,0:T(8,128)(2,1)}, bf16[16,32,256]{2,1,0:T(8,128)(2,1)}, u32[]{:S(2)}, u32[]{:S(2)}) collective-permute-start(bf16[16,32,256]{2,1,0:T(8,128)(2,1)} %collective-permute-done.3.refs_2_), channel_id=1, source_target_pairs={{0,1},{1,0},{2,3},{3,2},{4,5},{5,4},{6,7},{7,6},{8,9},{9,8},{10,11... | collective-permute-start | bytes 786440 | tf_op jit(solution)/shard_map/ppermute | solution.py:295
  23.5 8.2 %collective-permute-start.10 = (bf16[13,16,256]{2,1,0:T(8,128)(2,1)}, bf16[13,16,256]{2,1,0:T(8,128)(2,1)S(1)}, u32[]{:S(2)}, u32[]{:S(2)}) collective-permute-start(bf16[13,16,256]{2,1,0:T(8,128)(2,1)} %get-tuple-element.71), channel_id=1, source_target_pairs={{0,4},{1,5},{2,6},{3,7},{4,0},{5,1},{6,2},{7,3},{8,12},{9,13},{10,... | collective-permute-start | bytes 319496 | tf_op jit(solution)/shard_map/ppermute | solution.py:347
  25.6 7.0 %collective-permute-start.11 = (bf16[13,16,256]{2,1,0:T(8,128)(2,1)}, bf16[13,16,256]{2,1,0:T(8,128)(2,1)S(1)}, u32[]{:S(2)}, u32[]{:S(2)}) collective-permute-start(bf16[13,16,256]{2,1,0:T(8,128)(2,1)} %get-tuple-element.72), channel_id=1, source_target_pairs={{0,5},{1,4},{2,7},{3,6},{4,1},{5,0},{6,3},{7,2},{8,13},{9,12},{10,... | collective-permute-start | bytes 319496 | tf_op jit(solution)/shard_map/ppermute | solution.py:347
  26.7 8.2 %collective-permute-start.12 = (bf16[13,16,256]{2,1,0:T(8,128)(2,1)}, bf16[13,16,256]{2,1,0:T(8,128)(2,1)S(1)}, u32[]{:S(2)}, u32[]{:S(2)}) collective-permute-start(bf16[13,16,256]{2,1,0:T(8,128)(2,1)} %get-tuple-element.73), channel_id=1, source_target_pairs={{0,6},{1,7},{2,0},{3,1},{4,2},{5,3},{6,4},{7,5},{8,14},{9,15},{10,... | collective-permute-start | bytes 319496 | tf_op jit(solution)/shard_map/ppermute | solution.py:347
  29.9 7.2 %collective-permute-start.13 = (bf16[13,16,256]{2,1,0:T(8,128)(2,1)}, bf16[13,16,256]{2,1,0:T(8,128)(2,1)S(1)}, u32[]{:S(2)}, u32[]{:S(2)}) collective-permute-start(bf16[13,16,256]{2,1,0:T(8,128)(2,1)} %get-tuple-element.74), channel_id=1, source_target_pairs={{0,7},{1,6},{2,1},{3,0},{4,3},{5,2},{6,5},{7,4},{8,15},{9,14},{10,... | collective-permute-start | bytes 319496 | tf_op jit(solution)/shard_map/ppermute | solution.py:347
  30.2 6.9 %collective-permute-start.7 = (bf16[13,16,256]{2,1,0:T(8,128)(2,1)}, bf16[13,16,256]{2,1,0:T(8,128)(2,1)S(1)}, u32[]{:S(2)}, u32[]{:S(2)}) collective-permute-start(bf16[13,16,256]{2,1,0:T(8,128)(2,1)} %get-tuple-element.68), channel_id=1, source_target_pairs={{0,3},{1,2},{2,5},{3,4},{4,7},{5,6},{6,1},{7,0},{8,11},{9,10},{10,... | collective-permute-start | bytes 319496 | tf_op jit(solution)/shard_map/ppermute | solution.py:347
  31.7 6.7 %collective-permute-start.8 = (bf16[13,16,256]{2,1,0:T(8,128)(2,1)}, bf16[13,16,256]{2,1,0:T(8,128)(2,1)S(1)}, u32[]{:S(2)}, u32[]{:S(2)}) collective-permute-start(bf16[13,16,256]{2,1,0:T(8,128)(2,1)} %get-tuple-element.69), channel_id=1, source_target_pairs={{0,2},{1,3},{2,4},{3,5},{4,6},{5,7},{6,0},{7,1},{8,10},{9,11},{10,... | collective-permute-start | bytes 319496 | tf_op jit(solution)/shard_map/ppermute | solution.py:347
  32.6 5.7 %collective-permute-start.9 = (bf16[13,16,256]{2,1,0:T(8,128)(2,1)}, bf16[13,16,256]{2,1,0:T(8,128)(2,1)S(1)}, u32[]{:S(2)}, u32[]{:S(2)}) collective-permute-start(bf16[13,16,256]{2,1,0:T(8,128)(2,1)} %get-tuple-element.70), channel_id=1, source_target_pairs={{0,1},{1,0},{2,3},{3,2},{4,5},{5,4},{6,7},{7,6},{8,9},{9,8},{10,11... | collective-permute-start | bytes 319496 | tf_op jit(solution)/shard_map/ppermute | solution.py:347
  39.0 7.5 %collective-permute-start.14 = (bf16[128,256]{1,0:T(8,128)(2,1)S(1)}, bf16[128,256]{1,0:T(8,128)(2,1)S(1)}, u32[]{:S(2)}, u32[]{:S(2)}) collective-permute-start(bf16[128,256]{1,0:T(8,128)(2,1)S(1)} %get-tuple-element.87), channel_id=1, source_target_pairs={{0,16},{8,24},{16,0},{24,8},{1,17},{9,25},{17,1},{25,9},{2,18},{10... | collective-permute-start | bytes 196616 | tf_op jit(solution)/shard_map/ppermute | solution.py:362
  40.7 5.8 %collective-permute-start.15 = (bf16[128,256]{1,0:T(8,128)(2,1)S(1)}, bf16[128,256]{1,0:T(8,128)(2,1)S(1)}, u32[]{:S(2)}, u32[]{:S(2)}) collective-permute-start(bf16[128,256]{1,0:T(8,128)(2,1)S(1)} %get-tuple-element.88), channel_id=1, source_target_pairs={{0,8},{8,16},{16,24},{24,0},{1,9},{9,17},{17,25},{25,1},{2,10},{10... | collective-permute-start | bytes 196616 | tf_op jit(solution)/shard_map/ppermute | solution.py:362
  41.4 5.1 %collective-permute-start.16 = (bf16[128,256]{1,0:T(8,128)(2,1)S(1)}, bf16[128,256]{1,0:T(8,128)(2,1)S(1)}, u32[]{:S(2)}, u32[]{:S(2)}) collective-permute-start(bf16[128,256]{1,0:T(8,128)(2,1)S(1)} %get-tuple-element.89), channel_id=1, source_target_pairs={{0,24},{8,0},{16,8},{24,16},{1,25},{9,1},{17,9},{25,17},{2,26},{10... | collective-permute-start | bytes 196616 | tf_op jit(solution)/shard_map/ppermute | solution.py:362
  43.9 19.3 %copy-start = (bf16[4,4,256,256]{3,2,1,0:T(8,128)(2,1)S(1)}, bf16[4,4,256,256]{3,2,1,0:T(8,128)(2,1)}, u32[]{:S(2)}) copy-start(bf16[4,4,256,256]{3,2,1,0:T(8,128)(2,1)} %d_ref.7) | copy-start | bytes 6291460
  108.2 28.0 %copy-start.1 = (f32[4,4,32,256]{3,2,1,0:T(8,128)S(1)}, f32[4,4,32,256]{3,2,1,0:T(8,128)}, u32[]{:S(2)}) copy-start(f32[4,4,32,256]{3,2,1,0:T(8,128)} %param.12) | copy-start | bytes 1572868
  127.0 5.4 %collective-permute-start.17 = (bf16[8,16,256]{2,1,0:T(8,128)(2,1)S(1)}, bf16[8,16,256]{2,1,0:T(8,128)(2,1)S(1)}, u32[]{:S(2)}, u32[]{:S(2)}) collective-permute-start(bf16[8,16,256]{2,1,0:T(8,128)(2,1)S(1)} %all_to_all.47), channel_id=1, source_target_pairs={{0,24},{8,0},{16,8},{24,16},{1,25},{9,1},{17,9},{25,17},{2,26},{10... | collective-permute-start | bytes 196616 | tf_op jit(solution)/shard_map/ppermute | solution.py:444
  129.9 5.9 %collective-permute-start.18 = (bf16[8,16,256]{2,1,0:T(8,128)(2,1)S(1)}, bf16[8,16,256]{2,1,0:T(8,128)(2,1)S(1)}, u32[]{:S(2)}, u32[]{:S(2)}) collective-permute-start(bf16[8,16,256]{2,1,0:T(8,128)(2,1)S(1)} %all_to_all.47), channel_id=1, source_target_pairs={{0,16},{8,24},{16,0},{24,8},{1,17},{9,25},{17,1},{25,9},{2,18},{10... | collective-permute-start | bytes 196616 | tf_op jit(solution)/shard_map/ppermute | solution.py:444
  129.9 6.2 %collective-permute-start.19 = (bf16[8,16,256]{2,1,0:T(8,128)(2,1)S(1)}, bf16[8,16,256]{2,1,0:T(8,128)(2,1)S(1)}, u32[]{:S(2)}, u32[]{:S(2)}) collective-permute-start(bf16[8,16,256]{2,1,0:T(8,128)(2,1)S(1)} %all_to_all.47), channel_id=1, source_target_pairs={{0,8},{8,16},{16,24},{24,0},{1,9},{9,17},{17,25},{25,1},{2,10},{10... | collective-permute-start | bytes 196616 | tf_op jit(solution)/shard_map/ppermute | solution.py:444

commit v6 on v5

--- a/solution.py
+++ b/solution.py
@@ -10,6 +10,7 @@
 CAP = 6
 X, CORE, Y, Z = 4, 2, 4, 8
 OWNERS = X * CORE
+LAST = 2 * CORE + 1
 F32 = jnp.float32
 BF16 = jnp.bfloat16
 NT = (((1,), (1,)), ((), ()))
@@ -33,6 +34,8 @@
     note[...] = jnp.zeros_like(note)
     for o in range(OWNERS):
         count_ref[o] = 0
+    for i in range(CAP):
+        plan_ref[5, i] = -1
     for t in range(col_ref.shape[0]):
         c = col_ref[t]
         level, owner, inner = c // (sn * OWNERS), (c // sn) % OWNERS, c % sn
@@ -44,44 +47,69 @@
         plan_ref[2, t] = row_ref[t]
         plan_ref[3, t] = away
         plan_ref[4, t] = rank
+
+        @pl.when(away == LAST)
+        def _():
+            plan_ref[5, rank] = t
+
         mark = (level * sn + inner + 1).astype(F32)
         note[away, pl.ds(rank, 1), :] = jnp.full((1, note.shape[2]), mark, F32)
     note_ref[...] = note[...].astype(BF16)
 
 
-def tile_kernel(n_blocks, core_ref, plan_ref, note_ref, side_ref, a_ref, *refs):
+def first_tiles_kernel(n_blocks, core_ref, plan_ref, side_ref, a_ref, *refs):
     blocks = refs[:n_blocks]
     core = core_ref[0]
-    res_ref, out_refs = refs[n_blocks], refs[n_blocks + 1 : n_blocks + 1 + OWNERS]
-    send_ref, x_all, low_ref, sems, note_sems = refs[n_blocks + 1 + OWNERS :]
-    tiles = a_ref.shape[0]
+    res_ref, x_all, sems = refs[n_blocks:]
     mine = x_all.shape[0] // OWNERS
-    half = x_all.shape[1] // 2
-    per = send_ref.shape[0] // OWNERS
-    copies = [pltpu.make_async_copy(side_ref, res_ref, sems.at[len(blocks)])]
-    places = [0, 1, 4, 5] + [2 * X - 2 - 4 * core + i for i in range(2)] + [2 + 4 * core + i for i in range(2)]
+    own, rest = 2 * X - 2 - 4 * core, 2 + 4 * core
+    places = [0, 1, 4, own, own + 1, rest, rest + 1]
+    copies = [pltpu.make_async_copy(side_ref, res_ref, sems.at[n_blocks])]
     for i, block in enumerate(blocks):
-        target = x_all.at[pl.ds(places[i] * mine, mine)]
-        copies.append(pltpu.make_async_copy(block, target, sems.at[i]))
+        copies.append(pltpu.make_async_copy(block, x_all.at[pl.ds(places[i] * mine, mine)], sems.at[i]))
     for copy in copies:
         copy.start()
+    x_all[LAST * mine : (LAST + 1) * mine] = jnp.zeros((mine,) + x_all.shape[1:], BF16)
+    for copy in copies:
+        copy.wait()
+    for t in range(a_ref.shape[0]):
+        q = plan_ref[2, t]
+        res_ref[q] -= dot(x_all[plan_ref[0, t] * mine + plan_ref[1, t]], a_ref[t], NT)
+
+
+def last_tiles_kernel(plan_ref, note_ref, sum_ref, a_ref, block_ref, res_hbm, own_ref, *refs):
+    out_refs, (send_ref, x_last, res_ref, low_ref, sems, note_sems) = refs[: OWNERS - 1], refs[OWNERS - 1 :]
+    half = x_last.shape[1] // 2
+    per = own_ref.shape[0]
+    copies = [pltpu.make_async_copy(block_ref, x_last, sems.at[0])]
+    copies[0].start()
     send_ref[...] = jnp.zeros_like(send_ref)
     for o in range(OWNERS):
         copies.append(pltpu.make_async_copy(note_ref.at[o], send_ref.at[(o + 1) * per - 1], note_sems.at[o]))
         copies[-1].start()
+    res_ref[...] = sum_ref[...]
     for copy in copies:
         copy.wait()
-    for t in range(tiles):
+    for i in range(CAP):
+        t = jnp.maximum(plan_ref[5, i], 0)
+        there = (plan_ref[5, i] >= 0).astype(F32)
         q = plan_ref[2, t]
-        res_ref[q] -= dot(x_all[plan_ref[0, t] * mine + plan_ref[1, t]], a_ref[t], NT)
+        res_ref[q] -= there * dot(x_last[plan_ref[1, t]], a_ref[t], NT)
+    copies = [pltpu.make_async_copy(res_ref, res_hbm, sems.at[0])]
+    copies[0].start()
     low_ref[...] = res_ref[...].astype(BF16)
-    for t in range(tiles):
+    for t in range(a_ref.shape[0]):
         spot = plan_ref[3, t] * per + 2 * plan_ref[4, t]
         term = dot(low_ref[plan_ref[2, t]], a_ref[t], NN).astype(BF16)
         send_ref[spot] = term[:half]
         send_ref[spot + 1] = term[half:]
-    for o, ref in enumerate(out_refs):
-        ref[...] = send_ref[o * per : (o + 1) * per]
+    for i, ref in enumerate(out_refs):
+        piece = send_ref.at[pl.ds((i + 1) * per, per)]
+        copies.append(pltpu.make_async_copy(piece, ref, sems.at[i + 1]))
+        copies[-1].start()
+    own_ref[...] = send_ref[:per]
+    for copy in copies:
+        copy.wait()
 
 
 def in_hbm(x):
@@ -278,7 +306,7 @@
     plan, note = pl.pallas_call(
         functools.partial(plan_kernel, sn),
         out_shape=(
-            jax.ShapeDtypeStruct((5, tiles), jnp.int32),
+            jax.ShapeDtypeStruct((6, tiles), jnp.int32),
             pltpu.HBM((OWNERS, 16, T), BF16),
         ),
         in_specs=[SMEM, SMEM, SMEM],
@@ -293,28 +321,39 @@
     side = in_hbm(right_side)
     second, note, a_near = lax.optimization_barrier((second, note, a_near))
     cross_second, cross_third = other(second), other(third)
-    blocks = [e, swapped, third, cross_third, first, second, cross_second, cross_first]
+    blocks = [e, swapped, third, first, second, cross_second, cross_first]
 
     slot_rows = CAP * K + 16
+    part_sum = pl.pallas_call(
+        functools.partial(first_tiles_kernel, len(blocks)),
+        out_shape=jax.ShapeDtypeStruct((row_tiles, K, T), F32),
+        in_specs=[SMEM, SMEM, ANY, VMEM] + [ANY] * len(blocks),
+        out_specs=VMEM,
+        scratch_shapes=[pltpu.VMEM((OWNERS * mine, K, T), BF16), pltpu.SemaphoreType.DMA((len(blocks) + 1,))],
+        compiler_params=PARAMS,
+        name="first_tiles",
+    )(lax.axis_index("core").reshape(1), plan, side, a_near, *blocks)
+    slots = slot_rows // 16
     residual, *send = pl.pallas_call(
-        functools.partial(tile_kernel, len(blocks)),
+        last_tiles_kernel,
         out_shape=(
             jax.ShapeDtypeStruct((row_tiles, K, T), F32),
+            jax.ShapeDtypeStruct((slots, 16, T), BF16),
         )
-        + (jax.ShapeDtypeStruct((slot_rows // 16, 16, T), BF16),)
-        + (pltpu.HBM((slot_rows // 16, 16, T), BF16),) * (OWNERS - 1),
-        in_specs=[SMEM, SMEM, ANY, ANY, VMEM] + [ANY] * len(blocks),
-        out_specs=(VMEM,) * (1 + OWNERS),
+        + (pltpu.HBM((slots, 16, T), BF16),) * (OWNERS - 1),
+        in_specs=[SMEM, ANY, VMEM, VMEM, ANY],
+        out_specs=(ANY, VMEM) + (ANY,) * (OWNERS - 1),
         scratch_shapes=[
-            pltpu.VMEM((OWNERS * slot_rows // 16, 16, T), BF16),
-            pltpu.VMEM((OWNERS * mine, K, T), BF16),
+            pltpu.VMEM((OWNERS * slots, 16, T), BF16),
+            pltpu.VMEM((mine, K, T), BF16),
+            pltpu.VMEM((row_tiles, K, T), F32),
             pltpu.VMEM((row_tiles, K, T), BF16),
-            pltpu.SemaphoreType.DMA((len(blocks) + 1,)),
+            pltpu.SemaphoreType.DMA((OWNERS,)),
             pltpu.SemaphoreType.DMA((OWNERS,)),
         ],
         compiler_params=PARAMS,
-        name="tile_products",
-    )(lax.axis_index("core").reshape(1), plan, in_hbm(note), side, a_near, *blocks)
+        name="last_tiles",
+    )(plan, in_hbm(note), part_sum, a_near, cross_third)
 
     to = jnp.arange(mine * K)
     y = lax.axis_index("y")
@@ -338,7 +377,7 @@
     stage = pltpu.VMEM((n_terms + pad_terms, T), F32)
 
     recv = [first_send]
-    for away in (3, 2, 1, 4, 5, 6, 7):
+    for away in (4, 5, 6, 7, 3, 2, 1):
         step, swap = away // CORE, away % CORE
         perm = []
         for x in range(X):
@@ -441,7 +480,7 @@
                 name="backward_0",
             )(solved[0], arrived, *changes, diag_inverse)
     column = lax.all_to_all(change, "z", 0, 0, tiled=True)
-    far, ahead, behind = [lax.ppermute(column, "y", shift(Y, -s % Y)) for s in (2, 1, 3)]
+    behind, ahead, far = [lax.ppermute(column, "y", shift(Y, -s % Y)) for s in (3, 1, 2)]
     pieces = [column, ahead, far, behind]
     pieces = jnp.concatenate(pieces, axis=0).reshape(Y * Z * mine, T)
     sort = (to[:, None] == place[None, :]).astype(BF16)

time: 138 us -> 138 us (level)
  waiting for transfers between devices: 19.4 us -> 17 us
  Pallas kernels: 17.6 us -> 19.4 us
    pallas_call x1 -> x2, Pallas kernels: 4.83 us -> 6.71 us  [the longest x1 3.56 us: local(): pl.pallas_call(last_tiles_kernel, out_shape=(jax.ShapeDtypeStruct((row_ti...]
    ppermute x2, waiting for transfers between devices: 1.84 us -> 0.01 us  [local(): cross_second, cross_third = (other(second), other(third))]
  transfers between devices with their start and end apart: 20 -> 20, of which waited for: 11 -> 10; matrix products, arithmetic and copies ran while one was open for 0% -> 0% of each run, Pallas kernels for 5% -> 7%
where the time goes in v6:
time: 138 us; the launch traced here: 137 us
  blocking collectives  74.1 us (54%)
  starting transfers between devices  22.9 us (17%)
  Pallas kernels  19.4 us (14%)
  waiting for transfers between devices  17 us (12%)
  other arithmetic  1.45 us (1%)
    all_to_all x3, blocking collectives, local(): known.append(lax.all_to_all(out, ('core', 'x'), 0, 0, tiled=True))  23.5 us
    all_to_all x3, blocking collectives, local(): arrived = lax.all_to_all(out, ('core', 'x'), 0, 0, tiled=True)  23.2 us
    all_to_all x1, blocking collectives, local(): lax.all_to_all(total.astype(BF16).reshape(Z, mine, T), 'z', 0, 0, tiled=T...  16.6 us
    all_to_all x1, blocking collectives, local(): column = lax.all_to_all(change, 'z', 0, 0, tiled=True)  10.8 us
    ppermute x7, starting transfers between devices, local(): recv.append(lax.ppermute(send[away], snode, perm))  8.6 us
    ppermute x7, waiting for transfers between devices, local(): recv.append(lax.ppermute(send[away], snode, perm))  6.75 us
    ppermute x3, waiting for transfers between devices, along(): return lax.ppermute(block, snode, perm)  6 us
    ppermute x3, starting transfers between devices, local(): arrived = [lax.ppermute(part[s], 'y', shift(Y, s)) for s in (2, 1, 3)]  4.97 us
  transfers between devices with their start and end apart: 20, of which 10 were waited for; matrix products, arithmetic and copies ran while one was open for 0% of the time, Pallas kernels for 7%

profile of v6, /device:TPU:2, one launch (start us, length us, event | category | flops | bytes accessed | tf_op | source)
XLA Modules:
  0.0 137.1 jit_solution(150839329418746862)
XLA Ops:
  1.8 1.6 %collective-permute-start.2 = (bf16[16,32,256]{2,1,0:T(8,128)(2,1)S(1)}, bf16[16,32,256]{2,1,0:T(8,128)(2,1)}, u32[]{:S(2)}, u32[]{:S(2)}) collective-permute-start(bf16[16,32,256]{2,1,0:T(8,128)(2,1)S(1)} %bitcast.18), channel_id=1, source_target_pairs={{0,2},{1,7},{2,4},{3,1},{4,6},{5,3},{6,0},{7,5},{8,10},{9,15},{10,... | collective-permute-start | bytes 786440 | tf_op jit(solution)/shard_map/ppermute | solution.py:300
  3.5 1.5 %collective-permute-start.1 = (bf16[16,32,256]{2,1,0:T(8,128)(2,1)}, bf16[16,32,256]{2,1,0:T(8,128)(2,1)}, u32[]{:S(2)}, u32[]{:S(2)}) collective-permute-start(bf16[16,32,256]{2,1,0:T(8,128)(2,1)} %collective-permute-done.refs_1_), channel_id=1, source_target_pairs={{0,2},{1,7},{2,4},{3,1},{4,6},{5,3},{6,0},{7,5},{8,10},{9,15},{10,... | collective-permute-start | bytes 786440 | tf_op jit(solution)/shard_map/ppermute | solution.py:300
  5.0 3.7 %collective-permute-done.2.refs_3_ = bf16[16,32,256]{2,1,0:T(8,128)(2,1)} collective-permute-done((bf16[16,32,256]{2,1,0:T(8,128)(2,1)S(1)}, bf16[16,32,256]{2,1,0:T(8,128)(2,1)}, u32[]{:S(2)}, u32[]{:S(2)}) %collective-permute-start.2) | collective-permute-done | bytes 262176 | tf_op jit(solution)/shard_map/ppermute | solution.py:300
  8.6 1.2 collective-permute-start.3
  9.9 1.9 %bring_near.2.a_ref = bf16[24,256,256]{2,1,0:T(8,128)(2,1)S(1)} custom-call(bf16[24,256,256]{2,1,0:T(8,128)(2,1)} %refs_0_.2), custom_call_target="tpu_custom_call" | custom-call | tf_op jit(solution)/shard_map/bring_near/pallas_call | solution.py:145
  11.7 1.8 %plan.1 = (s32[6,24]{1,0:T(8,128)S(1)}, bf16[8,16,256]{2,1,0:T(8,128)(2,1)}) custom-call(s32[1]{0:T(128)} %bitcast.1.here_ref, s32[24]{0:T(128)} %col_ref.1, s32[24]{0:T(128)} %row_ref.1), custom_call_target="tpu_custom_call" | custom-call | tf_op jit(solution)/shard_map/plan/pallas_call | solution.py:306
  14.2 2.3 %collective-permute-done.3.refs_2_ = bf16[16,32,256]{2,1,0:T(8,128)(2,1)} collective-permute-done((bf16[16,32,256]{2,1,0:T(8,128)(2,1)}, bf16[16,32,256]{2,1,0:T(8,128)(2,1)}, u32[]{:S(2)}, u32[]{:S(2)}) %collective-permute-start.3) | collective-permute-done | bytes 262176 | tf_op jit(solution)/shard_map/ppermute | solution.py:300
  16.5 3.1 %first_tiles.1.sum_ref = f32[8,32,256]{2,1,0:T(8,128)S(1)} custom-call(s32[1]{0:T(128)} %bitcast.2.core_ref, s32[6,24]{1,0:T(8,128)S(1)} %get-tuple-element.60.plan_ref, f32[8,32,256]{2,1,0:T(8,128)} %side_ref.1, bf16[24,256,256]{2,1,0:T(8,128)(2,1)S(1)} %bring_near.2.a_ref, bf16[16,32,256]{2,1,0:T(8,128)(2,1)S(1)} %bitcast.19, ...), custom_call_target="tpu_custom_call" | custom-call | tf_op jit(solution)/shard_map/first_tiles/pallas_call | solution.py:327
  19.7 3.6 %last_tiles.1 = (f32[8,32,256]{2,1,0:T(8,128)}, bf16[13,16,256]{2,1,0:T(8,128)(2,1)S(1)}, bf16[13,16,256]{2,1,0:T(8,128)(2,1)}, bf16[13,16,256]{2,1,0:T(8,128)(2...) custom-call(s32[6,24]{1,0:T(8,128)S(1)} %get-tuple-element.60.plan_r, ...), custom_call_target="tpu_custom_call" | custom-call | tf_op jit(solution)/shard_map/last_tiles/pallas_call | solution.py:337
  23.5 3.5 %collective-permute-start.7 = (bf16[13,16,256]{2,1,0:T(8,128)(2,1)}, bf16[13,16,256]{2,1,0:T(8,128)(2,1)S(1)}, u32[]{:S(2)}, u32[]{:S(2)}) collective-permute-start(bf16[13,16,256]{2,1,0:T(8,128)(2,1)} %get-tuple-element.68), channel_id=1, source_target_pairs={{0,4},{1,5},{2,6},{3,7},{4,0},{5,1},{6,2},{7,3},{8,12},{9,13},{10,... | collective-permute-start | bytes 319496 | tf_op jit(solution)/shard_map/ppermute | solution.py:386
  27.1 3.2 %collective-permute-start.9 = (bf16[13,16,256]{2,1,0:T(8,128)(2,1)}, bf16[13,16,256]{2,1,0:T(8,128)(2,1)S(1)}, u32[]{:S(2)}, u32[]{:S(2)}) collective-permute-start(bf16[13,16,256]{2,1,0:T(8,128)(2,1)} %get-tuple-element.70), channel_id=1, source_target_pairs={{0,6},{1,7},{2,0},{3,1},{4,2},{5,3},{6,4},{7,5},{8,14},{9,15},{10,... | collective-permute-start | bytes 319496 | tf_op jit(solution)/shard_map/ppermute | solution.py:386
  32.2 1.9 %collective-permute-done.8.refs_2_ = bf16[13,16,256]{2,1,0:T(8,128)(2,1)S(1)} collective-permute-done((bf16[13,16,256]{2,1,0:T(8,128)(2,1)}, bf16[13,16,256]{2,1,0:T(8,128)(2,1)S(1)}, u32[]{:S(2)}, u32[]{:S(2)}) %collective-permute-start.8) | collective-permute-done | bytes 106528 | tf_op jit(solution)/shard_map/ppermute | solution.py:386
  34.2 1.3 collective-permute-done.9.refs_3_
  35.5 1.8 %collective-permute-done.10.refs_4_ = bf16[13,16,256]{2,1,0:T(8,128)(2,1)S(1)} collective-permute-done((bf16[13,16,256]{2,1,0:T(8,128)(2,1)}, bf16[13,16,256]{2,1,0:T(8,128)(2,1)S(1)}, u32[]{:S(2)}, u32[]{:S(2)}) %collective-permute-start.10) | collective-permute-done | bytes 106528 | tf_op jit(solution)/shard_map/ppermute | solution.py:386
  37.3 1.7 %collective-permute-done.12.refs_6_ = bf16[13,16,256]{2,1,0:T(8,128)(2,1)S(1)} collective-permute-done((bf16[13,16,256]{2,1,0:T(8,128)(2,1)}, bf16[13,16,256]{2,1,0:T(8,128)(2,1)S(1)}, u32[]{:S(2)}, u32[]{:S(2)}) %collective-permute-start.12) | collective-permute-done | bytes 106528 | tf_op jit(solution)/shard_map/ppermute | solution.py:386
  39.7 1.7 %collective-permute-start.14 = (bf16[128,256]{1,0:T(8,128)(2,1)S(1)}, bf16[128,256]{1,0:T(8,128)(2,1)S(1)}, u32[]{:S(2)}, u32[]{:S(2)}) collective-permute-start(bf16[128,256]{1,0:T(8,128)(2,1)S(1)} %get-tuple-element.87), channel_id=1, source_target_pairs={{0,16},{8,24},{16,0},{24,8},{1,17},{9,25},{17,1},{25,9},{2,18},{10... | collective-permute-start | bytes 196616 | tf_op jit(solution)/shard_map/ppermute | solution.py:401
  42.1 2.6 %collective-permute-start.16 = (bf16[128,256]{1,0:T(8,128)(2,1)S(1)}, bf16[128,256]{1,0:T(8,128)(2,1)S(1)}, u32[]{:S(2)}, u32[]{:S(2)}) collective-permute-start(bf16[128,256]{1,0:T(8,128)(2,1)S(1)} %get-tuple-element.89), channel_id=1, source_target_pairs={{0,24},{8,0},{16,8},{24,16},{1,25},{9,1},{17,9},{25,17},{2,26},{10... | collective-permute-start | bytes 196616 | tf_op jit(solution)/shard_map/ppermute | solution.py:401
  44.6 2.5 %bring_near.3.refs_1_.refs_2_.refs_3_.c_ref = bf16[3,4,3,256,256]{4,3,2,1,0:T(8,128)(2,1)S(1)} custom-call(bf16[3,4,3,256,256]{4,3,2,1,0:T(8,128)(2,1)} %refs_0_.3, bf16[128,256]{1,0:T(8,128)(2,1)S(1)} %get-tuple-element.86.refs_1_), custom_call_target="tpu_custom_call" | custom-call | tf_op jit(solution)/shard_map/bring_near/pallas_call | solution.py:145
  47.2 16.6 %all_to_all.40.parts_ref = bf16[8,16,256]{2,1,0:T(8,128)(2,1)S(1)} all-to-all(bf16[8,16,256]{2,1,0:T(8,128)(2,1)S(1)} %bitcast.21), channel_id=1, replica_groups=mesh['z'=8,'y'=4,'x'=4,'core'=2] {'z'}, dimensions={0} | all-to-all | bytes 131072 | tf_op jit(solution)/shard_map/all_to_all | solution.py:406
  64.1 8.2 %all_to_all.41.refs_0_ = bf16[8,8,256]{2,1,0:T(8,128)(2,1)S(1)} all-to-all(bf16[8,8,256]{2,1,0:T(8,128)(2,1)S(1)} %get-tuple-element.96), channel_id=1, replica_groups=mesh['z'=8,'y'=4,'x'=4,'core'=2] {'core','x'}, dimensions={0} | all-to-all | bytes 65536 | tf_op jit(solution)/shard_map/all_to_all | solution.py:431
  73.1 7.7 %all_to_all.42.refs_1_ = bf16[8,8,256]{2,1,0:T(8,128)(2,1)S(1)} all-to-all(bf16[8,8,256]{2,1,0:T(8,128)(2,1)S(1)} %get-tuple-element.100), channel_id=1, replica_groups=mesh['z'=8,'y'=4,'x'=4,'core'=2] {'core','x'}, dimensions={0} | all-to-all | bytes 65536 | tf_op jit(solution)/shard_map/all_to_all | solution.py:431
  81.6 7.7 %all_to_all.43.refs_2_ = bf16[8,8,256]{2,1,0:T(8,128)(2,1)S(1)} all-to-all(bf16[8,8,256]{2,1,0:T(8,128)(2,1)S(1)} %get-tuple-element.104), channel_id=1, replica_groups=mesh['z'=8,'y'=4,'x'=4,'core'=2] {'core','x'}, dimensions={0} | all-to-all | bytes 65536 | tf_op jit(solution)/shard_map/all_to_all | solution.py:431
  89.3 1.6 %turn.1 = (f32[4,256]{1,0:T(4,128)S(1)}, bf16[8,8,256]{2,1,0:T(8,128)(2,1)S(1)}, f32[128,256]{1,0:T(8,128)S(1)}) custom-call(f32[16,256]{1,0:T(8,128)S(1)} %get-tuple-element.94.g_ref, bf16[16,192]{1,0:T(8,128)(2,1)S(1)} %fusion.6.look_ref, bf16[192,16]{1,0:T(8,128)(2,1)S(1)} %fusion.3.scatter_ref, bf16[8,8,256]{2,1,0:T(8,128)(2,1)S(1)} %all_to_all.41.refs_0_, ...), custom_call_target="tpu_custom_call" | custom-call | tf_op jit(solution)/shard_map/turn/pallas_call | solution.py:445
  90.9 7.7 %all_to_all.44.recv_ref = bf16[8,8,256]{2,1,0:T(8,128)(2,1)S(1)} all-to-all(bf16[8,8,256]{2,1,0:T(8,128)(2,1)S(1)} %get-tuple-element.105), channel_id=1, replica_groups=mesh['z'=8,'y'=4,'x'=4,'core'=2] {'core','x'}, dimensions={0} | all-to-all | bytes 65536 | tf_op jit(solution)/shard_map/all_to_all | solution.py:457
  99.7 7.7 %all_to_all.45.recv_ref = bf16[8,8,256]{2,1,0:T(8,128)(2,1)S(1)} all-to-all(bf16[8,8,256]{2,1,0:T(8,128)(2,1)S(1)} %get-tuple-element.108), channel_id=1, replica_groups=mesh['z'=8,'y'=4,'x'=4,'core'=2] {'core','x'}, dimensions={0} | all-to-all | bytes 65536 | tf_op jit(solution)/shard_map/all_to_all | solution.py:457
  108.5 7.8 %all_to_all.46.recv_ref = bf16[8,8,256]{2,1,0:T(8,128)(2,1)S(1)} all-to-all(bf16[8,8,256]{2,1,0:T(8,128)(2,1)S(1)} %get-tuple-element.111), channel_id=1, replica_groups=mesh['z'=8,'y'=4,'x'=4,'core'=2] {'core','x'}, dimensions={0} | all-to-all | bytes 65536 | tf_op jit(solution)/shard_map/all_to_all | solution.py:457
  116.6 10.8 %all_to_all.47 = bf16[8,16,256]{2,1,0:T(8,128)(2,1)S(1)} all-to-all(bf16[8,16,256]{2,1,0:T(8,128)(2,1)S(1)} %backward_0.1), channel_id=1, replica_groups=mesh['z'=8,'y'=4,'x'=4,'core'=2] {'z'}, dimensions={0} | all-to-all | bytes 131072 | tf_op jit(solution)/shard_map/all_to_all | solution.py:482
  127.3 4.4 %collective-permute-start.18 = (bf16[8,16,256]{2,1,0:T(8,128)(2,1)S(1)}, bf16[8,16,256]{2,1,0:T(8,128)(2,1)S(1)}, u32[]{:S(2)}, u32[]{:S(2)}) collective-permute-start(bf16[8,16,256]{2,1,0:T(8,128)(2,1)S(1)} %all_to_all.47), channel_id=1, source_target_pairs={{0,16},{8,24},{16,0},{24,8},{1,17},{9,25},{17,1},{25,9},{2,18},{10... | collective-permute-start | bytes 196616 | tf_op jit(solution)/shard_map/ppermute | solution.py:483
  131.8 1.5 %collective-permute-done.19 = bf16[8,16,256]{2,1,0:T(8,128)(2,1)S(1)} collective-permute-done((bf16[8,16,256]{2,1,0:T(8,128)(2,1)S(1)}, bf16[8,16,256]{2,1,0:T(8,128)(2,1)S(1)}, u32[]{:S(2)}, u32[]{:S(2)}) %collective-permute-start.19) | collective-permute-done | bytes 65568 | tf_op jit(solution)/shard_map/ppermute | solution.py:483
  133.2 1.4 %collective-permute-done.18 = bf16[8,16,256]{2,1,0:T(8,128)(2,1)S(1)} collective-permute-done((bf16[8,16,256]{2,1,0:T(8,128)(2,1)S(1)}, bf16[8,16,256]{2,1,0:T(8,128)(2,1)S(1)}, u32[]{:S(2)}, u32[]{:S(2)}) %collective-permute-start.18) | collective-permute-done | bytes 65568 | tf_op jit(solution)/shard_map/ppermute | solution.py:483
  134.6 1.3 collective-permute-done.17
  136.0 1.2 convolution_add_fusion
  (51 shorter events, 9.9 us)
Async XLA Ops:
  1.7 1.8 %collective-permute-start = (bf16[16,32,256]{2,1,0:T(8,128)(2,1)S(1)}, bf16[16,32,256]{2,1,0:T(8,128)(2,1)}, u32[]{:S(2)}, u32[]{:S(2)}) collective-permute-start(bf16[16,32,256]{2,1,0:T(8,128)(2,1)S(1)} %bitcast.17), channel_id=1, source_target_pairs={{0,1},{1,0},{2,3},{3,2},{4,5},{5,4},{6,7},{7,6},{8,9},{9,8},{10,11... | collective-permute-start | bytes 786440 | tf_op jit(solution)/shard_map/ppermute | solution.py:303
  1.8 6.8 %collective-permute-start.2 = (bf16[16,32,256]{2,1,0:T(8,128)(2,1)S(1)}, bf16[16,32,256]{2,1,0:T(8,128)(2,1)}, u32[]{:S(2)}, u32[]{:S(2)}) collective-permute-start(bf16[16,32,256]{2,1,0:T(8,128)(2,1)S(1)} %bitcast.18), channel_id=1, source_target_pairs={{0,2},{1,7},{2,4},{3,1},{4,6},{5,3},{6,0},{7,5},{8,10},{9,15},{10,... | collective-permute-start | bytes 786440 | tf_op jit(solution)/shard_map/ppermute | solution.py:300
  3.5 10.3 %collective-permute-start.1 = (bf16[16,32,256]{2,1,0:T(8,128)(2,1)}, bf16[16,32,256]{2,1,0:T(8,128)(2,1)}, u32[]{:S(2)}, u32[]{:S(2)}) collective-permute-start(bf16[16,32,256]{2,1,0:T(8,128)(2,1)} %collective-permute-done.refs_1_), channel_id=1, source_target_pairs={{0,2},{1,7},{2,4},{3,1},{4,6},{5,3},{6,0},{7,5},{8,10},{9,15},{10,... | collective-permute-start | bytes 786440 | tf_op jit(solution)/shard_map/ppermute | solution.py:300
  8.6 7.9 %collective-permute-start.3 = (bf16[16,32,256]{2,1,0:T(8,128)(2,1)}, bf16[16,32,256]{2,1,0:T(8,128)(2,1)}, u32[]{:S(2)}, u32[]{:S(2)}) collective-permute-start(bf16[16,32,256]{2,1,0:T(8,128)(2,1)} %collective-permute-done.2.refs_3_), channel_id=1, source_target_pairs={{0,2},{1,7},{2,4},{3,1},{4,6},{5,3},{6,0},{7,5},{8,10},{9,15},{10,... | collective-permute-start | bytes 786440 | tf_op jit(solution)/shard_map/ppermute | solution.py:300
  13.6 3.0 %collective-permute-start.5 = (bf16[16,32,256]{2,1,0:T(8,128)(2,1)}, bf16[16,32,256]{2,1,0:T(8,128)(2,1)}, u32[]{:S(2)}, u32[]{:S(2)}) collective-permute-start(bf16[16,32,256]{2,1,0:T(8,128)(2,1)} %collective-permute-done.2.refs_3_), channel_id=1, source_target_pairs={{0,1},{1,0},{2,3},{3,2},{4,5},{5,4},{6,7},{7,6},{8,9},{9,8},{10,11... | collective-permute-start | bytes 786440 | tf_op jit(solution)/shard_map/ppermute | solution.py:319
  13.7 2.8 %collective-permute-start.4 = (bf16[16,32,256]{2,1,0:T(8,128)(2,1)}, bf16[16,32,256]{2,1,0:T(8,128)(2,1)}, u32[]{:S(2)}, u32[]{:S(2)}) collective-permute-start(bf16[16,32,256]{2,1,0:T(8,128)(2,1)} %collective-permute-done.1.refs_4_), channel_id=1, source_target_pairs={{0,1},{1,0},{2,3},{3,2},{4,5},{5,4},{6,7},{7,6},{8,9},{9,8},{10,11... | collective-permute-start | bytes 786440 | tf_op jit(solution)/shard_map/ppermute | solution.py:323
  16.5 3.2 %collective-permute-start.6 = (bf16[16,32,256]{2,1,0:T(8,128)(2,1)}, bf16[16,32,256]{2,1,0:T(8,128)(2,1)}, u32[]{:S(2)}, u32[]{:S(2)}) collective-permute-start(bf16[16,32,256]{2,1,0:T(8,128)(2,1)} %collective-permute-done.3.refs_2_), channel_id=1, source_target_pairs={{0,1},{1,0},{2,3},{3,2},{4,5},{5,4},{6,7},{7,6},{8,9},{9,8},{10,11... | collective-permute-start | bytes 786440 | tf_op jit(solution)/shard_map/ppermute | solution.py:323
  19.7 3.6 %copy-start.2 = (s32[3,4,3]{2,1,0:T(4,128)S(1)}, s32[3,4,3]{2,1,0:T(4,128)}, u32[]{:S(2)}) copy-start(s32[3,4,3]{2,1,0:T(4,128)} %param.15) | copy-start | bytes 436
  23.5 8.6 %collective-permute-start.7 = (bf16[13,16,256]{2,1,0:T(8,128)(2,1)}, bf16[13,16,256]{2,1,0:T(8,128)(2,1)S(1)}, u32[]{:S(2)}, u32[]{:S(2)}) collective-permute-start(bf16[13,16,256]{2,1,0:T(8,128)(2,1)} %get-tuple-element.68), channel_id=1, source_target_pairs={{0,4},{1,5},{2,6},{3,7},{4,0},{5,1},{6,2},{7,3},{8,12},{9,13},{10,... | collective-permute-start | bytes 319496 | tf_op jit(solution)/shard_map/ppermute | solution.py:386
  27.0 7.0 %collective-permute-start.8 = (bf16[13,16,256]{2,1,0:T(8,128)(2,1)}, bf16[13,16,256]{2,1,0:T(8,128)(2,1)S(1)}, u32[]{:S(2)}, u32[]{:S(2)}) collective-permute-start(bf16[13,16,256]{2,1,0:T(8,128)(2,1)} %get-tuple-element.69), channel_id=1, source_target_pairs={{0,5},{1,4},{2,7},{3,6},{4,1},{5,0},{6,3},{7,2},{8,13},{9,12},{10,... | collective-permute-start | bytes 319496 | tf_op jit(solution)/shard_map/ppermute | solution.py:386
  27.1 8.4 %collective-permute-start.9 = (bf16[13,16,256]{2,1,0:T(8,128)(2,1)}, bf16[13,16,256]{2,1,0:T(8,128)(2,1)S(1)}, u32[]{:S(2)}, u32[]{:S(2)}) collective-permute-start(bf16[13,16,256]{2,1,0:T(8,128)(2,1)} %get-tuple-element.70), channel_id=1, source_target_pairs={{0,6},{1,7},{2,0},{3,1},{4,2},{5,3},{6,4},{7,5},{8,14},{9,15},{10,... | collective-permute-start | bytes 319496 | tf_op jit(solution)/shard_map/ppermute | solution.py:386
  30.4 7.0 %collective-permute-start.10 = (bf16[13,16,256]{2,1,0:T(8,128)(2,1)}, bf16[13,16,256]{2,1,0:T(8,128)(2,1)S(1)}, u32[]{:S(2)}, u32[]{:S(2)}) collective-permute-start(bf16[13,16,256]{2,1,0:T(8,128)(2,1)} %get-tuple-element.71), channel_id=1, source_target_pairs={{0,7},{1,6},{2,1},{3,0},{4,3},{5,2},{6,5},{7,4},{8,15},{9,14},{10,... | collective-permute-start | bytes 319496 | tf_op jit(solution)/shard_map/ppermute | solution.py:386
  31.3 6.0 %collective-permute-start.11 = (bf16[13,16,256]{2,1,0:T(8,128)(2,1)}, bf16[13,16,256]{2,1,0:T(8,128)(2,1)S(1)}, u32[]{:S(2)}, u32[]{:S(2)}) collective-permute-start(bf16[13,16,256]{2,1,0:T(8,128)(2,1)} %get-tuple-element.72), channel_id=1, source_target_pairs={{0,3},{1,2},{2,5},{3,4},{4,7},{5,6},{6,1},{7,0},{8,11},{9,10},{10,... | collective-permute-start | bytes 319496 | tf_op jit(solution)/shard_map/ppermute | solution.py:386
  32.1 7.0 %collective-permute-start.12 = (bf16[13,16,256]{2,1,0:T(8,128)(2,1)}, bf16[13,16,256]{2,1,0:T(8,128)(2,1)S(1)}, u32[]{:S(2)}, u32[]{:S(2)}) collective-permute-start(bf16[13,16,256]{2,1,0:T(8,128)(2,1)} %get-tuple-element.73), channel_id=1, source_target_pairs={{0,2},{1,3},{2,4},{3,5},{4,6},{5,7},{6,0},{7,1},{8,10},{9,11},{10,... | collective-permute-start | bytes 319496 | tf_op jit(solution)/shard_map/ppermute | solution.py:386
  34.1 5.0 %collective-permute-start.13 = (bf16[13,16,256]{2,1,0:T(8,128)(2,1)}, bf16[13,16,256]{2,1,0:T(8,128)(2,1)S(1)}, u32[]{:S(2)}, u32[]{:S(2)}) collective-permute-start(bf16[13,16,256]{2,1,0:T(8,128)(2,1)} %get-tuple-element.74), channel_id=1, source_target_pairs={{0,1},{1,0},{2,3},{3,2},{4,5},{5,4},{6,7},{7,6},{8,9},{9,8},{10,11... | collective-permute-start | bytes 319496 | tf_op jit(solution)/shard_map/ppermute | solution.py:386
  39.7 7.5 %collective-permute-start.14 = (bf16[128,256]{1,0:T(8,128)(2,1)S(1)}, bf16[128,256]{1,0:T(8,128)(2,1)S(1)}, u32[]{:S(2)}, u32[]{:S(2)}) collective-permute-start(bf16[128,256]{1,0:T(8,128)(2,1)S(1)} %get-tuple-element.87), channel_id=1, source_target_pairs={{0,16},{8,24},{16,0},{24,8},{1,17},{9,25},{17,1},{25,9},{2,18},{10... | collective-permute-start | bytes 196616 | tf_op jit(solution)/shard_map/ppermute | solution.py:401
  41.4 5.8 %collective-permute-start.15 = (bf16[128,256]{1,0:T(8,128)(2,1)S(1)}, bf16[128,256]{1,0:T(8,128)(2,1)S(1)}, u32[]{:S(2)}, u32[]{:S(2)}) collective-permute-start(bf16[128,256]{1,0:T(8,128)(2,1)S(1)} %get-tuple-element.88), channel_id=1, source_target_pairs={{0,8},{8,16},{16,24},{24,0},{1,9},{9,17},{17,25},{25,1},{2,10},{10... | collective-permute-start | bytes 196616 | tf_op jit(solution)/shard_map/ppermute | solution.py:401
  42.1 5.1 %collective-permute-start.16 = (bf16[128,256]{1,0:T(8,128)(2,1)S(1)}, bf16[128,256]{1,0:T(8,128)(2,1)S(1)}, u32[]{:S(2)}, u32[]{:S(2)}) collective-permute-start(bf16[128,256]{1,0:T(8,128)(2,1)S(1)} %get-tuple-element.89), channel_id=1, source_target_pairs={{0,24},{8,0},{16,8},{24,16},{1,25},{9,1},{17,9},{25,17},{2,26},{10... | collective-permute-start | bytes 196616 | tf_op jit(solution)/shard_map/ppermute | solution.py:401
  44.6 19.2 %copy-start = (bf16[4,4,256,256]{3,2,1,0:T(8,128)(2,1)S(1)}, bf16[4,4,256,256]{3,2,1,0:T(8,128)(2,1)}, u32[]{:S(2)}) copy-start(bf16[4,4,256,256]{3,2,1,0:T(8,128)(2,1)} %d_ref.7) | copy-start | bytes 6291460
  108.5 27.5 %copy-start.1 = (f32[4,4,32,256]{3,2,1,0:T(8,128)S(1)}, f32[4,4,32,256]{3,2,1,0:T(8,128)}, u32[]{:S(2)}) copy-start(f32[4,4,32,256]{3,2,1,0:T(8,128)} %param.12) | copy-start | bytes 1572868
  127.3 5.9 %collective-permute-start.19 = (bf16[8,16,256]{2,1,0:T(8,128)(2,1)S(1)}, bf16[8,16,256]{2,1,0:T(8,128)(2,1)S(1)}, u32[]{:S(2)}, u32[]{:S(2)}) collective-permute-start(bf16[8,16,256]{2,1,0:T(8,128)(2,1)S(1)} %all_to_all.47), channel_id=1, source_target_pairs={{0,8},{8,16},{16,24},{24,0},{1,9},{9,17},{17,25},{25,1},{2,10},{10... | collective-permute-start | bytes 196616 | tf_op jit(solution)/shard_map/ppermute | solution.py:483
  127.3 7.3 %collective-permute-start.18 = (bf16[8,16,256]{2,1,0:T(8,128)(2,1)S(1)}, bf16[8,16,256]{2,1,0:T(8,128)(2,1)S(1)}, u32[]{:S(2)}, u32[]{:S(2)}) collective-permute-start(bf16[8,16,256]{2,1,0:T(8,128)(2,1)S(1)} %all_to_all.47), channel_id=1, source_target_pairs={{0,16},{8,24},{16,0},{24,8},{1,17},{9,25},{17,1},{25,9},{2,18},{10... | collective-permute-start | bytes 196616 | tf_op jit(solution)/shard_map/ppermute | solution.py:483
  131.7 4.3 %collective-permute-start.17 = (bf16[8,16,256]{2,1,0:T(8,128)(2,1)S(1)}, bf16[8,16,256]{2,1,0:T(8,128)(2,1)S(1)}, u32[]{:S(2)}, u32[]{:S(2)}) collective-permute-start(bf16[8,16,256]{2,1,0:T(8,128)(2,1)S(1)} %all_to_all.47), channel_id=1, source_target_pairs={{0,24},{8,0},{16,8},{24,16},{1,25},{9,1},{17,9},{25,17},{2,26},{10... | collective-permute-start | bytes 196616 | tf_op jit(solution)/shard_map/ppermute | solution.py:483

commit v7 on v6

--- a/solution.py
+++ b/solution.py
@@ -34,8 +34,9 @@
     note[...] = jnp.zeros_like(note)
     for o in range(OWNERS):
         count_ref[o] = 0
-    for i in range(CAP):
-        plan_ref[5, i] = -1
+    for o in range(OWNERS):
+        for i in range(CAP):
+            plan_ref[5 + o, i] = -1
     for t in range(col_ref.shape[0]):
         c = col_ref[t]
         level, owner, inner = c // (sn * OWNERS), (c // sn) % OWNERS, c % sn
@@ -47,34 +48,48 @@
         plan_ref[2, t] = row_ref[t]
         plan_ref[3, t] = away
         plan_ref[4, t] = rank
-
-        @pl.when(away == LAST)
-        def _():
-            plan_ref[5, rank] = t
-
+        plan_ref[5 + away, rank] = t
         mark = (level * sn + inner + 1).astype(F32)
         note[away, pl.ds(rank, 1), :] = jnp.full((1, note.shape[2]), mark, F32)
     note_ref[...] = note[...].astype(BF16)
 
 
-def first_tiles_kernel(n_blocks, core_ref, plan_ref, side_ref, a_ref, *refs):
-    blocks = refs[:n_blocks]
-    core = core_ref[0]
-    res_ref, x_all, sems = refs[n_blocks:]
+def add_slots(away, first, x_ref, plan_ref, a_ref, res_ref):
+    for i in range(CAP):
+        t = jnp.maximum(plan_ref[5 + away, i], 0)
+        there = (plan_ref[5 + away, i] >= 0).astype(F32)
+        res_ref[plan_ref[2, t]] -= there * dot(x_ref[first + plan_ref[1, t]], a_ref[t], NT)
+
+
+def first_tiles_kernel(core_ref, plan_ref, side_ref, a_ref, own, other, near, near_2, res_ref, x_all, sems):
     mine = x_all.shape[0] // OWNERS
-    own, rest = 2 * X - 2 - 4 * core, 2 + 4 * core
-    places = [0, 1, 4, own, own + 1, rest, rest + 1]
-    copies = [pltpu.make_async_copy(side_ref, res_ref, sems.at[n_blocks])]
-    for i, block in enumerate(blocks):
-        copies.append(pltpu.make_async_copy(block, x_all.at[pl.ds(places[i] * mine, mine)], sems.at[i]))
-    for copy in copies:
-        copy.start()
-    x_all[LAST * mine : (LAST + 1) * mine] = jnp.zeros((mine,) + x_all.shape[1:], BF16)
+    side = 2 * X - 2 - 4 * core_ref[0]
+    copies = [pltpu.make_async_copy(side_ref, res_ref, sems.at[4])]
+    copies[0].start()
+    x_all[...] = jnp.zeros_like(x_all)
+    for i, (block, place) in enumerate(((own, 0), (other, 1), (near, side), (near_2, side + 1))):
+        copies.append(pltpu.make_async_copy(block, x_all.at[pl.ds(place * mine, mine)], sems.at[i]))
+        copies[-1].start()
     for copy in copies:
         copy.wait()
     for t in range(a_ref.shape[0]):
         q = plan_ref[2, t]
         res_ref[q] -= dot(x_all[plan_ref[0, t] * mine + plan_ref[1, t]], a_ref[t], NT)
+
+
+def next_tiles_kernel(core_ref, plan_ref, sum_ref, a_ref, far, cross, cross_2, res_ref, x_ref, sems):
+    mine = x_ref.shape[0] // 3
+    sums = pltpu.make_async_copy(sum_ref, res_ref, sems.at[3])
+    sums.start()
+    copies = []
+    for i, block in enumerate((far, cross, cross_2)):
+        copies.append(pltpu.make_async_copy(block, x_ref.at[pl.ds(i * mine, mine)], sems.at[i]))
+        copies[-1].start()
+    side = 2 + 4 * core_ref[0]
+    sums.wait()
+    for i, away in enumerate((2 * CORE, side, side + 1)):
+        copies[i].wait()
+        add_slots(away, i * mine, x_ref, plan_ref, a_ref, res_ref)
 
 
 def last_tiles_kernel(plan_ref, note_ref, sum_ref, a_ref, block_ref, res_hbm, own_ref, *refs):
@@ -90,11 +105,7 @@
     res_ref[...] = sum_ref[...]
     for copy in copies:
         copy.wait()
-    for i in range(CAP):
-        t = jnp.maximum(plan_ref[5, i], 0)
-        there = (plan_ref[5, i] >= 0).astype(F32)
-        q = plan_ref[2, t]
-        res_ref[q] -= there * dot(x_last[plan_ref[1, t]], a_ref[t], NT)
+    add_slots(LAST, 0, x_last, plan_ref, a_ref, res_ref)
     copies = [pltpu.make_async_copy(res_ref, res_hbm, sems.at[0])]
     copies[0].start()
     low_ref[...] = res_ref[...].astype(BF16)
@@ -306,7 +317,7 @@
     plan, note = pl.pallas_call(
         functools.partial(plan_kernel, sn),
         out_shape=(
-            jax.ShapeDtypeStruct((6, tiles), jnp.int32),
+            jax.ShapeDtypeStruct((5 + OWNERS, tiles), jnp.int32),
             pltpu.HBM((OWNERS, 16, T), BF16),
         ),
         in_specs=[SMEM, SMEM, SMEM],
@@ -315,24 +326,34 @@
         compiler_params=PARAMS,
         name="plan",
     )(here, in_hbm(tile_col), in_hbm(tile_row))
+    (a_near,) = bring_near(swapped, a_tiles)
+    first, note, a_near = lax.optimization_barrier((first, note, a_near))
     third = along(first)
-    cross_first = other(first)
-    (a_near,) = bring_near(None, a_tiles)
+    cross_first, cross_second = other(first), other(second)
     side = in_hbm(right_side)
-    second, note, a_near = lax.optimization_barrier((second, note, a_near))
-    cross_second, cross_third = other(second), other(third)
-    blocks = [e, swapped, third, first, second, cross_second, cross_first]
 
     slot_rows = CAP * K + 16
+    core = lax.axis_index("core").reshape(1)
     part_sum = pl.pallas_call(
-        functools.partial(first_tiles_kernel, len(blocks)),
+        first_tiles_kernel,
+        out_shape=pltpu.HBM((row_tiles, K, T), F32),
+        in_specs=[SMEM, SMEM, ANY, VMEM] + [ANY] * 4,
+        out_specs=VMEM,
+        scratch_shapes=[pltpu.VMEM((OWNERS * mine, K, T), BF16), pltpu.SemaphoreType.DMA((5,))],
+        compiler_params=PARAMS,
+        name="first_tiles",
+    )(core, plan, side, a_near, e, swapped, first, second)
+    third, part_sum = lax.optimization_barrier((third, part_sum))
+    cross_third = other(third)
+    part_sum = pl.pallas_call(
+        next_tiles_kernel,
         out_shape=jax.ShapeDtypeStruct((row_tiles, K, T), F32),
-        in_specs=[SMEM, SMEM, ANY, VMEM] + [ANY] * len(blocks),
+        in_specs=[SMEM, SMEM, ANY, VMEM] + [ANY] * 3,
         out_specs=VMEM,
-        scratch_shapes=[pltpu.VMEM((OWNERS * mine, K, T), BF16), pltpu.SemaphoreType.DMA((len(blocks) + 1,))],
-        compiler_params=PARAMS,
-        name="first_tiles",
-    )(lax.axis_index("core").reshape(1), plan, side, a_near, *blocks)
+        scratch_shapes=[pltpu.VMEM((3 * mine, K, T), BF16), pltpu.SemaphoreType.DMA((4,))],
+        compiler_params=PARAMS,
+        name="next_tiles",
+    )(core, plan, in_hbm(part_sum), a_near, third, cross_second, cross_first)
     slots = slot_rows // 16
     residual, *send = pl.pallas_call(
         last_tiles_kernel,

time: 138 us -> 137 us (level)
  waiting for transfers between devices: 17 us -> 12 us
  Pallas kernels: 19.4 us -> 22.9 us
    ppermute x3, waiting for transfers between devices: 6 us -> 2.08 us  [along(): return lax.ppermute(block, snode, perm)]
    pallas_call x1 -> x2, Pallas kernels: 3.15 us -> 6.52 us  [the longest x1 3.74 us: local(): pl.pallas_call(first_tiles_kernel, out_shape=pltpu.HBM((row_tiles, K, T),...]
  transfers between devices with their start and end apart: 20 -> 20, of which waited for: 10 -> 10; matrix products, arithmetic and copies ran while one was open for 0% -> 0% of each run, Pallas kernels for 7% -> 9%
where the time goes in v7:
time: 137 us
  blocking collectives  74.5 us (54%)
  starting transfers between devices  23.5 us (17%)
  Pallas kernels  22.9 us (17%)
  waiting for transfers between devices  12 us (9%)
  other arithmetic  1.45 us (1%)
    all_to_all x3, blocking collectives, local(): known.append(lax.all_to_all(out, ('core', 'x'), 0, 0, tiled=True))  24 us
    all_to_all x3, blocking collectives, local(): arrived = lax.all_to_all(out, ('core', 'x'), 0, 0, tiled=True)  23.2 us
    all_to_all x1, blocking collectives, local(): lax.all_to_all(total.astype(BF16).reshape(Z, mine, T), 'z', 0, 0, tiled=T...  16.6 us
    all_to_all x1, blocking collectives, local(): column = lax.all_to_all(change, 'z', 0, 0, tiled=True)  10.8 us
    ppermute x7, starting transfers between devices, local(): recv.append(lax.ppermute(send[away], snode, perm))  9.06 us
    ppermute x7, waiting for transfers between devices, local(): recv.append(lax.ppermute(send[away], snode, perm))  5.63 us
    ppermute x3, starting transfers between devices, along(): return lax.ppermute(block, snode, perm)  4.98 us
    ppermute x3, starting transfers between devices, local(): arrived = [lax.ppermute(part[s], 'y', shift(Y, s)) for s in (2, 1, 3)]  4.96 us
  transfers between devices with their start and end apart: 20, of which 10 were waited for; matrix products, arithmetic and copies ran while one was open for 0% of the time, Pallas kernels for 9%

profile of v7, /device:TPU:2, one launch (start us, length us, event | category | flops | bytes accessed | tf_op | source)
XLA Modules:
  0.0 136.5 jit_solution(4676120997105692397)
XLA Ops:
  1.8 1.6 %collective-permute-start.1 = (bf16[16,32,256]{2,1,0:T(8,128)(2,1)S(1)}, bf16[16,32,256]{2,1,0:T(8,128)(2,1)}, u32[]{:S(2)}, u32[]{:S(2)}) collective-permute-start(bf16[16,32,256]{2,1,0:T(8,128)(2,1)S(1)} %bitcast.18), channel_id=1, source_target_pairs={{0,2},{1,7},{2,4},{3,1},{4,6},{5,3},{6,0},{7,5},{8,10},{9,15},{10,... | collective-permute-start | bytes 786440 | tf_op jit(solution)/shard_map/ppermute | solution.py:311
  3.5 1.5 %collective-permute-start.3 = (bf16[16,32,256]{2,1,0:T(8,128)(2,1)}, bf16[16,32,256]{2,1,0:T(8,128)(2,1)}, u32[]{:S(2)}, u32[]{:S(2)}) collective-permute-start(bf16[16,32,256]{2,1,0:T(8,128)(2,1)} %collective-permute-done.refs_1_.other), channel_id=1, source_target_pairs={{0,2},{1,7},{2,4},{3,1},{4,6},{5,3},{6,0},{7,5},{8,10},{9,15},{10,... | collective-permute-start | bytes 786440 | tf_op jit(solution)/shard_map/ppermute | solution.py:311
  5.0 1.9 %bring_near.2.a_ref = bf16[24,256,256]{2,1,0:T(8,128)(2,1)S(1)} custom-call(bf16[24,256,256]{2,1,0:T(8,128)(2,1)} %refs_0_.2, bf16[16,32,256]{2,1,0:T(8,128)(2,1)} %collective-permute-done.refs_1_.other), custom_call_target="tpu_custom_call" | custom-call | tf_op jit(solution)/shard_map/bring_near/pallas_call | solution.py:156
  6.8 1.9 %plan.1 = (s32[13,24]{1,0:T(8,128)S(1)}, bf16[8,16,256]{2,1,0:T(8,128)(2,1)}) custom-call(s32[1]{0:T(128)} %bitcast.1.here_ref, s32[24]{0:T(128)} %col_ref.1, s32[24]{0:T(128)} %row_ref.1), custom_call_target="tpu_custom_call" | custom-call | tf_op jit(solution)/shard_map/plan/pallas_call | solution.py:317
  8.8 1.9 %collective-permute-start.2 = (bf16[16,32,256]{2,1,0:T(8,128)(2,1)}, bf16[16,32,256]{2,1,0:T(8,128)(2,1)}, u32[]{:S(2)}, u32[]{:S(2)}) collective-permute-start(bf16[16,32,256]{2,1,0:T(8,128)(2,1)} %collective-permute-done.1.near), channel_id=1, source_target_pairs={{0,2},{1,7},{2,4},{3,1},{4,6},{5,3},{6,0},{7,5},{8,10},{9,15},{10,... | collective-permute-start | bytes 786440 | tf_op jit(solution)/shard_map/ppermute | solution.py:311
  11.4 3.7 %first_tiles.1.sum_ref = f32[8,32,256]{2,1,0:T(8,128)} custom-call(s32[1]{0:T(128)} %bitcast.2.core_ref, s32[13,24]{1,0:T(8,128)S(1)} %get-tuple-element.62.plan_ref, f32[8,32,256]{2,1,0:T(8,128)} %side_ref.1, bf16[24,256,256]{2,1,0:T(8,128)(2,1)S(1)} %bring_near.2.a_ref, bf16[16,32,256]{2,1,0:T(8,128)(2,1)S(1)} %bitcast.19, ...), custom_call_target="tpu_custom_call" | custom-call | tf_op jit(solution)/shard_map/first_tiles/pallas_call | solution.py:337
  15.2 1.3 collective-permute-done.2.far
  16.6 2.8 %next_tiles.1.sum_ref = f32[8,32,256]{2,1,0:T(8,128)S(1)} custom-call(s32[1]{0:T(128)} %bitcast.2.core_ref, s32[13,24]{1,0:T(8,128)S(1)} %get-tuple-element.62.plan_ref, f32[8,32,256]{2,1,0:T(8,128)} %first_tiles.1.sum_ref, bf16[24,256,256]{2,1,0:T(8,128)(2,1)S(1)} %bring_near.2.a_ref, bf16[16,32,256]{2,1,0:T(8,128)(2,1)} %collective-permute-done.2.far, ...), custom_call_target="tpu_custom_call" | custom-call | tf_op jit(solution)/shard_map/next_tiles/pallas_call | solution.py:348
  19.4 3.5 %last_tiles.1 = (f32[8,32,256]{2,1,0:T(8,128)}, bf16[13,16,256]{2,1,0:T(8,128)(2,1)S(1)}, bf16[13,16,256]{2,1,0:T(8,128)(2,1)}, bf16[13,16,256]{2,1,0:T(8,128)(2...) custom-call(s32[13,24]{1,0:T(8,128)S(1)} %get-tuple-element.62.plan_, ...), custom_call_target="tpu_custom_call" | custom-call | tf_op jit(solution)/shard_map/last_tiles/pallas_call | solution.py:358
  23.1 2.0 %collective-permute-start.7 = (bf16[13,16,256]{2,1,0:T(8,128)(2,1)}, bf16[13,16,256]{2,1,0:T(8,128)(2,1)S(1)}, u32[]{:S(2)}, u32[]{:S(2)}) collective-permute-start(bf16[13,16,256]{2,1,0:T(8,128)(2,1)} %get-tuple-element.72), channel_id=1, source_target_pairs={{0,4},{1,5},{2,6},{3,7},{4,0},{5,1},{6,2},{7,3},{8,12},{9,13},{10,... | collective-permute-start | bytes 319496 | tf_op jit(solution)/shard_map/ppermute | solution.py:407
  25.1 1.5 %collective-permute-start.8 = (bf16[13,16,256]{2,1,0:T(8,128)(2,1)}, bf16[13,16,256]{2,1,0:T(8,128)(2,1)S(1)}, u32[]{:S(2)}, u32[]{:S(2)}) collective-permute-start(bf16[13,16,256]{2,1,0:T(8,128)(2,1)} %get-tuple-element.73), channel_id=1, source_target_pairs={{0,5},{1,4},{2,7},{3,6},{4,1},{5,0},{6,3},{7,2},{8,13},{9,12},{10,... | collective-permute-start | bytes 319496 | tf_op jit(solution)/shard_map/ppermute | solution.py:407
  26.7 3.3 %collective-permute-start.9 = (bf16[13,16,256]{2,1,0:T(8,128)(2,1)}, bf16[13,16,256]{2,1,0:T(8,128)(2,1)S(1)}, u32[]{:S(2)}, u32[]{:S(2)}) collective-permute-start(bf16[13,16,256]{2,1,0:T(8,128)(2,1)} %get-tuple-element.74), channel_id=1, source_target_pairs={{0,6},{1,7},{2,0},{3,1},{4,2},{5,3},{6,4},{7,5},{8,14},{9,15},{10,... | collective-permute-start | bytes 319496 | tf_op jit(solution)/shard_map/ppermute | solution.py:407
  30.0 1.7 %collective-permute-start.11 = (bf16[13,16,256]{2,1,0:T(8,128)(2,1)}, bf16[13,16,256]{2,1,0:T(8,128)(2,1)S(1)}, u32[]{:S(2)}, u32[]{:S(2)}) collective-permute-start(bf16[13,16,256]{2,1,0:T(8,128)(2,1)} %get-tuple-element.76), channel_id=1, source_target_pairs={{0,3},{1,2},{2,5},{3,4},{4,7},{5,6},{6,1},{7,0},{8,11},{9,10},{10,... | collective-permute-start | bytes 319496 | tf_op jit(solution)/shard_map/ppermute | solution.py:407
  32.9 2.0 %collective-permute-done.9.refs_3_ = bf16[13,16,256]{2,1,0:T(8,128)(2,1)S(1)} collective-permute-done((bf16[13,16,256]{2,1,0:T(8,128)(2,1)}, bf16[13,16,256]{2,1,0:T(8,128)(2,1)S(1)}, u32[]{:S(2)}, u32[]{:S(2)}) %collective-permute-start.9) | collective-permute-done | bytes 106528 | tf_op jit(solution)/shard_map/ppermute | solution.py:407
  35.0 2.2 %collective-permute-done.10.refs_4_ = bf16[13,16,256]{2,1,0:T(8,128)(2,1)S(1)} collective-permute-done((bf16[13,16,256]{2,1,0:T(8,128)(2,1)}, bf16[13,16,256]{2,1,0:T(8,128)(2,1)S(1)}, u32[]{:S(2)}, u32[]{:S(2)}) %collective-permute-start.10) | collective-permute-done | bytes 106528 | tf_op jit(solution)/shard_map/ppermute | solution.py:407
  38.6 1.7 %collective-permute-start.14 = (bf16[128,256]{1,0:T(8,128)(2,1)S(1)}, bf16[128,256]{1,0:T(8,128)(2,1)S(1)}, u32[]{:S(2)}, u32[]{:S(2)}) collective-permute-start(bf16[128,256]{1,0:T(8,128)(2,1)S(1)} %get-tuple-element.91), channel_id=1, source_target_pairs={{0,16},{8,24},{16,0},{24,8},{1,17},{9,25},{17,1},{25,9},{2,18},{10... | collective-permute-start | bytes 196616 | tf_op jit(solution)/shard_map/ppermute | solution.py:422
  41.0 2.6 %collective-permute-start.16 = (bf16[128,256]{1,0:T(8,128)(2,1)S(1)}, bf16[128,256]{1,0:T(8,128)(2,1)S(1)}, u32[]{:S(2)}, u32[]{:S(2)}) collective-permute-start(bf16[128,256]{1,0:T(8,128)(2,1)S(1)} %get-tuple-element.93), channel_id=1, source_target_pairs={{0,24},{8,0},{16,8},{24,16},{1,25},{9,1},{17,9},{25,17},{2,26},{10... | collective-permute-start | bytes 196616 | tf_op jit(solution)/shard_map/ppermute | solution.py:422
  43.6 2.5 %bring_near.3.refs_1_.refs_2_.refs_3_.c_ref = bf16[3,4,3,256,256]{4,3,2,1,0:T(8,128)(2,1)S(1)} custom-call(bf16[3,4,3,256,256]{4,3,2,1,0:T(8,128)(2,1)} %refs_0_.3, bf16[128,256]{1,0:T(8,128)(2,1)S(1)} %get-tuple-element.90.refs_1_), custom_call_target="tpu_custom_call" | custom-call | tf_op jit(solution)/shard_map/bring_near/pallas_call | solution.py:156
  46.2 16.6 %all_to_all.40.parts_ref = bf16[8,16,256]{2,1,0:T(8,128)(2,1)S(1)} all-to-all(bf16[8,16,256]{2,1,0:T(8,128)(2,1)S(1)} %bitcast.21), channel_id=1, replica_groups=mesh['z'=8,'y'=4,'x'=4,'core'=2] {'z'}, dimensions={0} | all-to-all | bytes 131072 | tf_op jit(solution)/shard_map/all_to_all | solution.py:427
  63.0 8.6 %all_to_all.41.refs_0_ = bf16[8,8,256]{2,1,0:T(8,128)(2,1)S(1)} all-to-all(bf16[8,8,256]{2,1,0:T(8,128)(2,1)S(1)} %get-tuple-element.100), channel_id=1, replica_groups=mesh['z'=8,'y'=4,'x'=4,'core'=2] {'core','x'}, dimensions={0} | all-to-all | bytes 65536 | tf_op jit(solution)/shard_map/all_to_all | solution.py:452
  72.4 7.7 %all_to_all.42.refs_1_ = bf16[8,8,256]{2,1,0:T(8,128)(2,1)S(1)} all-to-all(bf16[8,8,256]{2,1,0:T(8,128)(2,1)S(1)} %get-tuple-element.104), channel_id=1, replica_groups=mesh['z'=8,'y'=4,'x'=4,'core'=2] {'core','x'}, dimensions={0} | all-to-all | bytes 65536 | tf_op jit(solution)/shard_map/all_to_all | solution.py:452
  81.0 7.7 %all_to_all.43.refs_2_ = bf16[8,8,256]{2,1,0:T(8,128)(2,1)S(1)} all-to-all(bf16[8,8,256]{2,1,0:T(8,128)(2,1)S(1)} %get-tuple-element.108), channel_id=1, replica_groups=mesh['z'=8,'y'=4,'x'=4,'core'=2] {'core','x'}, dimensions={0} | all-to-all | bytes 65536 | tf_op jit(solution)/shard_map/all_to_all | solution.py:452
  88.7 1.6 %turn.1 = (f32[4,256]{1,0:T(4,128)S(1)}, bf16[8,8,256]{2,1,0:T(8,128)(2,1)S(1)}, f32[128,256]{1,0:T(8,128)S(1)}) custom-call(f32[16,256]{1,0:T(8,128)S(1)} %get-tuple-element.98.g_ref, bf16[16,192]{1,0:T(8,128)(2,1)S(1)} %fusion.6.look_ref, bf16[192,16]{1,0:T(8,128)(2,1)S(1)} %fusion.3.scatter_ref, bf16[8,8,256]{2,1,0:T(8,128)(2,1)S(1)} %all_to_all.41.refs_0_, ...), custom_call_target="tpu_custom_call" | custom-call | tf_op jit(solution)/shard_map/turn/pallas_call | solution.py:466
  90.3 7.7 %all_to_all.44.recv_ref = bf16[8,8,256]{2,1,0:T(8,128)(2,1)S(1)} all-to-all(bf16[8,8,256]{2,1,0:T(8,128)(2,1)S(1)} %get-tuple-element.109), channel_id=1, replica_groups=mesh['z'=8,'y'=4,'x'=4,'core'=2] {'core','x'}, dimensions={0} | all-to-all | bytes 65536 | tf_op jit(solution)/shard_map/all_to_all | solution.py:478
  99.1 7.7 %all_to_all.45.recv_ref = bf16[8,8,256]{2,1,0:T(8,128)(2,1)S(1)} all-to-all(bf16[8,8,256]{2,1,0:T(8,128)(2,1)S(1)} %get-tuple-element.112), channel_id=1, replica_groups=mesh['z'=8,'y'=4,'x'=4,'core'=2] {'core','x'}, dimensions={0} | all-to-all | bytes 65536 | tf_op jit(solution)/shard_map/all_to_all | solution.py:478
  107.9 7.8 %all_to_all.46.recv_ref = bf16[8,8,256]{2,1,0:T(8,128)(2,1)S(1)} all-to-all(bf16[8,8,256]{2,1,0:T(8,128)(2,1)S(1)} %get-tuple-element.115), channel_id=1, replica_groups=mesh['z'=8,'y'=4,'x'=4,'core'=2] {'core','x'}, dimensions={0} | all-to-all | bytes 65536 | tf_op jit(solution)/shard_map/all_to_all | solution.py:478
  115.9 10.8 %all_to_all.47 = bf16[8,16,256]{2,1,0:T(8,128)(2,1)S(1)} all-to-all(bf16[8,16,256]{2,1,0:T(8,128)(2,1)S(1)} %backward_0.1), channel_id=1, replica_groups=mesh['z'=8,'y'=4,'x'=4,'core'=2] {'z'}, dimensions={0} | all-to-all | bytes 131072 | tf_op jit(solution)/shard_map/all_to_all | solution.py:503
  126.7 4.4 %collective-permute-start.18 = (bf16[8,16,256]{2,1,0:T(8,128)(2,1)S(1)}, bf16[8,16,256]{2,1,0:T(8,128)(2,1)S(1)}, u32[]{:S(2)}, u32[]{:S(2)}) collective-permute-start(bf16[8,16,256]{2,1,0:T(8,128)(2,1)S(1)} %all_to_all.47), channel_id=1, source_target_pairs={{0,16},{8,24},{16,0},{24,8},{1,17},{9,25},{17,1},{25,9},{2,18},{10... | collective-permute-start | bytes 196616 | tf_op jit(solution)/shard_map/ppermute | solution.py:504
  131.1 1.5 %collective-permute-done.19 = bf16[8,16,256]{2,1,0:T(8,128)(2,1)S(1)} collective-permute-done((bf16[8,16,256]{2,1,0:T(8,128)(2,1)S(1)}, bf16[8,16,256]{2,1,0:T(8,128)(2,1)S(1)}, u32[]{:S(2)}, u32[]{:S(2)}) %collective-permute-start.19) | collective-permute-done | bytes 65568 | tf_op jit(solution)/shard_map/ppermute | solution.py:504
  132.6 1.4 %collective-permute-done.18 = bf16[8,16,256]{2,1,0:T(8,128)(2,1)S(1)} collective-permute-done((bf16[8,16,256]{2,1,0:T(8,128)(2,1)S(1)}, bf16[8,16,256]{2,1,0:T(8,128)(2,1)S(1)}, u32[]{:S(2)}, u32[]{:S(2)}) %collective-permute-start.18) | collective-permute-done | bytes 65568 | tf_op jit(solution)/shard_map/ppermute | solution.py:504
  134.0 1.3 collective-permute-done.17
  135.4 1.2 convolution_add_fusion
  (52 shorter events, 10.2 us)
Async XLA Ops:
  1.7 1.8 %collective-permute-start = (bf16[16,32,256]{2,1,0:T(8,128)(2,1)S(1)}, bf16[16,32,256]{2,1,0:T(8,128)(2,1)}, u32[]{:S(2)}, u32[]{:S(2)}) collective-permute-start(bf16[16,32,256]{2,1,0:T(8,128)(2,1)S(1)} %bitcast.17), channel_id=1, source_target_pairs={{0,1},{1,0},{2,3},{3,2},{4,5},{5,4},{6,7},{7,6},{8,9},{9,8},{10,11... | collective-permute-start | bytes 786440 | tf_op jit(solution)/shard_map/ppermute | solution.py:314
  1.8 6.9 %collective-permute-start.1 = (bf16[16,32,256]{2,1,0:T(8,128)(2,1)S(1)}, bf16[16,32,256]{2,1,0:T(8,128)(2,1)}, u32[]{:S(2)}, u32[]{:S(2)}) collective-permute-start(bf16[16,32,256]{2,1,0:T(8,128)(2,1)S(1)} %bitcast.18), channel_id=1, source_target_pairs={{0,2},{1,7},{2,4},{3,1},{4,6},{5,3},{6,0},{7,5},{8,10},{9,15},{10,... | collective-permute-start | bytes 786440 | tf_op jit(solution)/shard_map/ppermute | solution.py:311
  3.5 8.0 %collective-permute-start.3 = (bf16[16,32,256]{2,1,0:T(8,128)(2,1)}, bf16[16,32,256]{2,1,0:T(8,128)(2,1)}, u32[]{:S(2)}, u32[]{:S(2)}) collective-permute-start(bf16[16,32,256]{2,1,0:T(8,128)(2,1)} %collective-permute-done.refs_1_.other), channel_id=1, source_target_pairs={{0,2},{1,7},{2,4},{3,1},{4,6},{5,3},{6,0},{7,5},{8,10},{9,15},{10,... | collective-permute-start | bytes 786440 | tf_op jit(solution)/shard_map/ppermute | solution.py:311
  8.8 7.7 %collective-permute-start.2 = (bf16[16,32,256]{2,1,0:T(8,128)(2,1)}, bf16[16,32,256]{2,1,0:T(8,128)(2,1)}, u32[]{:S(2)}, u32[]{:S(2)}) collective-permute-start(bf16[16,32,256]{2,1,0:T(8,128)(2,1)} %collective-permute-done.1.near), channel_id=1, source_target_pairs={{0,2},{1,7},{2,4},{3,1},{4,6},{5,3},{6,0},{7,5},{8,10},{9,15},{10,... | collective-permute-start | bytes 786440 | tf_op jit(solution)/shard_map/ppermute | solution.py:311
  10.7 5.9 %collective-permute-start.5 = (bf16[16,32,256]{2,1,0:T(8,128)(2,1)}, bf16[16,32,256]{2,1,0:T(8,128)(2,1)}, u32[]{:S(2)}, u32[]{:S(2)}) collective-permute-start(bf16[16,32,256]{2,1,0:T(8,128)(2,1)} %collective-permute-done.1.near), channel_id=1, source_target_pairs={{0,1},{1,0},{2,3},{3,2},{4,5},{5,4},{6,7},{7,6},{8,9},{9,8},{10,11... | collective-permute-start | bytes 786440 | tf_op jit(solution)/shard_map/ppermute | solution.py:332
  11.4 5.1 %collective-permute-start.4 = (bf16[16,32,256]{2,1,0:T(8,128)(2,1)}, bf16[16,32,256]{2,1,0:T(8,128)(2,1)}, u32[]{:S(2)}, u32[]{:S(2)}) collective-permute-start(bf16[16,32,256]{2,1,0:T(8,128)(2,1)} %collective-permute-done.3.near_2), channel_id=1, source_target_pairs={{0,1},{1,0},{2,3},{3,2},{4,5},{5,4},{6,7},{7,6},{8,9},{9,8},{10,11... | collective-permute-start | bytes 786440 | tf_op jit(solution)/shard_map/ppermute | solution.py:332
  16.5 2.8 %collective-permute-start.6 = (bf16[16,32,256]{2,1,0:T(8,128)(2,1)}, bf16[16,32,256]{2,1,0:T(8,128)(2,1)S(1)}, u32[]{:S(2)}, u32[]{:S(2)}) collective-permute-start(bf16[16,32,256]{2,1,0:T(8,128)(2,1)} %collective-permute-done.2.far), channel_id=1, source_target_pairs={{0,1},{1,0},{2,3},{3,2},{4,5},{5,4},{6,7},{7,6},{8,9},{9,8},{10,11... | collective-permute-start | bytes 786440 | tf_op jit(solution)/shard_map/ppermute | solution.py:347
  16.5 6.4 %copy-start.2 = (s32[3,4,3]{2,1,0:T(4,128)S(1)}, s32[3,4,3]{2,1,0:T(4,128)}, u32[]{:S(2)}) copy-start(s32[3,4,3]{2,1,0:T(4,128)} %param.15) | copy-start | bytes 436
  23.1 8.6 %collective-permute-start.7 = (bf16[13,16,256]{2,1,0:T(8,128)(2,1)}, bf16[13,16,256]{2,1,0:T(8,128)(2,1)S(1)}, u32[]{:S(2)}, u32[]{:S(2)}) collective-permute-start(bf16[13,16,256]{2,1,0:T(8,128)(2,1)} %get-tuple-element.72), channel_id=1, source_target_pairs={{0,4},{1,5},{2,6},{3,7},{4,0},{5,1},{6,2},{7,3},{8,12},{9,13},{10,... | collective-permute-start | bytes 319496 | tf_op jit(solution)/shard_map/ppermute | solution.py:407
  25.1 7.2 %collective-permute-start.8 = (bf16[13,16,256]{2,1,0:T(8,128)(2,1)}, bf16[13,16,256]{2,1,0:T(8,128)(2,1)S(1)}, u32[]{:S(2)}, u32[]{:S(2)}) collective-permute-start(bf16[13,16,256]{2,1,0:T(8,128)(2,1)} %get-tuple-element.73), channel_id=1, source_target_pairs={{0,5},{1,4},{2,7},{3,6},{4,1},{5,0},{6,3},{7,2},{8,13},{9,12},{10,... | collective-permute-start | bytes 319496 | tf_op jit(solution)/shard_map/ppermute | solution.py:407
  26.7 8.3 %collective-permute-start.9 = (bf16[13,16,256]{2,1,0:T(8,128)(2,1)}, bf16[13,16,256]{2,1,0:T(8,128)(2,1)S(1)}, u32[]{:S(2)}, u32[]{:S(2)}) collective-permute-start(bf16[13,16,256]{2,1,0:T(8,128)(2,1)} %get-tuple-element.74), channel_id=1, source_target_pairs={{0,6},{1,7},{2,0},{3,1},{4,2},{5,3},{6,4},{7,5},{8,14},{9,15},{10,... | collective-permute-start | bytes 319496 | tf_op jit(solution)/shard_map/ppermute | solution.py:407
  30.0 7.1 %collective-permute-start.10 = (bf16[13,16,256]{2,1,0:T(8,128)(2,1)}, bf16[13,16,256]{2,1,0:T(8,128)(2,1)S(1)}, u32[]{:S(2)}, u32[]{:S(2)}) collective-permute-start(bf16[13,16,256]{2,1,0:T(8,128)(2,1)} %get-tuple-element.75), channel_id=1, source_target_pairs={{0,7},{1,6},{2,1},{3,0},{4,3},{5,2},{6,5},{7,4},{8,15},{9,14},{10,... | collective-permute-start | bytes 319496 | tf_op jit(solution)/shard_map/ppermute | solution.py:407
  30.0 7.1 %collective-permute-start.11 = (bf16[13,16,256]{2,1,0:T(8,128)(2,1)}, bf16[13,16,256]{2,1,0:T(8,128)(2,1)S(1)}, u32[]{:S(2)}, u32[]{:S(2)}) collective-permute-start(bf16[13,16,256]{2,1,0:T(8,128)(2,1)} %get-tuple-element.76), channel_id=1, source_target_pairs={{0,3},{1,2},{2,5},{3,4},{4,7},{5,6},{6,1},{7,0},{8,11},{9,10},{10,... | collective-permute-start | bytes 319496 | tf_op jit(solution)/shard_map/ppermute | solution.py:407
  31.7 6.3 %collective-permute-start.12 = (bf16[13,16,256]{2,1,0:T(8,128)(2,1)}, bf16[13,16,256]{2,1,0:T(8,128)(2,1)S(1)}, u32[]{:S(2)}, u32[]{:S(2)}) collective-permute-start(bf16[13,16,256]{2,1,0:T(8,128)(2,1)} %get-tuple-element.77), channel_id=1, source_target_pairs={{0,2},{1,3},{2,4},{3,5},{4,6},{5,7},{6,0},{7,1},{8,10},{9,11},{10,... | collective-permute-start | bytes 319496 | tf_op jit(solution)/shard_map/ppermute | solution.py:407
  32.3 5.7 %collective-permute-start.13 = (bf16[13,16,256]{2,1,0:T(8,128)(2,1)}, bf16[13,16,256]{2,1,0:T(8,128)(2,1)S(1)}, u32[]{:S(2)}, u32[]{:S(2)}) collective-permute-start(bf16[13,16,256]{2,1,0:T(8,128)(2,1)} %get-tuple-element.78), channel_id=1, source_target_pairs={{0,1},{1,0},{2,3},{3,2},{4,5},{5,4},{6,7},{7,6},{8,9},{9,8},{10,11... | collective-permute-start | bytes 319496 | tf_op jit(solution)/shard_map/ppermute | solution.py:407
  38.6 7.5 %collective-permute-start.14 = (bf16[128,256]{1,0:T(8,128)(2,1)S(1)}, bf16[128,256]{1,0:T(8,128)(2,1)S(1)}, u32[]{:S(2)}, u32[]{:S(2)}) collective-permute-start(bf16[128,256]{1,0:T(8,128)(2,1)S(1)} %get-tuple-element.91), channel_id=1, source_target_pairs={{0,16},{8,24},{16,0},{24,8},{1,17},{9,25},{17,1},{25,9},{2,18},{10... | collective-permute-start | bytes 196616 | tf_op jit(solution)/shard_map/ppermute | solution.py:422
  40.3 5.8 %collective-permute-start.15 = (bf16[128,256]{1,0:T(8,128)(2,1)S(1)}, bf16[128,256]{1,0:T(8,128)(2,1)S(1)}, u32[]{:S(2)}, u32[]{:S(2)}) collective-permute-start(bf16[128,256]{1,0:T(8,128)(2,1)S(1)} %get-tuple-element.92), channel_id=1, source_target_pairs={{0,8},{8,16},{16,24},{24,0},{1,9},{9,17},{17,25},{25,1},{2,10},{10... | collective-permute-start | bytes 196616 | tf_op jit(solution)/shard_map/ppermute | solution.py:422
  41.0 5.1 %collective-permute-start.16 = (bf16[128,256]{1,0:T(8,128)(2,1)S(1)}, bf16[128,256]{1,0:T(8,128)(2,1)S(1)}, u32[]{:S(2)}, u32[]{:S(2)}) collective-permute-start(bf16[128,256]{1,0:T(8,128)(2,1)S(1)} %get-tuple-element.93), channel_id=1, source_target_pairs={{0,24},{8,0},{16,8},{24,16},{1,25},{9,1},{17,9},{25,17},{2,26},{10... | collective-permute-start | bytes 196616 | tf_op jit(solution)/shard_map/ppermute | solution.py:422
  43.6 19.3 %copy-start = (bf16[4,4,256,256]{3,2,1,0:T(8,128)(2,1)S(1)}, bf16[4,4,256,256]{3,2,1,0:T(8,128)(2,1)}, u32[]{:S(2)}) copy-start(bf16[4,4,256,256]{3,2,1,0:T(8,128)(2,1)} %d_ref.7) | copy-start | bytes 6291460
  107.8 27.5 %copy-start.1 = (f32[4,4,32,256]{3,2,1,0:T(8,128)S(1)}, f32[4,4,32,256]{3,2,1,0:T(8,128)}, u32[]{:S(2)}) copy-start(f32[4,4,32,256]{3,2,1,0:T(8,128)} %param.12) | copy-start | bytes 1572868
  126.7 5.9 %collective-permute-start.19 = (bf16[8,16,256]{2,1,0:T(8,128)(2,1)S(1)}, bf16[8,16,256]{2,1,0:T(8,128)(2,1)S(1)}, u32[]{:S(2)}, u32[]{:S(2)}) collective-permute-start(bf16[8,16,256]{2,1,0:T(8,128)(2,1)S(1)} %all_to_all.47), channel_id=1, source_target_pairs={{0,8},{8,16},{16,24},{24,0},{1,9},{9,17},{17,25},{25,1},{2,10},{10... | collective-permute-start | bytes 196616 | tf_op jit(solution)/shard_map/ppermute | solution.py:504
  126.7 7.3 %collective-permute-start.18 = (bf16[8,16,256]{2,1,0:T(8,128)(2,1)S(1)}, bf16[8,16,256]{2,1,0:T(8,128)(2,1)S(1)}, u32[]{:S(2)}, u32[]{:S(2)}) collective-permute-start(bf16[8,16,256]{2,1,0:T(8,128)(2,1)S(1)} %all_to_all.47), channel_id=1, source_target_pairs={{0,16},{8,24},{16,0},{24,8},{1,17},{9,25},{17,1},{25,9},{2,18},{10... | collective-permute-start | bytes 196616 | tf_op jit(solution)/shard_map/ppermute | solution.py:504
  131.1 4.3 %collective-permute-start.17 = (bf16[8,16,256]{2,1,0:T(8,128)(2,1)S(1)}, bf16[8,16,256]{2,1,0:T(8,128)(2,1)S(1)}, u32[]{:S(2)}, u32[]{:S(2)}) collective-permute-start(bf16[8,16,256]{2,1,0:T(8,128)(2,1)S(1)} %all_to_all.47), channel_id=1, source_target_pairs={{0,24},{8,0},{16,8},{24,16},{1,25},{9,1},{17,9},{25,17},{2,26},{10... | collective-permute-start | bytes 196616 | tf_op jit(solution)/shard_map/ppermute | solution.py:504

commit v8 on v7

--- a/solution.py
+++ b/solution.py
@@ -61,35 +61,19 @@
         res_ref[plan_ref[2, t]] -= there * dot(x_ref[first + plan_ref[1, t]], a_ref[t], NT)
 
 
-def first_tiles_kernel(core_ref, plan_ref, side_ref, a_ref, own, other, near, near_2, res_ref, x_all, sems):
-    mine = x_all.shape[0] // OWNERS
-    side = 2 * X - 2 - 4 * core_ref[0]
-    copies = [pltpu.make_async_copy(side_ref, res_ref, sems.at[4])]
-    copies[0].start()
-    x_all[...] = jnp.zeros_like(x_all)
-    for i, (block, place) in enumerate(((own, 0), (other, 1), (near, side), (near_2, side + 1))):
-        copies.append(pltpu.make_async_copy(block, x_all.at[pl.ds(place * mine, mine)], sems.at[i]))
-        copies[-1].start()
-    for copy in copies:
-        copy.wait()
-    for t in range(a_ref.shape[0]):
-        q = plan_ref[2, t]
-        res_ref[q] -= dot(x_all[plan_ref[0, t] * mine + plan_ref[1, t]], a_ref[t], NT)
-
-
-def next_tiles_kernel(core_ref, plan_ref, sum_ref, a_ref, far, cross, cross_2, res_ref, x_ref, sems):
-    mine = x_ref.shape[0] // 3
-    sums = pltpu.make_async_copy(sum_ref, res_ref, sems.at[3])
+def tiles_kernel(aways, core_ref, plan_ref, sum_ref, a_ref, *refs):
+    blocks, (res_ref, x_ref, sems) = refs[: len(aways)], refs[len(aways) :]
+    mine = x_ref.shape[0] // len(aways)
+    sums = pltpu.make_async_copy(sum_ref, res_ref, sems.at[len(aways)])
     sums.start()
     copies = []
-    for i, block in enumerate((far, cross, cross_2)):
+    for i, block in enumerate(blocks):
         copies.append(pltpu.make_async_copy(block, x_ref.at[pl.ds(i * mine, mine)], sems.at[i]))
         copies[-1].start()
-    side = 2 + 4 * core_ref[0]
     sums.wait()
-    for i, away in enumerate((2 * CORE, side, side + 1)):
+    for i, (at, per_core) in enumerate(aways):
         copies[i].wait()
-        add_slots(away, i * mine, x_ref, plan_ref, a_ref, res_ref)
+        add_slots(at + per_core * core_ref[0], i * mine, x_ref, plan_ref, a_ref, res_ref)
 
 
 def last_tiles_kernel(plan_ref, note_ref, sum_ref, a_ref, block_ref, res_hbm, own_ref, *refs):
@@ -330,30 +314,29 @@
     first, note, a_near = lax.optimization_barrier((first, note, a_near))
     third = along(first)
     cross_first, cross_second = other(first), other(second)
-    side = in_hbm(right_side)
 
     slot_rows = CAP * K + 16
     core = lax.axis_index("core").reshape(1)
-    part_sum = pl.pallas_call(
-        first_tiles_kernel,
-        out_shape=pltpu.HBM((row_tiles, K, T), F32),
-        in_specs=[SMEM, SMEM, ANY, VMEM] + [ANY] * 4,
-        out_specs=VMEM,
-        scratch_shapes=[pltpu.VMEM((OWNERS * mine, K, T), BF16), pltpu.SemaphoreType.DMA((5,))],
-        compiler_params=PARAMS,
-        name="first_tiles",
-    )(core, plan, side, a_near, e, swapped, first, second)
+    def take_off(name, out_kind, aways, so_far, blocks):
+        n = len(blocks)
+        return pl.pallas_call(
+            functools.partial(tiles_kernel, aways),
+            out_shape=out_kind((row_tiles, K, T), F32),
+            in_specs=[SMEM, SMEM, ANY, VMEM] + [ANY] * n,
+            out_specs=VMEM,
+            scratch_shapes=[pltpu.VMEM((n * mine, K, T), BF16), pltpu.SemaphoreType.DMA((n + 1,))],
+            compiler_params=PARAMS,
+            name=name,
+        )(core, plan, in_hbm(so_far), a_near, *blocks)
+
+    own, rest = 2 * X - 2, 2
+    first_aways = ((0, 0), (1, 0), (own, -4), (own + 1, -4))
+    part_sum = take_off("first_tiles", pltpu.HBM, first_aways, right_side, (e, swapped, first, second))
     third, part_sum = lax.optimization_barrier((third, part_sum))
     cross_third = other(third)
-    part_sum = pl.pallas_call(
-        next_tiles_kernel,
-        out_shape=jax.ShapeDtypeStruct((row_tiles, K, T), F32),
-        in_specs=[SMEM, SMEM, ANY, VMEM] + [ANY] * 3,
-        out_specs=VMEM,
-        scratch_shapes=[pltpu.VMEM((3 * mine, K, T), BF16), pltpu.SemaphoreType.DMA((4,))],
-        compiler_params=PARAMS,
-        name="next_tiles",
-    )(core, plan, in_hbm(part_sum), a_near, third, cross_second, cross_first)
+    next_aways = ((2 * CORE, 0), (rest, 4), (rest + 1, 4))
+    next_blocks = (third, cross_second, cross_first)
+    part_sum = take_off("next_tiles", jax.ShapeDtypeStruct, next_aways, part_sum, next_blocks)
     slots = slot_rows // 16
     residual, *send = pl.pallas_call(
         last_tiles_kernel,

time: 137 us -> 137 us (level)
  no operation moved by 1% of the time
where the time goes in v8:
time: 137 us
  blocking collectives  74.6 us (54%)
  starting transfers between devices  23.5 us (17%)
  Pallas kernels  22.9 us (17%)
  waiting for transfers between devices  11.9 us (9%)
  other arithmetic  1.45 us (1%)
    all_to_all x3, blocking collectives, local(): known.append(lax.all_to_all(out, ('core', 'x'), 0, 0, tiled=True))  24 us
    all_to_all x3, blocking collectives, local(): arrived = lax.all_to_all(out, ('core', 'x'), 0, 0, tiled=True)  23.2 us
    all_to_all x1, blocking collectives, local(): lax.all_to_all(total.astype(BF16).reshape(Z, mine, T), 'z', 0, 0, tiled=T...  16.6 us
    all_to_all x1, blocking collectives, local(): column = lax.all_to_all(change, 'z', 0, 0, tiled=True)  10.8 us
    ppermute x7, starting transfers between devices, local(): recv.append(lax.ppermute(send[away], snode, perm))  9.07 us
    pallas_call x2, Pallas kernels, take_off(): pl.pallas_call(functools.partial(tiles_kernel, aways), out_shape=out_kind...  6.55 us
    ppermute x7, waiting for transfers between devices, local(): recv.append(lax.ppermute(send[away], snode, perm))  5.62 us
    ppermute x3, starting transfers between devices, along(): return lax.ppermute(block, snode, perm)  4.98 us
  transfers between devices with their start and end apart: 20, of which 10 were waited for; matrix products, arithmetic and copies ran while one was open for 0% of the time, Pallas kernels for 9%

profile of v8, /device:TPU:2, one launch (start us, length us, event | category | flops | bytes accessed | tf_op | source)
XLA Modules:
  0.0 136.5 jit_solution(8609549990618959467)
XLA Ops:
  1.8 1.6 %collective-permute-start.1 = (bf16[16,32,256]{2,1,0:T(8,128)(2,1)S(1)}, bf16[16,32,256]{2,1,0:T(8,128)(2,1)}, u32[]{:S(2)}, u32[]{:S(2)}) collective-permute-start(bf16[16,32,256]{2,1,0:T(8,128)(2,1)S(1)} %bitcast.18), channel_id=1, source_target_pairs={{0,2},{1,7},{2,4},{3,1},{4,6},{5,3},{6,0},{7,5},{8,10},{9,15},{10,... | collective-permute-start | bytes 786440 | tf_op jit(solution)/shard_map/ppermute | solution.py:295
  3.5 1.5 %collective-permute-start.3 = (bf16[16,32,256]{2,1,0:T(8,128)(2,1)}, bf16[16,32,256]{2,1,0:T(8,128)(2,1)}, u32[]{:S(2)}, u32[]{:S(2)}) collective-permute-start(bf16[16,32,256]{2,1,0:T(8,128)(2,1)} %collective-permute-done.refs_1_), channel_id=1, source_target_pairs={{0,2},{1,7},{2,4},{3,1},{4,6},{5,3},{6,0},{7,5},{8,10},{9,15},{10,... | collective-permute-start | bytes 786440 | tf_op jit(solution)/shard_map/ppermute | solution.py:295
  5.0 1.9 %bring_near.2.a_ref = bf16[24,256,256]{2,1,0:T(8,128)(2,1)S(1)} custom-call(bf16[24,256,256]{2,1,0:T(8,128)(2,1)} %refs_0_.2, bf16[16,32,256]{2,1,0:T(8,128)(2,1)} %collective-permute-done.refs_1_), custom_call_target="tpu_custom_call" | custom-call | tf_op jit(solution)/shard_map/bring_near/pallas_call | solution.py:140
  6.8 1.9 %plan.1 = (s32[13,24]{1,0:T(8,128)S(1)}, bf16[8,16,256]{2,1,0:T(8,128)(2,1)}) custom-call(s32[1]{0:T(128)} %bitcast.1.here_ref, s32[24]{0:T(128)} %col_ref.1, s32[24]{0:T(128)} %row_ref.1), custom_call_target="tpu_custom_call" | custom-call | tf_op jit(solution)/shard_map/plan/pallas_call | solution.py:301
  8.8 1.9 %collective-permute-start.2 = (bf16[16,32,256]{2,1,0:T(8,128)(2,1)}, bf16[16,32,256]{2,1,0:T(8,128)(2,1)}, u32[]{:S(2)}, u32[]{:S(2)}) collective-permute-start(bf16[16,32,256]{2,1,0:T(8,128)(2,1)} %collective-permute-done.1.refs_2_), channel_id=1, source_target_pairs={{0,2},{1,7},{2,4},{3,1},{4,6},{5,3},{6,0},{7,5},{8,10},{9,15},{10,... | collective-permute-start | bytes 786440 | tf_op jit(solution)/shard_map/ppermute | solution.py:295
  11.4 3.8 %first_tiles.1.sum_ref = f32[8,32,256]{2,1,0:T(8,128)} custom-call(s32[1]{0:T(128)} %bitcast.2.core_ref, s32[13,24]{1,0:T(8,128)S(1)} %get-tuple-element.62.plan_ref, f32[8,32,256]{2,1,0:T(8,128)} %sum_ref.1, bf16[24,256,256]{2,1,0:T(8,128)(2,1)S(1)} %bring_near.2.a_ref, bf16[16,32,256]{2,1,0:T(8,128)(2,1)S(1)} %bitcast.19, ...), custom_call_target="tpu_custom_call" | custom-call | tf_op jit(solution)/shard_map/first_tiles/pallas_call | solution.py:322
  15.2 1.3 collective-permute-done.2.refs_0_
  16.6 2.8 %next_tiles.1.sum_ref = f32[8,32,256]{2,1,0:T(8,128)S(1)} custom-call(s32[1]{0:T(128)} %bitcast.2.core_ref, s32[13,24]{1,0:T(8,128)S(1)} %get-tuple-element.62.plan_ref, f32[8,32,256]{2,1,0:T(8,128)} %first_tiles.1.sum_ref, bf16[24,256,256]{2,1,0:T(8,128)(2,1)S(1)} %bring_near.2.a_ref, bf16[16,32,256]{2,1,0:T(8,128)(2,1)} %collective-permute-done.2.refs_0_, ...), custom_call_target="tpu_custom_call" | custom-call | tf_op jit(solution)/shard_map/next_tiles/pallas_call | solution.py:322
  19.4 3.5 %last_tiles.1 = (f32[8,32,256]{2,1,0:T(8,128)}, bf16[13,16,256]{2,1,0:T(8,128)(2,1)S(1)}, bf16[13,16,256]{2,1,0:T(8,128)(2,1)}, bf16[13,16,256]{2,1,0:T(8,128)(2...) custom-call(s32[13,24]{1,0:T(8,128)S(1)} %get-tuple-element.62.plan_, ...), custom_call_target="tpu_custom_call" | custom-call | tf_op jit(solution)/shard_map/last_tiles/pallas_call | solution.py:341
  23.1 2.0 %collective-permute-start.7 = (bf16[13,16,256]{2,1,0:T(8,128)(2,1)}, bf16[13,16,256]{2,1,0:T(8,128)(2,1)S(1)}, u32[]{:S(2)}, u32[]{:S(2)}) collective-permute-start(bf16[13,16,256]{2,1,0:T(8,128)(2,1)} %get-tuple-element.72), channel_id=1, source_target_pairs={{0,4},{1,5},{2,6},{3,7},{4,0},{5,1},{6,2},{7,3},{8,12},{9,13},{10,... | collective-permute-start | bytes 319496 | tf_op jit(solution)/shard_map/ppermute | solution.py:390
  25.1 1.5 %collective-permute-start.8 = (bf16[13,16,256]{2,1,0:T(8,128)(2,1)}, bf16[13,16,256]{2,1,0:T(8,128)(2,1)S(1)}, u32[]{:S(2)}, u32[]{:S(2)}) collective-permute-start(bf16[13,16,256]{2,1,0:T(8,128)(2,1)} %get-tuple-element.73), channel_id=1, source_target_pairs={{0,5},{1,4},{2,7},{3,6},{4,1},{5,0},{6,3},{7,2},{8,13},{9,12},{10,... | collective-permute-start | bytes 319496 | tf_op jit(solution)/shard_map/ppermute | solution.py:390
  26.7 3.3 %collective-permute-start.9 = (bf16[13,16,256]{2,1,0:T(8,128)(2,1)}, bf16[13,16,256]{2,1,0:T(8,128)(2,1)S(1)}, u32[]{:S(2)}, u32[]{:S(2)}) collective-permute-start(bf16[13,16,256]{2,1,0:T(8,128)(2,1)} %get-tuple-element.74), channel_id=1, source_target_pairs={{0,6},{1,7},{2,0},{3,1},{4,2},{5,3},{6,4},{7,5},{8,14},{9,15},{10,... | collective-permute-start | bytes 319496 | tf_op jit(solution)/shard_map/ppermute | solution.py:390
  30.0 1.7 %collective-permute-start.11 = (bf16[13,16,256]{2,1,0:T(8,128)(2,1)}, bf16[13,16,256]{2,1,0:T(8,128)(2,1)S(1)}, u32[]{:S(2)}, u32[]{:S(2)}) collective-permute-start(bf16[13,16,256]{2,1,0:T(8,128)(2,1)} %get-tuple-element.76), channel_id=1, source_target_pairs={{0,3},{1,2},{2,5},{3,4},{4,7},{5,6},{6,1},{7,0},{8,11},{9,10},{10,... | collective-permute-start | bytes 319496 | tf_op jit(solution)/shard_map/ppermute | solution.py:390
  32.9 2.0 %collective-permute-done.9.refs_3_ = bf16[13,16,256]{2,1,0:T(8,128)(2,1)S(1)} collective-permute-done((bf16[13,16,256]{2,1,0:T(8,128)(2,1)}, bf16[13,16,256]{2,1,0:T(8,128)(2,1)S(1)}, u32[]{:S(2)}, u32[]{:S(2)}) %collective-permute-start.9) | collective-permute-done | bytes 106528 | tf_op jit(solution)/shard_map/ppermute | solution.py:390
  35.0 2.2 %collective-permute-done.10.refs_4_ = bf16[13,16,256]{2,1,0:T(8,128)(2,1)S(1)} collective-permute-done((bf16[13,16,256]{2,1,0:T(8,128)(2,1)}, bf16[13,16,256]{2,1,0:T(8,128)(2,1)S(1)}, u32[]{:S(2)}, u32[]{:S(2)}) %collective-permute-start.10) | collective-permute-done | bytes 106528 | tf_op jit(solution)/shard_map/ppermute | solution.py:390
  38.6 1.7 %collective-permute-start.14 = (bf16[128,256]{1,0:T(8,128)(2,1)S(1)}, bf16[128,256]{1,0:T(8,128)(2,1)S(1)}, u32[]{:S(2)}, u32[]{:S(2)}) collective-permute-start(bf16[128,256]{1,0:T(8,128)(2,1)S(1)} %get-tuple-element.91), channel_id=1, source_target_pairs={{0,16},{8,24},{16,0},{24,8},{1,17},{9,25},{17,1},{25,9},{2,18},{10... | collective-permute-start | bytes 196616 | tf_op jit(solution)/shard_map/ppermute | solution.py:405
  41.0 2.6 %collective-permute-start.16 = (bf16[128,256]{1,0:T(8,128)(2,1)S(1)}, bf16[128,256]{1,0:T(8,128)(2,1)S(1)}, u32[]{:S(2)}, u32[]{:S(2)}) collective-permute-start(bf16[128,256]{1,0:T(8,128)(2,1)S(1)} %get-tuple-element.93), channel_id=1, source_target_pairs={{0,24},{8,0},{16,8},{24,16},{1,25},{9,1},{17,9},{25,17},{2,26},{10... | collective-permute-start | bytes 196616 | tf_op jit(solution)/shard_map/ppermute | solution.py:405
  43.6 2.5 %bring_near.3.refs_1_.refs_2_.refs_3_.c_ref = bf16[3,4,3,256,256]{4,3,2,1,0:T(8,128)(2,1)S(1)} custom-call(bf16[3,4,3,256,256]{4,3,2,1,0:T(8,128)(2,1)} %refs_0_.3, bf16[128,256]{1,0:T(8,128)(2,1)S(1)} %get-tuple-element.90.refs_1_), custom_call_target="tpu_custom_call" | custom-call | tf_op jit(solution)/shard_map/bring_near/pallas_call | solution.py:140
  46.2 16.6 %all_to_all.40.parts_ref = bf16[8,16,256]{2,1,0:T(8,128)(2,1)S(1)} all-to-all(bf16[8,16,256]{2,1,0:T(8,128)(2,1)S(1)} %bitcast.21), channel_id=1, replica_groups=mesh['z'=8,'y'=4,'x'=4,'core'=2] {'z'}, dimensions={0} | all-to-all | bytes 131072 | tf_op jit(solution)/shard_map/all_to_all | solution.py:410
  63.0 8.6 %all_to_all.41.refs_0_ = bf16[8,8,256]{2,1,0:T(8,128)(2,1)S(1)} all-to-all(bf16[8,8,256]{2,1,0:T(8,128)(2,1)S(1)} %get-tuple-element.100), channel_id=1, replica_groups=mesh['z'=8,'y'=4,'x'=4,'core'=2] {'core','x'}, dimensions={0} | all-to-all | bytes 65536 | tf_op jit(solution)/shard_map/all_to_all | solution.py:435
  72.5 7.7 %all_to_all.42.refs_1_ = bf16[8,8,256]{2,1,0:T(8,128)(2,1)S(1)} all-to-all(bf16[8,8,256]{2,1,0:T(8,128)(2,1)S(1)} %get-tuple-element.104), channel_id=1, replica_groups=mesh['z'=8,'y'=4,'x'=4,'core'=2] {'core','x'}, dimensions={0} | all-to-all | bytes 65536 | tf_op jit(solution)/shard_map/all_to_all | solution.py:435
  81.0 7.7 %all_to_all.43.refs_2_ = bf16[8,8,256]{2,1,0:T(8,128)(2,1)S(1)} all-to-all(bf16[8,8,256]{2,1,0:T(8,128)(2,1)S(1)} %get-tuple-element.108), channel_id=1, replica_groups=mesh['z'=8,'y'=4,'x'=4,'core'=2] {'core','x'}, dimensions={0} | all-to-all | bytes 65536 | tf_op jit(solution)/shard_map/all_to_all | solution.py:435
  88.7 1.6 %turn.1 = (f32[4,256]{1,0:T(4,128)S(1)}, bf16[8,8,256]{2,1,0:T(8,128)(2,1)S(1)}, f32[128,256]{1,0:T(8,128)S(1)}) custom-call(f32[16,256]{1,0:T(8,128)S(1)} %get-tuple-element.98.g_ref, bf16[16,192]{1,0:T(8,128)(2,1)S(1)} %fusion.6.look_ref, bf16[192,16]{1,0:T(8,128)(2,1)S(1)} %fusion.3.scatter_ref, bf16[8,8,256]{2,1,0:T(8,128)(2,1)S(1)} %all_to_all.41.refs_0_, ...), custom_call_target="tpu_custom_call" | custom-call | tf_op jit(solution)/shard_map/turn/pallas_call | solution.py:449
  90.3 7.7 %all_to_all.44.recv_ref = bf16[8,8,256]{2,1,0:T(8,128)(2,1)S(1)} all-to-all(bf16[8,8,256]{2,1,0:T(8,128)(2,1)S(1)} %get-tuple-element.109), channel_id=1, replica_groups=mesh['z'=8,'y'=4,'x'=4,'core'=2] {'core','x'}, dimensions={0} | all-to-all | bytes 65536 | tf_op jit(solution)/shard_map/all_to_all | solution.py:461
  99.1 7.7 %all_to_all.45.recv_ref = bf16[8,8,256]{2,1,0:T(8,128)(2,1)S(1)} all-to-all(bf16[8,8,256]{2,1,0:T(8,128)(2,1)S(1)} %get-tuple-element.112), channel_id=1, replica_groups=mesh['z'=8,'y'=4,'x'=4,'core'=2] {'core','x'}, dimensions={0} | all-to-all | bytes 65536 | tf_op jit(solution)/shard_map/all_to_all | solution.py:461
  107.9 7.8 %all_to_all.46.recv_ref = bf16[8,8,256]{2,1,0:T(8,128)(2,1)S(1)} all-to-all(bf16[8,8,256]{2,1,0:T(8,128)(2,1)S(1)} %get-tuple-element.115), channel_id=1, replica_groups=mesh['z'=8,'y'=4,'x'=4,'core'=2] {'core','x'}, dimensions={0} | all-to-all | bytes 65536 | tf_op jit(solution)/shard_map/all_to_all | solution.py:461
  115.9 10.8 %all_to_all.47 = bf16[8,16,256]{2,1,0:T(8,128)(2,1)S(1)} all-to-all(bf16[8,16,256]{2,1,0:T(8,128)(2,1)S(1)} %backward_0.1), channel_id=1, replica_groups=mesh['z'=8,'y'=4,'x'=4,'core'=2] {'z'}, dimensions={0} | all-to-all | bytes 131072 | tf_op jit(solution)/shard_map/all_to_all | solution.py:486
  126.7 4.4 %collective-permute-start.18 = (bf16[8,16,256]{2,1,0:T(8,128)(2,1)S(1)}, bf16[8,16,256]{2,1,0:T(8,128)(2,1)S(1)}, u32[]{:S(2)}, u32[]{:S(2)}) collective-permute-start(bf16[8,16,256]{2,1,0:T(8,128)(2,1)S(1)} %all_to_all.47), channel_id=1, source_target_pairs={{0,16},{8,24},{16,0},{24,8},{1,17},{9,25},{17,1},{25,9},{2,18},{10... | collective-permute-start | bytes 196616 | tf_op jit(solution)/shard_map/ppermute | solution.py:487
  131.2 1.5 %collective-permute-done.19 = bf16[8,16,256]{2,1,0:T(8,128)(2,1)S(1)} collective-permute-done((bf16[8,16,256]{2,1,0:T(8,128)(2,1)S(1)}, bf16[8,16,256]{2,1,0:T(8,128)(2,1)S(1)}, u32[]{:S(2)}, u32[]{:S(2)}) %collective-permute-start.19) | collective-permute-done | bytes 65568 | tf_op jit(solution)/shard_map/ppermute | solution.py:487
  132.6 1.4 %collective-permute-done.18 = bf16[8,16,256]{2,1,0:T(8,128)(2,1)S(1)} collective-permute-done((bf16[8,16,256]{2,1,0:T(8,128)(2,1)S(1)}, bf16[8,16,256]{2,1,0:T(8,128)(2,1)S(1)}, u32[]{:S(2)}, u32[]{:S(2)}) %collective-permute-start.18) | collective-permute-done | bytes 65568 | tf_op jit(solution)/shard_map/ppermute | solution.py:487
  134.0 1.3 collective-permute-done.17
  135.4 1.2 convolution_add_fusion
  (52 shorter events, 10.2 us)
Async XLA Ops:
  1.7 1.8 %collective-permute-start = (bf16[16,32,256]{2,1,0:T(8,128)(2,1)S(1)}, bf16[16,32,256]{2,1,0:T(8,128)(2,1)}, u32[]{:S(2)}, u32[]{:S(2)}) collective-permute-start(bf16[16,32,256]{2,1,0:T(8,128)(2,1)S(1)} %bitcast.17), channel_id=1, source_target_pairs={{0,1},{1,0},{2,3},{3,2},{4,5},{5,4},{6,7},{7,6},{8,9},{9,8},{10,11... | collective-permute-start | bytes 786440 | tf_op jit(solution)/shard_map/ppermute | solution.py:298
  1.8 6.9 %collective-permute-start.1 = (bf16[16,32,256]{2,1,0:T(8,128)(2,1)S(1)}, bf16[16,32,256]{2,1,0:T(8,128)(2,1)}, u32[]{:S(2)}, u32[]{:S(2)}) collective-permute-start(bf16[16,32,256]{2,1,0:T(8,128)(2,1)S(1)} %bitcast.18), channel_id=1, source_target_pairs={{0,2},{1,7},{2,4},{3,1},{4,6},{5,3},{6,0},{7,5},{8,10},{9,15},{10,... | collective-permute-start | bytes 786440 | tf_op jit(solution)/shard_map/ppermute | solution.py:295
  3.5 8.0 %collective-permute-start.3 = (bf16[16,32,256]{2,1,0:T(8,128)(2,1)}, bf16[16,32,256]{2,1,0:T(8,128)(2,1)}, u32[]{:S(2)}, u32[]{:S(2)}) collective-permute-start(bf16[16,32,256]{2,1,0:T(8,128)(2,1)} %collective-permute-done.refs_1_), channel_id=1, source_target_pairs={{0,2},{1,7},{2,4},{3,1},{4,6},{5,3},{6,0},{7,5},{8,10},{9,15},{10,... | collective-permute-start | bytes 786440 | tf_op jit(solution)/shard_map/ppermute | solution.py:295
  8.8 7.7 %collective-permute-start.2 = (bf16[16,32,256]{2,1,0:T(8,128)(2,1)}, bf16[16,32,256]{2,1,0:T(8,128)(2,1)}, u32[]{:S(2)}, u32[]{:S(2)}) collective-permute-start(bf16[16,32,256]{2,1,0:T(8,128)(2,1)} %collective-permute-done.1.refs_2_), channel_id=1, source_target_pairs={{0,2},{1,7},{2,4},{3,1},{4,6},{5,3},{6,0},{7,5},{8,10},{9,15},{10,... | collective-permute-start | bytes 786440 | tf_op jit(solution)/shard_map/ppermute | solution.py:295
  10.7 5.9 %collective-permute-start.5 = (bf16[16,32,256]{2,1,0:T(8,128)(2,1)}, bf16[16,32,256]{2,1,0:T(8,128)(2,1)}, u32[]{:S(2)}, u32[]{:S(2)}) collective-permute-start(bf16[16,32,256]{2,1,0:T(8,128)(2,1)} %collective-permute-done.1.refs_2_), channel_id=1, source_target_pairs={{0,1},{1,0},{2,3},{3,2},{4,5},{5,4},{6,7},{7,6},{8,9},{9,8},{10,11... | collective-permute-start | bytes 786440 | tf_op jit(solution)/shard_map/ppermute | solution.py:316
  11.4 5.1 %collective-permute-start.4 = (bf16[16,32,256]{2,1,0:T(8,128)(2,1)}, bf16[16,32,256]{2,1,0:T(8,128)(2,1)}, u32[]{:S(2)}, u32[]{:S(2)}) collective-permute-start(bf16[16,32,256]{2,1,0:T(8,128)(2,1)} %collective-permute-done.3.refs_3_), channel_id=1, source_target_pairs={{0,1},{1,0},{2,3},{3,2},{4,5},{5,4},{6,7},{7,6},{8,9},{9,8},{10,11... | collective-permute-start | bytes 786440 | tf_op jit(solution)/shard_map/ppermute | solution.py:316
  16.5 2.8 %collective-permute-start.6 = (bf16[16,32,256]{2,1,0:T(8,128)(2,1)}, bf16[16,32,256]{2,1,0:T(8,128)(2,1)S(1)}, u32[]{:S(2)}, u32[]{:S(2)}) collective-permute-start(bf16[16,32,256]{2,1,0:T(8,128)(2,1)} %collective-permute-done.2.refs_0_), channel_id=1, source_target_pairs={{0,1},{1,0},{2,3},{3,2},{4,5},{5,4},{6,7},{7,6},{8,9},{9,8},{10,11... | collective-permute-start | bytes 786440 | tf_op jit(solution)/shard_map/ppermute | solution.py:336
  16.5 6.4 %copy-start.2 = (s32[3,4,3]{2,1,0:T(4,128)S(1)}, s32[3,4,3]{2,1,0:T(4,128)}, u32[]{:S(2)}) copy-start(s32[3,4,3]{2,1,0:T(4,128)} %param.15) | copy-start | bytes 436
  23.1 8.6 %collective-permute-start.7 = (bf16[13,16,256]{2,1,0:T(8,128)(2,1)}, bf16[13,16,256]{2,1,0:T(8,128)(2,1)S(1)}, u32[]{:S(2)}, u32[]{:S(2)}) collective-permute-start(bf16[13,16,256]{2,1,0:T(8,128)(2,1)} %get-tuple-element.72), channel_id=1, source_target_pairs={{0,4},{1,5},{2,6},{3,7},{4,0},{5,1},{6,2},{7,3},{8,12},{9,13},{10,... | collective-permute-start | bytes 319496 | tf_op jit(solution)/shard_map/ppermute | solution.py:390
  25.1 7.2 %collective-permute-start.8 = (bf16[13,16,256]{2,1,0:T(8,128)(2,1)}, bf16[13,16,256]{2,1,0:T(8,128)(2,1)S(1)}, u32[]{:S(2)}, u32[]{:S(2)}) collective-permute-start(bf16[13,16,256]{2,1,0:T(8,128)(2,1)} %get-tuple-element.73), channel_id=1, source_target_pairs={{0,5},{1,4},{2,7},{3,6},{4,1},{5,0},{6,3},{7,2},{8,13},{9,12},{10,... | collective-permute-start | bytes 319496 | tf_op jit(solution)/shard_map/ppermute | solution.py:390
  26.7 8.3 %collective-permute-start.9 = (bf16[13,16,256]{2,1,0:T(8,128)(2,1)}, bf16[13,16,256]{2,1,0:T(8,128)(2,1)S(1)}, u32[]{:S(2)}, u32[]{:S(2)}) collective-permute-start(bf16[13,16,256]{2,1,0:T(8,128)(2,1)} %get-tuple-element.74), channel_id=1, source_target_pairs={{0,6},{1,7},{2,0},{3,1},{4,2},{5,3},{6,4},{7,5},{8,14},{9,15},{10,... | collective-permute-start | bytes 319496 | tf_op jit(solution)/shard_map/ppermute | solution.py:390
  30.0 7.1 %collective-permute-start.10 = (bf16[13,16,256]{2,1,0:T(8,128)(2,1)}, bf16[13,16,256]{2,1,0:T(8,128)(2,1)S(1)}, u32[]{:S(2)}, u32[]{:S(2)}) collective-permute-start(bf16[13,16,256]{2,1,0:T(8,128)(2,1)} %get-tuple-element.75), channel_id=1, source_target_pairs={{0,7},{1,6},{2,1},{3,0},{4,3},{5,2},{6,5},{7,4},{8,15},{9,14},{10,... | collective-permute-start | bytes 319496 | tf_op jit(solution)/shard_map/ppermute | solution.py:390
  30.0 7.1 %collective-permute-start.11 = (bf16[13,16,256]{2,1,0:T(8,128)(2,1)}, bf16[13,16,256]{2,1,0:T(8,128)(2,1)S(1)}, u32[]{:S(2)}, u32[]{:S(2)}) collective-permute-start(bf16[13,16,256]{2,1,0:T(8,128)(2,1)} %get-tuple-element.76), channel_id=1, source_target_pairs={{0,3},{1,2},{2,5},{3,4},{4,7},{5,6},{6,1},{7,0},{8,11},{9,10},{10,... | collective-permute-start | bytes 319496 | tf_op jit(solution)/shard_map/ppermute | solution.py:390
  31.7 6.3 %collective-permute-start.12 = (bf16[13,16,256]{2,1,0:T(8,128)(2,1)}, bf16[13,16,256]{2,1,0:T(8,128)(2,1)S(1)}, u32[]{:S(2)}, u32[]{:S(2)}) collective-permute-start(bf16[13,16,256]{2,1,0:T(8,128)(2,1)} %get-tuple-element.77), channel_id=1, source_target_pairs={{0,2},{1,3},{2,4},{3,5},{4,6},{5,7},{6,0},{7,1},{8,10},{9,11},{10,... | collective-permute-start | bytes 319496 | tf_op jit(solution)/shard_map/ppermute | solution.py:390
  32.3 5.7 %collective-permute-start.13 = (bf16[13,16,256]{2,1,0:T(8,128)(2,1)}, bf16[13,16,256]{2,1,0:T(8,128)(2,1)S(1)}, u32[]{:S(2)}, u32[]{:S(2)}) collective-permute-start(bf16[13,16,256]{2,1,0:T(8,128)(2,1)} %get-tuple-element.78), channel_id=1, source_target_pairs={{0,1},{1,0},{2,3},{3,2},{4,5},{5,4},{6,7},{7,6},{8,9},{9,8},{10,11... | collective-permute-start | bytes 319496 | tf_op jit(solution)/shard_map/ppermute | solution.py:390
  38.6 7.5 %collective-permute-start.14 = (bf16[128,256]{1,0:T(8,128)(2,1)S(1)}, bf16[128,256]{1,0:T(8,128)(2,1)S(1)}, u32[]{:S(2)}, u32[]{:S(2)}) collective-permute-start(bf16[128,256]{1,0:T(8,128)(2,1)S(1)} %get-tuple-element.91), channel_id=1, source_target_pairs={{0,16},{8,24},{16,0},{24,8},{1,17},{9,25},{17,1},{25,9},{2,18},{10... | collective-permute-start | bytes 196616 | tf_op jit(solution)/shard_map/ppermute | solution.py:405
  40.3 5.8 %collective-permute-start.15 = (bf16[128,256]{1,0:T(8,128)(2,1)S(1)}, bf16[128,256]{1,0:T(8,128)(2,1)S(1)}, u32[]{:S(2)}, u32[]{:S(2)}) collective-permute-start(bf16[128,256]{1,0:T(8,128)(2,1)S(1)} %get-tuple-element.92), channel_id=1, source_target_pairs={{0,8},{8,16},{16,24},{24,0},{1,9},{9,17},{17,25},{25,1},{2,10},{10... | collective-permute-start | bytes 196616 | tf_op jit(solution)/shard_map/ppermute | solution.py:405
  41.0 5.1 %collective-permute-start.16 = (bf16[128,256]{1,0:T(8,128)(2,1)S(1)}, bf16[128,256]{1,0:T(8,128)(2,1)S(1)}, u32[]{:S(2)}, u32[]{:S(2)}) collective-permute-start(bf16[128,256]{1,0:T(8,128)(2,1)S(1)} %get-tuple-element.93), channel_id=1, source_target_pairs={{0,24},{8,0},{16,8},{24,16},{1,25},{9,1},{17,9},{25,17},{2,26},{10... | collective-permute-start | bytes 196616 | tf_op jit(solution)/shard_map/ppermute | solution.py:405
  43.6 19.3 %copy-start = (bf16[4,4,256,256]{3,2,1,0:T(8,128)(2,1)S(1)}, bf16[4,4,256,256]{3,2,1,0:T(8,128)(2,1)}, u32[]{:S(2)}) copy-start(bf16[4,4,256,256]{3,2,1,0:T(8,128)(2,1)} %d_ref.7) | copy-start | bytes 6291460
  107.9 27.5 %copy-start.1 = (f32[4,4,32,256]{3,2,1,0:T(8,128)S(1)}, f32[4,4,32,256]{3,2,1,0:T(8,128)}, u32[]{:S(2)}) copy-start(f32[4,4,32,256]{3,2,1,0:T(8,128)} %param.12) | copy-start | bytes 1572868
  126.7 5.9 %collective-permute-start.19 = (bf16[8,16,256]{2,1,0:T(8,128)(2,1)S(1)}, bf16[8,16,256]{2,1,0:T(8,128)(2,1)S(1)}, u32[]{:S(2)}, u32[]{:S(2)}) collective-permute-start(bf16[8,16,256]{2,1,0:T(8,128)(2,1)S(1)} %all_to_all.47), channel_id=1, source_target_pairs={{0,8},{8,16},{16,24},{24,0},{1,9},{9,17},{17,25},{25,1},{2,10},{10... | collective-permute-start | bytes 196616 | tf_op jit(solution)/shard_map/ppermute | solution.py:487
  126.7 7.3 %collective-permute-start.18 = (bf16[8,16,256]{2,1,0:T(8,128)(2,1)S(1)}, bf16[8,16,256]{2,1,0:T(8,128)(2,1)S(1)}, u32[]{:S(2)}, u32[]{:S(2)}) collective-permute-start(bf16[8,16,256]{2,1,0:T(8,128)(2,1)S(1)} %all_to_all.47), channel_id=1, source_target_pairs={{0,16},{8,24},{16,0},{24,8},{1,17},{9,25},{17,1},{25,9},{2,18},{10... | collective-permute-start | bytes 196616 | tf_op jit(solution)/shard_map/ppermute | solution.py:487
  131.1 4.3 %collective-permute-start.17 = (bf16[8,16,256]{2,1,0:T(8,128)(2,1)S(1)}, bf16[8,16,256]{2,1,0:T(8,128)(2,1)S(1)}, u32[]{:S(2)}, u32[]{:S(2)}) collective-permute-start(bf16[8,16,256]{2,1,0:T(8,128)(2,1)S(1)} %all_to_all.47), channel_id=1, source_target_pairs={{0,24},{8,0},{16,8},{24,16},{1,25},{9,1},{17,9},{25,17},{2,26},{10... | collective-permute-start | bytes 196616 | tf_op jit(solution)/shard_map/ppermute | solution.py:487

commit v9 on v8

--- a/solution.py
+++ b/solution.py
@@ -36,7 +36,8 @@
         count_ref[o] = 0
     for o in range(OWNERS):
         for i in range(CAP):
-            plan_ref[5 + o, i] = -1
+            plan_ref[5 + o, i] = 0
+            plan_ref[5 + OWNERS + o, i] = -1
     for t in range(col_ref.shape[0]):
         c = col_ref[t]
         level, owner, inner = c // (sn * OWNERS), (c // sn) % OWNERS, c % sn
@@ -49,6 +50,7 @@
         plan_ref[3, t] = away
         plan_ref[4, t] = rank
         plan_ref[5 + away, rank] = t
+        plan_ref[5 + OWNERS + away, rank] = level * sn + inner
         mark = (level * sn + inner + 1).astype(F32)
         note[away, pl.ds(rank, 1), :] = jnp.full((1, note.shape[2]), mark, F32)
     note_ref[...] = note[...].astype(BF16)
@@ -56,14 +58,15 @@
 
 def add_slots(away, first, x_ref, plan_ref, a_ref, res_ref):
     for i in range(CAP):
-        t = jnp.maximum(plan_ref[5 + away, i], 0)
-        there = (plan_ref[5 + away, i] >= 0).astype(F32)
-        res_ref[plan_ref[2, t]] -= there * dot(x_ref[first + plan_ref[1, t]], a_ref[t], NT)
+        t, spot = plan_ref[5 + away, i], plan_ref[5 + OWNERS + away, i]
+        at = jnp.where(spot >= 0, first + spot, x_ref.shape[0] - 1)
+        res_ref[plan_ref[2, t]] -= dot(x_ref[at], a_ref[t], NT)
 
 
 def tiles_kernel(aways, core_ref, plan_ref, sum_ref, a_ref, *refs):
     blocks, (res_ref, x_ref, sems) = refs[: len(aways)], refs[len(aways) :]
     mine = x_ref.shape[0] // len(aways)
+    x_ref[x_ref.shape[0] - 1] = jnp.zeros(x_ref.shape[1:], BF16)
     sums = pltpu.make_async_copy(sum_ref, res_ref, sems.at[len(aways)])
     sums.start()
     copies = []
@@ -80,8 +83,10 @@
     out_refs, (send_ref, x_last, res_ref, low_ref, sems, note_sems) = refs[: OWNERS - 1], refs[OWNERS - 1 :]
     half = x_last.shape[1] // 2
     per = own_ref.shape[0]
-    copies = [pltpu.make_async_copy(block_ref, x_last, sems.at[0])]
+    mine = block_ref.shape[0]
+    copies = [pltpu.make_async_copy(block_ref, x_last.at[pl.ds(0, mine)], sems.at[0])]
     copies[0].start()
+    x_last[mine] = jnp.zeros(x_last.shape[1:], BF16)
     send_ref[...] = jnp.zeros_like(send_ref)
     for o in range(OWNERS):
         copies.append(pltpu.make_async_copy(note_ref.at[o], send_ref.at[(o + 1) * per - 1], note_sems.at[o]))
@@ -301,7 +306,7 @@
     plan, note = pl.pallas_call(
         functools.partial(plan_kernel, sn),
         out_shape=(
-            jax.ShapeDtypeStruct((5 + OWNERS, tiles), jnp.int32),
+            jax.ShapeDtypeStruct((5 + 2 * OWNERS, tiles), jnp.int32),
             pltpu.HBM((OWNERS, 16, T), BF16),
         ),
         in_specs=[SMEM, SMEM, SMEM],
@@ -324,7 +329,7 @@
             out_shape=out_kind((row_tiles, K, T), F32),
             in_specs=[SMEM, SMEM, ANY, VMEM] + [ANY] * n,
             out_specs=VMEM,
-            scratch_shapes=[pltpu.VMEM((n * mine, K, T), BF16), pltpu.SemaphoreType.DMA((n + 1,))],
+            scratch_shapes=[pltpu.VMEM((n * mine + 1, K, T), BF16), pltpu.SemaphoreType.DMA((n + 1,))],
             compiler_params=PARAMS,
             name=name,
         )(core, plan, in_hbm(so_far), a_near, *blocks)
@@ -349,7 +354,7 @@
         out_specs=(ANY, VMEM) + (ANY,) * (OWNERS - 1),
         scratch_shapes=[
             pltpu.VMEM((OWNERS * slots, 16, T), BF16),
-            pltpu.VMEM((mine, K, T), BF16),
+            pltpu.VMEM((mine + 1, K, T), BF16),
             pltpu.VMEM((row_tiles, K, T), F32),
             pltpu.VMEM((row_tiles, K, T), BF16),
             pltpu.SemaphoreType.DMA((OWNERS,)),

time: 137 us -> 137 us (level)
  transfers between devices with their start and end apart: 20 -> 20, of which waited for: 10 -> 10; matrix products, arithmetic and copies ran while one was open for 0% -> 0% of each run, Pallas kernels for 9% -> 10%
where the time goes in v9:
time: 137 us
  blocking collectives  74.6 us (54%)
  starting transfers between devices  23.5 us (17%)
  Pallas kernels  23.2 us (17%)
  waiting for transfers between devices  11.8 us (9%)
  other arithmetic  1.45 us (1%)
    all_to_all x3, blocking collectives, local(): known.append(lax.all_to_all(out, ('core', 'x'), 0, 0, tiled=True))  24 us
    all_to_all x3, blocking collectives, local(): arrived = lax.all_to_all(out, ('core', 'x'), 0, 0, tiled=True)  23.2 us
    all_to_all x1, blocking collectives, local(): lax.all_to_all(total.astype(BF16).reshape(Z, mine, T), 'z', 0, 0, tiled=T...  16.6 us
    all_to_all x1, blocking collectives, local(): column = lax.all_to_all(change, 'z', 0, 0, tiled=True)  10.8 us
    ppermute x7, starting transfers between devices, local(): recv.append(lax.ppermute(send[away], snode, perm))  9.06 us
    pallas_call x2, Pallas kernels, take_off(): pl.pallas_call(functools.partial(tiles_kernel, aways), out_shape=out_kind...  6.67 us
    ppermute x7, waiting for transfers between devices, local(): recv.append(lax.ppermute(send[away], snode, perm))  5.63 us
    ppermute x3, starting transfers between devices, local(): arrived = [lax.ppermute(part[s], 'y', shift(Y, s)) for s in (2, 1, 3)]  5 us
  transfers between devices with their start and end apart: 20, of which 10 were waited for; matrix products, arithmetic and copies ran while one was open for 0% of the time, Pallas kernels for 10%

profile of v9, /device:TPU:2, one launch (start us, length us, event | category | flops | bytes accessed | tf_op | source)
XLA Modules:
  0.0 136.7 jit_solution(15254777267146582874)
XLA Ops:
  1.8 1.6 %collective-permute-start.1 = (bf16[16,32,256]{2,1,0:T(8,128)(2,1)S(1)}, bf16[16,32,256]{2,1,0:T(8,128)(2,1)}, u32[]{:S(2)}, u32[]{:S(2)}) collective-permute-start(bf16[16,32,256]{2,1,0:T(8,128)(2,1)S(1)} %bitcast.18), channel_id=1, source_target_pairs={{0,2},{1,7},{2,4},{3,1},{4,6},{5,3},{6,0},{7,5},{8,10},{9,15},{10,... | collective-permute-start | bytes 786440 | tf_op jit(solution)/shard_map/ppermute | solution.py:300
  3.5 1.5 %collective-permute-start.3 = (bf16[16,32,256]{2,1,0:T(8,128)(2,1)}, bf16[16,32,256]{2,1,0:T(8,128)(2,1)}, u32[]{:S(2)}, u32[]{:S(2)}) collective-permute-start(bf16[16,32,256]{2,1,0:T(8,128)(2,1)} %collective-permute-done.refs_1_), channel_id=1, source_target_pairs={{0,2},{1,7},{2,4},{3,1},{4,6},{5,3},{6,0},{7,5},{8,10},{9,15},{10,... | collective-permute-start | bytes 786440 | tf_op jit(solution)/shard_map/ppermute | solution.py:300
  5.0 1.9 %bring_near.2.a_ref = bf16[24,256,256]{2,1,0:T(8,128)(2,1)S(1)} custom-call(bf16[24,256,256]{2,1,0:T(8,128)(2,1)} %refs_0_.2, bf16[16,32,256]{2,1,0:T(8,128)(2,1)} %collective-permute-done.refs_1_), custom_call_target="tpu_custom_call" | custom-call | tf_op jit(solution)/shard_map/bring_near/pallas_call | solution.py:145
  6.8 2.0 %plan.1 = (s32[21,24]{1,0:T(8,128)S(1)}, bf16[8,16,256]{2,1,0:T(8,128)(2,1)}) custom-call(s32[1]{0:T(128)} %bitcast.1.here_ref, s32[24]{0:T(128)} %col_ref.1, s32[24]{0:T(128)} %row_ref.1), custom_call_target="tpu_custom_call" | custom-call | tf_op jit(solution)/shard_map/plan/pallas_call | solution.py:306
  8.9 1.9 %collective-permute-start.2 = (bf16[16,32,256]{2,1,0:T(8,128)(2,1)}, bf16[16,32,256]{2,1,0:T(8,128)(2,1)}, u32[]{:S(2)}, u32[]{:S(2)}) collective-permute-start(bf16[16,32,256]{2,1,0:T(8,128)(2,1)} %collective-permute-done.1.refs_2_), channel_id=1, source_target_pairs={{0,2},{1,7},{2,4},{3,1},{4,6},{5,3},{6,0},{7,5},{8,10},{9,15},{10,... | collective-permute-start | bytes 786440 | tf_op jit(solution)/shard_map/ppermute | solution.py:300
  11.4 3.8 %first_tiles.1.sum_ref = f32[8,32,256]{2,1,0:T(8,128)} custom-call(s32[1]{0:T(128)} %bitcast.2.core_ref, s32[21,24]{1,0:T(8,128)S(1)} %get-tuple-element.62.plan_ref, f32[8,32,256]{2,1,0:T(8,128)} %sum_ref.1, bf16[24,256,256]{2,1,0:T(8,128)(2,1)S(1)} %bring_near.2.a_ref, bf16[16,32,256]{2,1,0:T(8,128)(2,1)S(1)} %bitcast.19, ...), custom_call_target="tpu_custom_call" | custom-call | tf_op jit(solution)/shard_map/first_tiles/pallas_call | solution.py:327
  15.3 1.2 collective-permute-done.2.refs_0_
  16.6 2.8 %next_tiles.1.sum_ref = f32[8,32,256]{2,1,0:T(8,128)S(1)} custom-call(s32[1]{0:T(128)} %bitcast.2.core_ref, s32[21,24]{1,0:T(8,128)S(1)} %get-tuple-element.62.plan_ref, f32[8,32,256]{2,1,0:T(8,128)} %first_tiles.1.sum_ref, bf16[24,256,256]{2,1,0:T(8,128)(2,1)S(1)} %bring_near.2.a_ref, bf16[16,32,256]{2,1,0:T(8,128)(2,1)} %collective-permute-done.2.refs_0_, ...), custom_call_target="tpu_custom_call" | custom-call | tf_op jit(solution)/shard_map/next_tiles/pallas_call | solution.py:327
  19.4 3.6 %last_tiles.1 = (f32[8,32,256]{2,1,0:T(8,128)}, bf16[13,16,256]{2,1,0:T(8,128)(2,1)S(1)}, bf16[13,16,256]{2,1,0:T(8,128)(2,1)}, bf16[13,16,256]{2,1,0:T(8,128)(2...) custom-call(s32[21,24]{1,0:T(8,128)S(1)} %get-tuple-element.62.plan_, ...), custom_call_target="tpu_custom_call" | custom-call | tf_op jit(solution)/shard_map/last_tiles/pallas_call | solution.py:346
  23.3 2.1 %collective-permute-start.7 = (bf16[13,16,256]{2,1,0:T(8,128)(2,1)}, bf16[13,16,256]{2,1,0:T(8,128)(2,1)S(1)}, u32[]{:S(2)}, u32[]{:S(2)}) collective-permute-start(bf16[13,16,256]{2,1,0:T(8,128)(2,1)} %get-tuple-element.72), channel_id=1, source_target_pairs={{0,4},{1,5},{2,6},{3,7},{4,0},{5,1},{6,2},{7,3},{8,12},{9,13},{10,... | collective-permute-start | bytes 319496 | tf_op jit(solution)/shard_map/ppermute | solution.py:395
  25.3 1.4 %collective-permute-start.8 = (bf16[13,16,256]{2,1,0:T(8,128)(2,1)}, bf16[13,16,256]{2,1,0:T(8,128)(2,1)S(1)}, u32[]{:S(2)}, u32[]{:S(2)}) collective-permute-start(bf16[13,16,256]{2,1,0:T(8,128)(2,1)} %get-tuple-element.73), channel_id=1, source_target_pairs={{0,5},{1,4},{2,7},{3,6},{4,1},{5,0},{6,3},{7,2},{8,13},{9,12},{10,... | collective-permute-start | bytes 319496 | tf_op jit(solution)/shard_map/ppermute | solution.py:395
  26.8 3.3 %collective-permute-start.9 = (bf16[13,16,256]{2,1,0:T(8,128)(2,1)}, bf16[13,16,256]{2,1,0:T(8,128)(2,1)S(1)}, u32[]{:S(2)}, u32[]{:S(2)}) collective-permute-start(bf16[13,16,256]{2,1,0:T(8,128)(2,1)} %get-tuple-element.74), channel_id=1, source_target_pairs={{0,6},{1,7},{2,0},{3,1},{4,2},{5,3},{6,4},{7,5},{8,14},{9,15},{10,... | collective-permute-start | bytes 319496 | tf_op jit(solution)/shard_map/ppermute | solution.py:395
  30.1 1.7 %collective-permute-start.11 = (bf16[13,16,256]{2,1,0:T(8,128)(2,1)}, bf16[13,16,256]{2,1,0:T(8,128)(2,1)S(1)}, u32[]{:S(2)}, u32[]{:S(2)}) collective-permute-start(bf16[13,16,256]{2,1,0:T(8,128)(2,1)} %get-tuple-element.76), channel_id=1, source_target_pairs={{0,3},{1,2},{2,5},{3,4},{4,7},{5,6},{6,1},{7,0},{8,11},{9,10},{10,... | collective-permute-start | bytes 319496 | tf_op jit(solution)/shard_map/ppermute | solution.py:395
  33.1 2.0 %collective-permute-done.9.refs_3_ = bf16[13,16,256]{2,1,0:T(8,128)(2,1)S(1)} collective-permute-done((bf16[13,16,256]{2,1,0:T(8,128)(2,1)}, bf16[13,16,256]{2,1,0:T(8,128)(2,1)S(1)}, u32[]{:S(2)}, u32[]{:S(2)}) %collective-permute-start.9) | collective-permute-done | bytes 106528 | tf_op jit(solution)/shard_map/ppermute | solution.py:395
  35.1 2.2 %collective-permute-done.10.refs_4_ = bf16[13,16,256]{2,1,0:T(8,128)(2,1)S(1)} collective-permute-done((bf16[13,16,256]{2,1,0:T(8,128)(2,1)}, bf16[13,16,256]{2,1,0:T(8,128)(2,1)S(1)}, u32[]{:S(2)}, u32[]{:S(2)}) %collective-permute-start.10) | collective-permute-done | bytes 106528 | tf_op jit(solution)/shard_map/ppermute | solution.py:395
  38.7 1.8 %collective-permute-start.14 = (bf16[128,256]{1,0:T(8,128)(2,1)S(1)}, bf16[128,256]{1,0:T(8,128)(2,1)S(1)}, u32[]{:S(2)}, u32[]{:S(2)}) collective-permute-start(bf16[128,256]{1,0:T(8,128)(2,1)S(1)} %get-tuple-element.91), channel_id=1, source_target_pairs={{0,16},{8,24},{16,0},{24,8},{1,17},{9,25},{17,1},{25,9},{2,18},{10... | collective-permute-start | bytes 196616 | tf_op jit(solution)/shard_map/ppermute | solution.py:410
  41.2 2.6 %collective-permute-start.16 = (bf16[128,256]{1,0:T(8,128)(2,1)S(1)}, bf16[128,256]{1,0:T(8,128)(2,1)S(1)}, u32[]{:S(2)}, u32[]{:S(2)}) collective-permute-start(bf16[128,256]{1,0:T(8,128)(2,1)S(1)} %get-tuple-element.93), channel_id=1, source_target_pairs={{0,24},{8,0},{16,8},{24,16},{1,25},{9,1},{17,9},{25,17},{2,26},{10... | collective-permute-start | bytes 196616 | tf_op jit(solution)/shard_map/ppermute | solution.py:410
  43.7 2.5 %bring_near.3.refs_1_.refs_2_.refs_3_.c_ref = bf16[3,4,3,256,256]{4,3,2,1,0:T(8,128)(2,1)S(1)} custom-call(bf16[3,4,3,256,256]{4,3,2,1,0:T(8,128)(2,1)} %refs_0_.3, bf16[128,256]{1,0:T(8,128)(2,1)S(1)} %get-tuple-element.90.refs_1_), custom_call_target="tpu_custom_call" | custom-call | tf_op jit(solution)/shard_map/bring_near/pallas_call | solution.py:145
  46.4 16.6 %all_to_all.40.parts_ref = bf16[8,16,256]{2,1,0:T(8,128)(2,1)S(1)} all-to-all(bf16[8,16,256]{2,1,0:T(8,128)(2,1)S(1)} %bitcast.21), channel_id=1, replica_groups=mesh['z'=8,'y'=4,'x'=4,'core'=2] {'z'}, dimensions={0} | all-to-all | bytes 131072 | tf_op jit(solution)/shard_map/all_to_all | solution.py:415
  63.2 8.6 %all_to_all.41.refs_0_ = bf16[8,8,256]{2,1,0:T(8,128)(2,1)S(1)} all-to-all(bf16[8,8,256]{2,1,0:T(8,128)(2,1)S(1)} %get-tuple-element.100), channel_id=1, replica_groups=mesh['z'=8,'y'=4,'x'=4,'core'=2] {'core','x'}, dimensions={0} | all-to-all | bytes 65536 | tf_op jit(solution)/shard_map/all_to_all | solution.py:440
  72.6 7.7 %all_to_all.42.refs_1_ = bf16[8,8,256]{2,1,0:T(8,128)(2,1)S(1)} all-to-all(bf16[8,8,256]{2,1,0:T(8,128)(2,1)S(1)} %get-tuple-element.104), channel_id=1, replica_groups=mesh['z'=8,'y'=4,'x'=4,'core'=2] {'core','x'}, dimensions={0} | all-to-all | bytes 65536 | tf_op jit(solution)/shard_map/all_to_all | solution.py:440
  81.2 7.7 %all_to_all.43.refs_2_ = bf16[8,8,256]{2,1,0:T(8,128)(2,1)S(1)} all-to-all(bf16[8,8,256]{2,1,0:T(8,128)(2,1)S(1)} %get-tuple-element.108), channel_id=1, replica_groups=mesh['z'=8,'y'=4,'x'=4,'core'=2] {'core','x'}, dimensions={0} | all-to-all | bytes 65536 | tf_op jit(solution)/shard_map/all_to_all | solution.py:440
  88.9 1.6 %turn.1 = (f32[4,256]{1,0:T(4,128)S(1)}, bf16[8,8,256]{2,1,0:T(8,128)(2,1)S(1)}, f32[128,256]{1,0:T(8,128)S(1)}) custom-call(f32[16,256]{1,0:T(8,128)S(1)} %get-tuple-element.98.g_ref, bf16[16,192]{1,0:T(8,128)(2,1)S(1)} %fusion.6.look_ref, bf16[192,16]{1,0:T(8,128)(2,1)S(1)} %fusion.3.scatter_ref, bf16[8,8,256]{2,1,0:T(8,128)(2,1)S(1)} %all_to_all.41.refs_0_, ...), custom_call_target="tpu_custom_call" | custom-call | tf_op jit(solution)/shard_map/turn/pallas_call | solution.py:454
  90.5 7.7 %all_to_all.44.recv_ref = bf16[8,8,256]{2,1,0:T(8,128)(2,1)S(1)} all-to-all(bf16[8,8,256]{2,1,0:T(8,128)(2,1)S(1)} %get-tuple-element.109), channel_id=1, replica_groups=mesh['z'=8,'y'=4,'x'=4,'core'=2] {'core','x'}, dimensions={0} | all-to-all | bytes 65536 | tf_op jit(solution)/shard_map/all_to_all | solution.py:466
  99.3 7.7 %all_to_all.45.recv_ref = bf16[8,8,256]{2,1,0:T(8,128)(2,1)S(1)} all-to-all(bf16[8,8,256]{2,1,0:T(8,128)(2,1)S(1)} %get-tuple-element.112), channel_id=1, replica_groups=mesh['z'=8,'y'=4,'x'=4,'core'=2] {'core','x'}, dimensions={0} | all-to-all | bytes 65536 | tf_op jit(solution)/shard_map/all_to_all | solution.py:466
  108.0 7.8 %all_to_all.46.recv_ref = bf16[8,8,256]{2,1,0:T(8,128)(2,1)S(1)} all-to-all(bf16[8,8,256]{2,1,0:T(8,128)(2,1)S(1)} %get-tuple-element.115), channel_id=1, replica_groups=mesh['z'=8,'y'=4,'x'=4,'core'=2] {'core','x'}, dimensions={0} | all-to-all | bytes 65536 | tf_op jit(solution)/shard_map/all_to_all | solution.py:466
  116.1 10.8 %all_to_all.47 = bf16[8,16,256]{2,1,0:T(8,128)(2,1)S(1)} all-to-all(bf16[8,16,256]{2,1,0:T(8,128)(2,1)S(1)} %backward_0.1), channel_id=1, replica_groups=mesh['z'=8,'y'=4,'x'=4,'core'=2] {'z'}, dimensions={0} | all-to-all | bytes 131072 | tf_op jit(solution)/shard_map/all_to_all | solution.py:491
  126.9 4.4 %collective-permute-start.18 = (bf16[8,16,256]{2,1,0:T(8,128)(2,1)S(1)}, bf16[8,16,256]{2,1,0:T(8,128)(2,1)S(1)}, u32[]{:S(2)}, u32[]{:S(2)}) collective-permute-start(bf16[8,16,256]{2,1,0:T(8,128)(2,1)S(1)} %all_to_all.47), channel_id=1, source_target_pairs={{0,16},{8,24},{16,0},{24,8},{1,17},{9,25},{17,1},{25,9},{2,18},{10... | collective-permute-start | bytes 196616 | tf_op jit(solution)/shard_map/ppermute | solution.py:492
  131.3 1.5 %collective-permute-done.19 = bf16[8,16,256]{2,1,0:T(8,128)(2,1)S(1)} collective-permute-done((bf16[8,16,256]{2,1,0:T(8,128)(2,1)S(1)}, bf16[8,16,256]{2,1,0:T(8,128)(2,1)S(1)}, u32[]{:S(2)}, u32[]{:S(2)}) %collective-permute-start.19) | collective-permute-done | bytes 65568 | tf_op jit(solution)/shard_map/ppermute | solution.py:492
  132.8 1.4 %collective-permute-done.18 = bf16[8,16,256]{2,1,0:T(8,128)(2,1)S(1)} collective-permute-done((bf16[8,16,256]{2,1,0:T(8,128)(2,1)S(1)}, bf16[8,16,256]{2,1,0:T(8,128)(2,1)S(1)}, u32[]{:S(2)}, u32[]{:S(2)}) %collective-permute-start.18) | collective-permute-done | bytes 65568 | tf_op jit(solution)/shard_map/ppermute | solution.py:492
  134.2 1.3 collective-permute-done.17
  135.5 1.2 convolution_add_fusion
  (52 shorter events, 10.1 us)
Async XLA Ops:
  1.7 1.8 %collective-permute-start = (bf16[16,32,256]{2,1,0:T(8,128)(2,1)S(1)}, bf16[16,32,256]{2,1,0:T(8,128)(2,1)}, u32[]{:S(2)}, u32[]{:S(2)}) collective-permute-start(bf16[16,32,256]{2,1,0:T(8,128)(2,1)S(1)} %bitcast.17), channel_id=1, source_target_pairs={{0,1},{1,0},{2,3},{3,2},{4,5},{5,4},{6,7},{7,6},{8,9},{9,8},{10,11... | collective-permute-start | bytes 786440 | tf_op jit(solution)/shard_map/ppermute | solution.py:303
  1.8 7.1 %collective-permute-start.1 = (bf16[16,32,256]{2,1,0:T(8,128)(2,1)S(1)}, bf16[16,32,256]{2,1,0:T(8,128)(2,1)}, u32[]{:S(2)}, u32[]{:S(2)}) collective-permute-start(bf16[16,32,256]{2,1,0:T(8,128)(2,1)S(1)} %bitcast.18), channel_id=1, source_target_pairs={{0,2},{1,7},{2,4},{3,1},{4,6},{5,3},{6,0},{7,5},{8,10},{9,15},{10,... | collective-permute-start | bytes 786440 | tf_op jit(solution)/shard_map/ppermute | solution.py:300
  3.5 8.0 %collective-permute-start.3 = (bf16[16,32,256]{2,1,0:T(8,128)(2,1)}, bf16[16,32,256]{2,1,0:T(8,128)(2,1)}, u32[]{:S(2)}, u32[]{:S(2)}) collective-permute-start(bf16[16,32,256]{2,1,0:T(8,128)(2,1)} %collective-permute-done.refs_1_), channel_id=1, source_target_pairs={{0,2},{1,7},{2,4},{3,1},{4,6},{5,3},{6,0},{7,5},{8,10},{9,15},{10,... | collective-permute-start | bytes 786440 | tf_op jit(solution)/shard_map/ppermute | solution.py:300
  8.9 7.6 %collective-permute-start.2 = (bf16[16,32,256]{2,1,0:T(8,128)(2,1)}, bf16[16,32,256]{2,1,0:T(8,128)(2,1)}, u32[]{:S(2)}, u32[]{:S(2)}) collective-permute-start(bf16[16,32,256]{2,1,0:T(8,128)(2,1)} %collective-permute-done.1.refs_2_), channel_id=1, source_target_pairs={{0,2},{1,7},{2,4},{3,1},{4,6},{5,3},{6,0},{7,5},{8,10},{9,15},{10,... | collective-permute-start | bytes 786440 | tf_op jit(solution)/shard_map/ppermute | solution.py:300
  10.8 5.7 %collective-permute-start.5 = (bf16[16,32,256]{2,1,0:T(8,128)(2,1)}, bf16[16,32,256]{2,1,0:T(8,128)(2,1)}, u32[]{:S(2)}, u32[]{:S(2)}) collective-permute-start(bf16[16,32,256]{2,1,0:T(8,128)(2,1)} %collective-permute-done.1.refs_2_), channel_id=1, source_target_pairs={{0,1},{1,0},{2,3},{3,2},{4,5},{5,4},{6,7},{7,6},{8,9},{9,8},{10,11... | collective-permute-start | bytes 786440 | tf_op jit(solution)/shard_map/ppermute | solution.py:321
  11.4 5.1 %collective-permute-start.4 = (bf16[16,32,256]{2,1,0:T(8,128)(2,1)}, bf16[16,32,256]{2,1,0:T(8,128)(2,1)}, u32[]{:S(2)}, u32[]{:S(2)}) collective-permute-start(bf16[16,32,256]{2,1,0:T(8,128)(2,1)} %collective-permute-done.3.refs_3_), channel_id=1, source_target_pairs={{0,1},{1,0},{2,3},{3,2},{4,5},{5,4},{6,7},{7,6},{8,9},{9,8},{10,11... | collective-permute-start | bytes 786440 | tf_op jit(solution)/shard_map/ppermute | solution.py:321
  16.5 2.9 %collective-permute-start.6 = (bf16[16,32,256]{2,1,0:T(8,128)(2,1)}, bf16[16,32,256]{2,1,0:T(8,128)(2,1)S(1)}, u32[]{:S(2)}, u32[]{:S(2)}) collective-permute-start(bf16[16,32,256]{2,1,0:T(8,128)(2,1)} %collective-permute-done.2.refs_0_), channel_id=1, source_target_pairs={{0,1},{1,0},{2,3},{3,2},{4,5},{5,4},{6,7},{7,6},{8,9},{9,8},{10,11... | collective-permute-start | bytes 786440 | tf_op jit(solution)/shard_map/ppermute | solution.py:341
  16.5 6.5 %copy-start.2 = (s32[3,4,3]{2,1,0:T(4,128)S(1)}, s32[3,4,3]{2,1,0:T(4,128)}, u32[]{:S(2)}) copy-start(s32[3,4,3]{2,1,0:T(4,128)} %param.15) | copy-start | bytes 436
  23.3 8.6 %collective-permute-start.7 = (bf16[13,16,256]{2,1,0:T(8,128)(2,1)}, bf16[13,16,256]{2,1,0:T(8,128)(2,1)S(1)}, u32[]{:S(2)}, u32[]{:S(2)}) collective-permute-start(bf16[13,16,256]{2,1,0:T(8,128)(2,1)} %get-tuple-element.72), channel_id=1, source_target_pairs={{0,4},{1,5},{2,6},{3,7},{4,0},{5,1},{6,2},{7,3},{8,12},{9,13},{10,... | collective-permute-start | bytes 319496 | tf_op jit(solution)/shard_map/ppermute | solution.py:395
  25.3 7.1 %collective-permute-start.8 = (bf16[13,16,256]{2,1,0:T(8,128)(2,1)}, bf16[13,16,256]{2,1,0:T(8,128)(2,1)S(1)}, u32[]{:S(2)}, u32[]{:S(2)}) collective-permute-start(bf16[13,16,256]{2,1,0:T(8,128)(2,1)} %get-tuple-element.73), channel_id=1, source_target_pairs={{0,5},{1,4},{2,7},{3,6},{4,1},{5,0},{6,3},{7,2},{8,13},{9,12},{10,... | collective-permute-start | bytes 319496 | tf_op jit(solution)/shard_map/ppermute | solution.py:395
  26.8 8.3 %collective-permute-start.9 = (bf16[13,16,256]{2,1,0:T(8,128)(2,1)}, bf16[13,16,256]{2,1,0:T(8,128)(2,1)S(1)}, u32[]{:S(2)}, u32[]{:S(2)}) collective-permute-start(bf16[13,16,256]{2,1,0:T(8,128)(2,1)} %get-tuple-element.74), channel_id=1, source_target_pairs={{0,6},{1,7},{2,0},{3,1},{4,2},{5,3},{6,4},{7,5},{8,14},{9,15},{10,... | collective-permute-start | bytes 319496 | tf_op jit(solution)/shard_map/ppermute | solution.py:395
  30.1 7.1 %collective-permute-start.10 = (bf16[13,16,256]{2,1,0:T(8,128)(2,1)}, bf16[13,16,256]{2,1,0:T(8,128)(2,1)S(1)}, u32[]{:S(2)}, u32[]{:S(2)}) collective-permute-start(bf16[13,16,256]{2,1,0:T(8,128)(2,1)} %get-tuple-element.75), channel_id=1, source_target_pairs={{0,7},{1,6},{2,1},{3,0},{4,3},{5,2},{6,5},{7,4},{8,15},{9,14},{10,... | collective-permute-start | bytes 319496 | tf_op jit(solution)/shard_map/ppermute | solution.py:395
  30.1 7.1 %collective-permute-start.11 = (bf16[13,16,256]{2,1,0:T(8,128)(2,1)}, bf16[13,16,256]{2,1,0:T(8,128)(2,1)S(1)}, u32[]{:S(2)}, u32[]{:S(2)}) collective-permute-start(bf16[13,16,256]{2,1,0:T(8,128)(2,1)} %get-tuple-element.76), channel_id=1, source_target_pairs={{0,3},{1,2},{2,5},{3,4},{4,7},{5,6},{6,1},{7,0},{8,11},{9,10},{10,... | collective-permute-start | bytes 319496 | tf_op jit(solution)/shard_map/ppermute | solution.py:395
  31.8 6.3 %collective-permute-start.12 = (bf16[13,16,256]{2,1,0:T(8,128)(2,1)}, bf16[13,16,256]{2,1,0:T(8,128)(2,1)S(1)}, u32[]{:S(2)}, u32[]{:S(2)}) collective-permute-start(bf16[13,16,256]{2,1,0:T(8,128)(2,1)} %get-tuple-element.77), channel_id=1, source_target_pairs={{0,2},{1,3},{2,4},{3,5},{4,6},{5,7},{6,0},{7,1},{8,10},{9,11},{10,... | collective-permute-start | bytes 319496 | tf_op jit(solution)/shard_map/ppermute | solution.py:395
  32.5 5.7 %collective-permute-start.13 = (bf16[13,16,256]{2,1,0:T(8,128)(2,1)}, bf16[13,16,256]{2,1,0:T(8,128)(2,1)S(1)}, u32[]{:S(2)}, u32[]{:S(2)}) collective-permute-start(bf16[13,16,256]{2,1,0:T(8,128)(2,1)} %get-tuple-element.78), channel_id=1, source_target_pairs={{0,1},{1,0},{2,3},{3,2},{4,5},{5,4},{6,7},{7,6},{8,9},{9,8},{10,11... | collective-permute-start | bytes 319496 | tf_op jit(solution)/shard_map/ppermute | solution.py:395
  38.7 7.5 %collective-permute-start.14 = (bf16[128,256]{1,0:T(8,128)(2,1)S(1)}, bf16[128,256]{1,0:T(8,128)(2,1)S(1)}, u32[]{:S(2)}, u32[]{:S(2)}) collective-permute-start(bf16[128,256]{1,0:T(8,128)(2,1)S(1)} %get-tuple-element.91), channel_id=1, source_target_pairs={{0,16},{8,24},{16,0},{24,8},{1,17},{9,25},{17,1},{25,9},{2,18},{10... | collective-permute-start | bytes 196616 | tf_op jit(solution)/shard_map/ppermute | solution.py:410
  40.5 5.8 %collective-permute-start.15 = (bf16[128,256]{1,0:T(8,128)(2,1)S(1)}, bf16[128,256]{1,0:T(8,128)(2,1)S(1)}, u32[]{:S(2)}, u32[]{:S(2)}) collective-permute-start(bf16[128,256]{1,0:T(8,128)(2,1)S(1)} %get-tuple-element.92), channel_id=1, source_target_pairs={{0,8},{8,16},{16,24},{24,0},{1,9},{9,17},{17,25},{25,1},{2,10},{10... | collective-permute-start | bytes 196616 | tf_op jit(solution)/shard_map/ppermute | solution.py:410
  41.2 5.1 %collective-permute-start.16 = (bf16[128,256]{1,0:T(8,128)(2,1)S(1)}, bf16[128,256]{1,0:T(8,128)(2,1)S(1)}, u32[]{:S(2)}, u32[]{:S(2)}) collective-permute-start(bf16[128,256]{1,0:T(8,128)(2,1)S(1)} %get-tuple-element.93), channel_id=1, source_target_pairs={{0,24},{8,0},{16,8},{24,16},{1,25},{9,1},{17,9},{25,17},{2,26},{10... | collective-permute-start | bytes 196616 | tf_op jit(solution)/shard_map/ppermute | solution.py:410
  43.7 19.3 %copy-start = (bf16[4,4,256,256]{3,2,1,0:T(8,128)(2,1)S(1)}, bf16[4,4,256,256]{3,2,1,0:T(8,128)(2,1)}, u32[]{:S(2)}) copy-start(bf16[4,4,256,256]{3,2,1,0:T(8,128)(2,1)} %d_ref.7) | copy-start | bytes 6291460
  108.0 27.5 %copy-start.1 = (f32[4,4,32,256]{3,2,1,0:T(8,128)S(1)}, f32[4,4,32,256]{3,2,1,0:T(8,128)}, u32[]{:S(2)}) copy-start(f32[4,4,32,256]{3,2,1,0:T(8,128)} %param.12) | copy-start | bytes 1572868
  126.9 5.9 %collective-permute-start.19 = (bf16[8,16,256]{2,1,0:T(8,128)(2,1)S(1)}, bf16[8,16,256]{2,1,0:T(8,128)(2,1)S(1)}, u32[]{:S(2)}, u32[]{:S(2)}) collective-permute-start(bf16[8,16,256]{2,1,0:T(8,128)(2,1)S(1)} %all_to_all.47), channel_id=1, source_target_pairs={{0,8},{8,16},{16,24},{24,0},{1,9},{9,17},{17,25},{25,1},{2,10},{10... | collective-permute-start | bytes 196616 | tf_op jit(solution)/shard_map/ppermute | solution.py:492
  126.9 7.3 %collective-permute-start.18 = (bf16[8,16,256]{2,1,0:T(8,128)(2,1)S(1)}, bf16[8,16,256]{2,1,0:T(8,128)(2,1)S(1)}, u32[]{:S(2)}, u32[]{:S(2)}) collective-permute-start(bf16[8,16,256]{2,1,0:T(8,128)(2,1)S(1)} %all_to_all.47), channel_id=1, source_target_pairs={{0,16},{8,24},{16,0},{24,8},{1,17},{9,25},{17,1},{25,9},{2,18},{10... | collective-permute-start | bytes 196616 | tf_op jit(solution)/shard_map/ppermute | solution.py:492
  131.2 4.3 %collective-permute-start.17 = (bf16[8,16,256]{2,1,0:T(8,128)(2,1)S(1)}, bf16[8,16,256]{2,1,0:T(8,128)(2,1)S(1)}, u32[]{:S(2)}, u32[]{:S(2)}) collective-permute-start(bf16[8,16,256]{2,1,0:T(8,128)(2,1)S(1)} %all_to_all.47), channel_id=1, source_target_pairs={{0,24},{8,0},{16,8},{24,16},{1,25},{9,1},{17,9},{25,17},{2,26},{10... | collective-permute-start | bytes 196616 | tf_op jit(solution)/shard_map/ppermute | solution.py:492
